TPU v7x, 32 devices: a whole 2x2x4 slice. The times are simulated.
32 devices in a mesh: fsdp: 8 (over z, y), dp: 4 (over x, core).
Axes of the slice: x: 2, y: 2, z: 4, core: 2. Of those that a mesh axis runs over, the one named last changes fastest.
Arguments:
- tokens: bfloat16 [128, 64, 2048], P(('fsdp', 'dp')), may hold values from -6 to 6
- cotangent: bfloat16 [128, 64, 2048], P(('fsdp', 'dp')), may hold values from -6 to 6
- lengths: int32 [128], replicated, may hold values from 16 to 64, as said below
- dealing: int32 [128], replicated, may hold values from 0 to 127, as said below
- attn_gain: float32 [2048], P('fsdp'), may hold values from 0.25 to 1.75
- attn_shift: float32 [2048], P('fsdp'), may hold values from -3 to 3
- query_weight: float32 [2048, 2048], P('fsdp'), may hold values from -0.125 to 0.125
- query_bias: float32 [2048], P('fsdp'), may hold values from -3 to 3
- keyval_weight: float32 [2048, 256], P('fsdp'), may hold values from -0.125 to 0.125
- value_bias: float32 [128], P('fsdp'), may hold values from -3 to 3
- output_weight: float32 [2048, 2048], P('fsdp'), may hold values from -0.5 to 0.5
- output_bias: float32 [2048], P('fsdp'), may hold values from -3 to 3
- mlp_gain: float32 [2048], P('fsdp'), may hold values from 0.25 to 1.75
- mlp_shift: float32 [2048], P('fsdp'), may hold values from -3 to 3
- up_weight: float32 [2048, 8192], P('fsdp'), may hold values from -0.125 to 0.125
- up_bias: float32 [8192], P('fsdp'), may hold values from -3 to 3
- down_weight: float32 [8192, 2048], P('fsdp'), may hold values from -0.0625 to 0.0625
- down_bias: float32 [2048], P('fsdp'), may hold values from -3 to 3
Outputs:
- block_out: bfloat16 [128, 64, 2048], P(('fsdp', 'dp'))
- input_grad: bfloat16 [128, 64, 2048], P(('fsdp', 'dp'))
- attn_gain_grad: float32 [2048], P('fsdp')
- attn_shift_grad: float32 [2048], P('fsdp')
- query_weight_grad: float32 [2048, 2048], P('fsdp')
- query_bias_grad: float32 [2048], P('fsdp')
- keyval_weight_grad: float32 [2048, 256], P('fsdp')
- value_bias_grad: float32 [128], P('fsdp')
- output_weight_grad: float32 [2048, 2048], P('fsdp')
- output_bias_grad: float32 [2048], P('fsdp')
- mlp_gain_grad: float32 [2048], P('fsdp')
- mlp_shift_grad: float32 [2048], P('fsdp')
- up_weight_grad: float32 [2048, 8192], P('fsdp')
- up_bias_grad: float32 [8192], P('fsdp')
- down_weight_grad: float32 [8192, 2048], P('fsdp')
- down_bias_grad: float32 [2048], P('fsdp')
Inputs may be any that keep to these rules, and one draw needn't show every extreme that they name: lengths[j] belongs to the sequence at dealt position j; the slots of a sequence past its length are padding. The 2 lengths of one micro-batch of one device (dealt positions g * 16 + r * 4 + m * 2 + k for k below 2) sum to at most 80; some micro-batch sums to exactly 80 and holds a sequence of 64 tokens. dealing is a permutation. Dealt position g * 16 + r * 4 + m * 2 + k is sequence k of micro-batch m of the device with fsdp index g and dp index r; sequence g * 16 + q * 4 + l is the l-th sequence held in the arrays by the device with fsdp index g and dp index q. Every sequence is dealt within its own fsdp index, and no device is dealt more than one sequence held by any one device.
All inputs are finite; a program needn't handle non-finite values.
Results may differ from a plain program's by a relative error of at most 0.018.
Values may be sent and summed in bfloat16 or wider, within the bound.
A program may use at most 448 MiB of HBM per device.

v0:
```python
import math

import jax
import jax.numpy as jnp
from jax import lax
from jax.sharding import PartitionSpec as P

HEADS = 16
HEAD = 128
MB = 2
SEATS = 2
PACK = 80


epsilon = 1e-05
gelu_scale = 0.7978845608028654
gelu_cubic = 0.044715


def layer_norm(row_data, gain_vec, shift_vec):
    center = row_data - jnp.mean(row_data, axis=-1, keepdims=True)
    spread = jnp.mean(center * center, axis=-1, keepdims=True)
    return center * lax.rsqrt(spread + epsilon) * gain_vec + shift_vec


def gelu_tanh(values):
    return (
        0.5
        * values
        * (1.0 + jnp.tanh(gelu_scale * (values + gelu_cubic * values * values * values)))
    )


def to_low(values):
    return values.astype(jnp.bfloat16)


def as_float(values):
    return values.astype(jnp.float32)


def product(left_mat, right_mat):
    return jnp.dot(left_mat, right_mat, preferred_element_type=jnp.float32)


def product_rows(left_mat, right_mat):
    return lax.dot_general(
        left_mat, right_mat, (((0,), (0,)), ((), ())), preferred_element_type=jnp.float32
    )


def product_cols(left_mat, right_mat):
    return lax.dot_general(
        left_mat, right_mat, (((1,), (1,)), ((), ())), preferred_element_type=jnp.float32
    )


def score_rows(query_rows, key_rows, score_scale, allowed):
    query_heads = query_rows.reshape(query_rows.shape[0], HEADS, HEAD)
    scores = (
        jnp.einsum("shd,td->hst", query_heads, key_rows, preferred_element_type=jnp.float32)
        * score_scale
    )
    return jnp.where(allowed[None], scores, -1e30)


def column_sum(values):
    return jnp.sum(as_float(values), axis=0)


def shards(
    tokens,
    cotangent,
    lengths,
    dealing,
    attn_gain,
    attn_shift,
    query_weight,
    query_bias,
    keyval_weight,
    value_bias,
    output_weight,
    output_bias,
    mlp_gain,
    mlp_shift,
    up_weight,
    up_bias,
    down_weight,
    down_bias,
):
    held_count = tokens.shape[0]
    slot_len = tokens.shape[1]
    model_width = tokens.shape[2]
    group_devices = lax.axis_size("dp")
    my_dp = lax.axis_index("dp")
    group_seqs = held_count * group_devices
    group_base = lax.axis_index("fsdp") * group_seqs
    in_group = lax.dynamic_slice_in_dim(dealing, group_base, group_seqs) - group_base
    in_group = in_group.reshape(group_devices, held_count)
    senders = in_group // held_count
    held_slot = in_group % held_count
    from_me = senders == my_dp
    send_used = jnp.any(from_me, axis=1)
    send_index = jnp.sum(jnp.where(from_me, held_slot, 0), axis=1)
    zero_low = jnp.zeros((), jnp.bfloat16)
    send_tokens = jnp.where(
        send_used[:, None, None], jnp.take(tokens, send_index, axis=0), zero_low
    )
    send_cotangent = jnp.where(
        send_used[:, None, None], jnp.take(cotangent, send_index, axis=0), zero_low
    )
    got_tokens, got_cotangent = (
        lax.all_to_all(send_tokens, "dp", split_axis=0, concat_axis=0, tiled=True),
        lax.all_to_all(send_cotangent, "dp", split_axis=0, concat_axis=0, tiled=True),
    )
    my_senders = lax.dynamic_index_in_dim(senders, my_dp, 0, keepdims=False)
    my_lengths = lax.dynamic_slice_in_dim(
        lengths, group_base + my_dp * held_count, held_count
    ).reshape(MB, SEATS)
    seat_starts = jnp.cumsum(my_lengths, axis=1) - my_lengths
    seat_ends = seat_starts + my_lengths
    pack_rows = jnp.arange(PACK)
    inside = (pack_rows[None, :, None] >= seat_starts[:, None, :]) & (
        pack_rows[None, :, None] < seat_ends[:, None, :]
    )
    row_valid = jnp.any(inside, axis=2)
    seat_ids = jnp.arange(SEATS)
    seat_of = jnp.sum(jnp.where(inside, seat_ids[None, None, :], 0), axis=2)
    segment = jnp.where(row_valid, seat_of, -1)
    offset_in = pack_rows[None, :] - jnp.sum(jnp.where(inside, seat_starts[:, None, :], 0), axis=2)
    sender_seat = my_senders.reshape(MB, SEATS)
    source_dev = jnp.sum(jnp.where(inside, sender_seat[:, None, :], 0), axis=2)
    source_row = jnp.where(row_valid, source_dev * slot_len + offset_in, 0)
    flat_tokens = got_tokens.reshape(group_devices * slot_len, model_width)
    flat_cotangent = got_cotangent.reshape(group_devices * slot_len, model_width)
    packed_tokens = jnp.where(
        row_valid[..., None], jnp.take(flat_tokens, source_row, axis=0), zero_low
    )
    packed_cotangent = jnp.where(
        row_valid[..., None], jnp.take(flat_cotangent, source_row, axis=0), zero_low
    )
    low_attn_gain = to_low(attn_gain)
    low_attn_shift = to_low(attn_shift)
    low_query_weight = to_low(query_weight)
    low_query_bias = to_low(query_bias)
    low_keyval_weight = to_low(keyval_weight)
    low_value_bias = to_low(value_bias)
    low_output_weight = to_low(output_weight)
    low_output_bias = to_low(output_bias)
    low_mlp_gain = to_low(mlp_gain)
    low_mlp_shift = to_low(mlp_shift)
    low_up_weight = to_low(up_weight)
    low_up_bias = to_low(up_bias)
    low_down_weight = to_low(down_weight)
    low_down_bias = to_low(down_bias)
    causal = pack_rows[None, :] <= pack_rows[:, None]
    score_scale = 1.0 / math.sqrt(HEAD)
    zero_keys = jnp.zeros((HEAD,), jnp.float32)
    block_list = []
    grad_list = []
    store_normed_attn = []
    store_grad_query = []
    store_grad_keyval = []
    store_attended = []
    store_grad_branch = []
    store_normed_mlp = []
    store_grad_hidden = []
    store_activated = []
    store_grad_mixed = []
    small_terms = []
    for micro_index in range(MB):
        row_data = as_float(packed_tokens[micro_index])
        valid_mask = row_valid[micro_index]
        micro_segment = segment[micro_index]
        allowed = causal & (micro_segment[:, None] == micro_segment[None, :]) & valid_mask[None, :]
        attn_full = (
            lax.all_gather(low_attn_gain, "fsdp", axis=0, tiled=True),
            lax.all_gather(low_attn_shift, "fsdp", axis=0, tiled=True),
            lax.all_gather(low_query_weight, "fsdp", axis=0, tiled=True),
            lax.all_gather(low_query_bias, "fsdp", axis=0, tiled=True),
            lax.all_gather(low_keyval_weight, "fsdp", axis=0, tiled=True),
            lax.all_gather(low_value_bias, "fsdp", axis=0, tiled=True),
            lax.all_gather(low_output_weight, "fsdp", axis=0, tiled=True),
            lax.all_gather(low_output_bias, "fsdp", axis=0, tiled=True),
        )
        normed_attn = to_low(layer_norm(row_data, as_float(attn_full[0]), as_float(attn_full[1])))
        query_rows = to_low(product(normed_attn, attn_full[2]) + as_float(attn_full[3]))
        value_shift = jnp.concatenate([zero_keys, as_float(attn_full[5])])
        keyval_rows = to_low(product(normed_attn, attn_full[4]) + value_shift)
        key_rows = keyval_rows[:, :HEAD]
        value_rows = keyval_rows[:, HEAD:]
        scores = score_rows(query_rows, key_rows, score_scale, allowed)
        row_max = jnp.max(scores, axis=-1, keepdims=True)
        expscores = jnp.exp(scores - row_max)
        row_total = jnp.sum(expscores, axis=-1, keepdims=True)
        probabilities = expscores / row_total
        log_total = row_max + jnp.log(row_total)
        attended = jnp.einsum(
            "hst,td->shd", to_low(probabilities), value_rows, preferred_element_type=jnp.float32
        )
        attended_low = to_low(attended.reshape(PACK, model_width))
        middle = row_data + (product(attended_low, attn_full[6]) + as_float(attn_full[7]))
        mlp_full = (
            lax.all_gather(low_mlp_gain, "fsdp", axis=0, tiled=True),
            lax.all_gather(low_mlp_shift, "fsdp", axis=0, tiled=True),
            lax.all_gather(low_up_weight, "fsdp", axis=0, tiled=True),
            lax.all_gather(low_up_bias, "fsdp", axis=0, tiled=True),
            lax.all_gather(low_down_weight, "fsdp", axis=0, tiled=True),
            lax.all_gather(low_down_bias, "fsdp", axis=0, tiled=True),
        )
        normed_mlp = to_low(layer_norm(middle, as_float(mlp_full[0]), as_float(mlp_full[1])))
        hidden = product(normed_mlp, mlp_full[2]) + as_float(mlp_full[3])
        activated = to_low(gelu_tanh(hidden))
        mlp_out = product(activated, mlp_full[4]) + as_float(mlp_full[5])
        block_list.append(to_low(jnp.where(valid_mask[:, None], middle + mlp_out, 0.0)))
        grad_out = jnp.where(valid_mask[:, None], as_float(packed_cotangent[micro_index]), 0.0)
        grad_mixed = to_low(grad_out)
        grad_activated = product_cols(grad_mixed, mlp_full[4])
        _, gelu_pull = jax.vjp(gelu_tanh, hidden)
        grad_hidden = to_low(gelu_pull(grad_activated)[0])
        grad_normed_mlp = product_cols(grad_hidden, mlp_full[2])
        _, norm_mlp_pull = jax.vjp(layer_norm, middle, as_float(mlp_full[0]), as_float(mlp_full[1]))
        grad_mid_norm, mlp_gain_term, mlp_shift_term = norm_mlp_pull(grad_normed_mlp)
        grad_middle = grad_out + grad_mid_norm
        grad_branch = to_low(grad_middle)
        grad_attended = to_low(product_cols(grad_branch, attn_full[6]))
        grad_heads = grad_attended.reshape(PACK, HEADS, HEAD)
        scores = score_rows(query_rows, key_rows, score_scale, allowed)
        probabilities = jnp.exp(scores - log_total)
        grad_probs = jnp.einsum(
            "shd,td->hst", grad_heads, value_rows, preferred_element_type=jnp.float32
        )
        grad_values = jnp.einsum(
            "hst,shd->td", to_low(probabilities), grad_heads, preferred_element_type=jnp.float32
        )
        row_inner = jnp.sum(probabilities * grad_probs, axis=-1, keepdims=True)
        grad_scores = to_low(probabilities * (grad_probs - row_inner))
        query_heads = query_rows.reshape(PACK, HEADS, HEAD)
        grad_query = (
            jnp.einsum("hst,td->shd", grad_scores, key_rows, preferred_element_type=jnp.float32)
            * score_scale
        )
        grad_query = to_low(grad_query.reshape(PACK, model_width))
        grad_keys = (
            jnp.einsum("hst,shd->td", grad_scores, query_heads, preferred_element_type=jnp.float32)
            * score_scale
        )
        grad_keyval = to_low(jnp.concatenate([grad_keys, grad_values], axis=1))
        grad_normed_attn = product_cols(grad_query, attn_full[2]) + product_cols(
            grad_keyval, attn_full[4]
        )
        _, norm_attn_pull = jax.vjp(
            layer_norm, row_data, as_float(attn_full[0]), as_float(attn_full[1])
        )
        grad_rows_norm, attn_gain_term, attn_shift_term = norm_attn_pull(grad_normed_attn)
        grad_list.append(to_low(grad_middle + grad_rows_norm))
        store_normed_attn.append(normed_attn)
        store_grad_query.append(grad_query)
        store_grad_keyval.append(grad_keyval)
        store_attended.append(attended_low)
        store_grad_branch.append(grad_branch)
        store_normed_mlp.append(normed_mlp)
        store_grad_hidden.append(grad_hidden)
        store_activated.append(activated)
        store_grad_mixed.append(grad_mixed)
        small_terms.append(
            (
                attn_gain_term,
                attn_shift_term,
                column_sum(grad_query),
                column_sum(grad_branch),
                mlp_gain_term,
                mlp_shift_term,
                column_sum(grad_mixed),
                column_sum(grad_keyval[:, HEAD:]),
                column_sum(grad_hidden),
            )
        )
    small_sums = [
        jnp.sum(jnp.stack([term[index] for term in small_terms]), axis=0) for index in range(9)
    ]
    all_normed_attn = jnp.concatenate(store_normed_attn, axis=0)
    all_grad_query = jnp.concatenate(store_grad_query, axis=0)
    all_grad_keyval = jnp.concatenate(store_grad_keyval, axis=0)
    all_attended = jnp.concatenate(store_attended, axis=0)
    all_grad_branch = jnp.concatenate(store_grad_branch, axis=0)
    all_normed_mlp = jnp.concatenate(store_normed_mlp, axis=0)
    all_grad_hidden = jnp.concatenate(store_grad_hidden, axis=0)
    all_activated = jnp.concatenate(store_activated, axis=0)
    all_grad_mixed = jnp.concatenate(store_grad_mixed, axis=0)
    query_full = product_rows(all_normed_attn, all_grad_query)
    keyval_full = product_rows(all_normed_attn, all_grad_keyval)
    output_full = product_rows(all_attended, all_grad_branch)
    up_full = product_rows(all_normed_mlp, all_grad_hidden)
    down_full = product_rows(all_activated, all_grad_mixed)
    local_grads = (
        lax.psum_scatter(
            small_sums[0].astype(jnp.bfloat16), "fsdp", scatter_dimension=0, tiled=True
        ).astype(jnp.float32),
        lax.psum_scatter(
            small_sums[1].astype(jnp.bfloat16), "fsdp", scatter_dimension=0, tiled=True
        ).astype(jnp.float32),
        lax.psum_scatter(
            query_full.astype(jnp.bfloat16), "fsdp", scatter_dimension=0, tiled=True
        ).astype(jnp.float32),
        lax.psum_scatter(
            small_sums[2].astype(jnp.bfloat16), "fsdp", scatter_dimension=0, tiled=True
        ).astype(jnp.float32),
        lax.psum_scatter(
            keyval_full.astype(jnp.bfloat16), "fsdp", scatter_dimension=0, tiled=True
        ).astype(jnp.float32),
        lax.psum_scatter(
            small_sums[7].astype(jnp.bfloat16), "fsdp", scatter_dimension=0, tiled=True
        ).astype(jnp.float32),
        lax.psum_scatter(
            output_full.astype(jnp.bfloat16), "fsdp", scatter_dimension=0, tiled=True
        ).astype(jnp.float32),
        lax.psum_scatter(
            small_sums[3].astype(jnp.bfloat16), "fsdp", scatter_dimension=0, tiled=True
        ).astype(jnp.float32),
        lax.psum_scatter(
            small_sums[4].astype(jnp.bfloat16), "fsdp", scatter_dimension=0, tiled=True
        ).astype(jnp.float32),
        lax.psum_scatter(
            small_sums[5].astype(jnp.bfloat16), "fsdp", scatter_dimension=0, tiled=True
        ).astype(jnp.float32),
        lax.psum_scatter(
            up_full.astype(jnp.bfloat16), "fsdp", scatter_dimension=0, tiled=True
        ).astype(jnp.float32),
        lax.psum_scatter(
            small_sums[8].astype(jnp.bfloat16), "fsdp", scatter_dimension=0, tiled=True
        ).astype(jnp.float32),
        lax.psum_scatter(
            down_full.astype(jnp.bfloat16), "fsdp", scatter_dimension=0, tiled=True
        ).astype(jnp.float32),
        lax.psum_scatter(
            small_sums[6].astype(jnp.bfloat16), "fsdp", scatter_dimension=0, tiled=True
        ).astype(jnp.float32),
    )
    total_grads = (
        lax.psum(local_grads[0].astype(jnp.bfloat16), "dp").astype(jnp.float32),
        lax.psum(local_grads[1].astype(jnp.bfloat16), "dp").astype(jnp.float32),
        lax.psum(local_grads[2].astype(jnp.bfloat16), "dp").astype(jnp.float32),
        lax.psum(local_grads[3].astype(jnp.bfloat16), "dp").astype(jnp.float32),
        lax.psum(local_grads[4].astype(jnp.bfloat16), "dp").astype(jnp.float32),
        lax.psum(local_grads[5].astype(jnp.bfloat16), "dp").astype(jnp.float32),
        lax.psum(local_grads[6].astype(jnp.bfloat16), "dp").astype(jnp.float32),
        lax.psum(local_grads[7].astype(jnp.bfloat16), "dp").astype(jnp.float32),
        lax.psum(local_grads[8].astype(jnp.bfloat16), "dp").astype(jnp.float32),
        lax.psum(local_grads[9].astype(jnp.bfloat16), "dp").astype(jnp.float32),
        lax.psum(local_grads[10].astype(jnp.bfloat16), "dp").astype(jnp.float32),
        lax.psum(local_grads[11].astype(jnp.bfloat16), "dp").astype(jnp.float32),
        lax.psum(local_grads[12].astype(jnp.bfloat16), "dp").astype(jnp.float32),
        lax.psum(local_grads[13].astype(jnp.bfloat16), "dp").astype(jnp.float32),
    )
    block_packed = jnp.concatenate(block_list, axis=0)
    grad_packed = jnp.concatenate(grad_list, axis=0)
    slot_pos = jnp.arange(slot_len)
    flat_starts = (seat_starts + jnp.arange(MB)[:, None] * PACK).reshape(held_count)
    flat_lengths = my_lengths.reshape(held_count)
    in_sequence = slot_pos[None, :] < flat_lengths[:, None]
    pack_index = jnp.where(in_sequence, flat_starts[:, None] + slot_pos[None, :], 0)
    block_all = jnp.where(
        in_sequence[..., None], jnp.take(block_packed, pack_index, axis=0), zero_low
    )
    grad_all = jnp.where(
        in_sequence[..., None], jnp.take(grad_packed, pack_index, axis=0), zero_low
    )
    device_ids = jnp.arange(group_devices)
    back_hits = my_senders[None, :] == device_ids[:, None]
    back_used = jnp.any(back_hits, axis=1)
    back_index = jnp.sum(jnp.where(back_hits, jnp.arange(held_count)[None, :], 0), axis=1)
    send_out = jnp.where(
        back_used[:, None, None], jnp.take(block_all, back_index, axis=0), zero_low
    )
    send_grad = jnp.where(
        back_used[:, None, None], jnp.take(grad_all, back_index, axis=0), zero_low
    )
    got_out, got_grad = (
        lax.all_to_all(send_out, "dp", split_axis=0, concat_axis=0, tiled=True),
        lax.all_to_all(send_grad, "dp", split_axis=0, concat_axis=0, tiled=True),
    )
    owners = (send_index[None, :] == jnp.arange(held_count)[:, None]) & send_used[None, :]
    owner_index = jnp.sum(jnp.where(owners, device_ids[None, :], 0), axis=1)
    block_out = jnp.take(got_out, owner_index, axis=0)
    input_grad = jnp.take(got_grad, owner_index, axis=0)
    return (
        block_out,
        input_grad,
        total_grads[0],
        total_grads[1],
        total_grads[2],
        total_grads[3],
        total_grads[4],
        total_grads[5],
        total_grads[6],
        total_grads[7],
        total_grads[8],
        total_grads[9],
        total_grads[10],
        total_grads[11],
        total_grads[12],
        total_grads[13],
    )


def solution(mesh):
    in_specs = (
        P(("fsdp", "dp"), None, None),
        P(("fsdp", "dp"), None, None),
        P(),
        P(),
        P("fsdp"),
        P("fsdp"),
        P("fsdp", None),
        P("fsdp"),
        P("fsdp", None),
        P("fsdp"),
        P("fsdp", None),
        P("fsdp"),
        P("fsdp"),
        P("fsdp"),
        P("fsdp", None),
        P("fsdp"),
        P("fsdp", None),
        P("fsdp"),
    )
    out_specs = (
        P(("fsdp", "dp"), None, None),
        P(("fsdp", "dp"), None, None),
        P("fsdp"),
        P("fsdp"),
        P("fsdp", None),
        P("fsdp"),
        P("fsdp", None),
        P("fsdp"),
        P("fsdp", None),
        P("fsdp"),
        P("fsdp"),
        P("fsdp"),
        P("fsdp", None),
        P("fsdp"),
        P("fsdp", None),
        P("fsdp"),
    )
    return jax.shard_map(shards, mesh=mesh, in_specs=in_specs, out_specs=out_specs, check_vma=False)
```

profile of v0, /device:TPU:9, one launch (start us, length us, event | category | flops | bytes accessed | tf_op | source)
XLA Modules:
  0.0 3384.6 jit_solution(3375600129707056963)
XLA Ops:
  60.7 15.3 all-gather
  106.7 16.6 all-reduce.1
  123.3 22.3 all_gather.67
  145.6 28.6 all-to-all-start
  205.2 98.1 %all-gather.17.cloned.1.call-done = bf16[2048,2048]{1,0:T(8,128)(2,1)} async-done(((bf16[256,2048]{1,0:T(8,128)(2,1)}), bf16[2048,2048]{1,0:T(8,128)(2,1)}) %all-gather.17.cloned.1.call-update) | async-done | bytes 8388624 | tf_op jit(solution)/shard_map/all_gather | solution.py:183
  312.5 631.2 %all-gather.19.cloned.1.call-done = bf16[2048,8192]{1,0:T(8,128)(2,1)} async-done(((bf16[256,8192]{1,0:T(8,128)(2,1)}), bf16[2048,8192]{1,0:T(8,128)(2,1)}) %all-gather.19.cloned.1.call-update) | async-done | bytes 33554448 | tf_op jit(solution)/shard_map/all_gather | solution.py:206
  943.7 18.9 convolution_add_fusion
  962.6 620.8 %all-gather.21.cloned.1.call-done = bf16[8192,2048]{1,0:T(8,128)(2,1)} async-done(((bf16[1024,2048]{1,0:T(8,128)(2,1)}), bf16[8192,2048]{1,0:T(8,128)(2,1)}) %all-gather.21.cloned.1.call-update) | async-done | bytes 33554448 | tf_op jit(solution)/shard_map/all_gather | solution.py:208
  1583.4 18.5 convert_reduce_fusion
  1601.9 16.7 fusion.171
  1618.7 15.2 convolution_add_fusion.1
  1633.9 17.8 convert_reduce_fusion.1
  1651.7 17.4 multiply_reduce_fusion.1
  1702.8 15.5 convolution_convert_fusion.1
  1719.4 15.7 convolution_convert_fusion
  1770.5 17.1 fusion.25
  1787.7 113.5 %reduce-scatter.6.cloned.1.call-done = bf16[256,2048]{1,0:T(8,128)(2,1)} async-done(((bf16[2048,2048]{1,0:T(8,128)(2,1)}), bf16[256,2048]{1,0:T(8,128)(2,1)}) %reduce-scatter.6.cloned.1.call-update) | async-done | bytes 1048592 | tf_op jit(solution)/shard_map/reduce_scatter | solution.py:303
  1901.2 152.2 %reduce-scatter.10.cloned.1.call-done = bf16[256,2048]{1,0:T(8,128)(2,1)} async-done(((bf16[2048,2048]{1,0:T(8,128)(2,1)}), bf16[256,2048]{1,0:T(8,128)(2,1)}) %reduce-scatter.10.cloned.1.call-update) | async-done | bytes 1048592 | tf_op jit(solution)/shard_map/reduce_scatter | solution.py:315
  2053.5 547.5 %reduce-scatter.12.cloned.1.call-done = bf16[256,8192]{1,0:T(8,128)(2,1)} async-done(((bf16[2048,8192]{1,0:T(8,128)(2,1)}), bf16[256,8192]{1,0:T(8,128)(2,1)}) %reduce-scatter.12.cloned.1.call-update) | async-done | bytes 4194320 | tf_op jit(solution)/shard_map/reduce_scatter | solution.py:327
  2601.0 546.7 %reduce-scatter.14.cloned.1.call-done = bf16[1024,2048]{1,0:T(8,128)(2,1)} async-done(((bf16[8192,2048]{1,0:T(8,128)(2,1)}), bf16[1024,2048]{1,0:T(8,128)(2,1)}) %reduce-scatter.14.cloned.1.call-update) | async-done | bytes 4194320 | tf_op jit(solution)/shard_map/reduce_scatter | solution.py:333
  3149.0 14.9 fusion.24
  3175.3 25.4 all-to-all-done.3
  3204.9 27.1 all-reduce.11
  3253.3 110.5 %all-reduce.16.cloned.1.call-done = (bf16[256,2048]{1,0:T(8,128)(2,1)}, bf16[256,256]{1,0:T(8,128)(2,1)}, bf16[256,2048]{1,0:T(8,128)(2,1)}, bf16[256,8192]{1,0:T(8,128)(2,1)}, bf16[1024,2048]{1,0:T(8,128)(2,1)}) async-done(((bf16[256,2048]{1,0:T(8,128)(2,1)}, bf16[256,256]{1,0:T(8,128)(2,1)}, bf16[256,2048]{1,0:T(8,128)(2,1)}, bf16[256,8192]{1,0:T(8,128)(2,1)}, bf16[1024,2048]{1,0:T(8,128)(2,1)}), ...) | async-done | bytes 10616848 | tf_op jit(solution)/shard_map/psum | solution.py:343
  (402 shorter events, 242.6 us)
Async XLA Ops:
  7.2 185.1 %all-gather.13.cloned.1.call-start = ((), (), s32[]{:S(2)}) async-start(), calls=%async_computation.9 | async-start | bytes 1179648 | tf_op jit(solution)/shard_map/all_gather | solution.py:181
  9.0 186.4 %all-gather.15.cloned.1.call-start = ((), (), s32[]{:S(2)}) async-start(), calls=%async_computation.10 | async-start | bytes 9437184 | tf_op jit(solution)/shard_map/all_gather | solution.py:179
  11.8 291.6 %all-gather.17.cloned.1.call-start = ((), (), s32[]{:S(2)}) async-start(), calls=%async_computation.11 | async-start | bytes 9437184 | tf_op jit(solution)/shard_map/all_gather | solution.py:183
  13.0 930.7 %all-gather.19.cloned.1.call-start = ((), (), s32[]{:S(2)}) async-start(), calls=%async_computation.12 | async-start | bytes 37748736 | tf_op jit(solution)/shard_map/all_gather | solution.py:206
  19.1 1564.4 %all-gather.21.cloned.1.call-start = ((), (), s32[]{:S(2)}) async-start(), calls=%async_computation.13 | async-start | bytes 37748736 | tf_op jit(solution)/shard_map/all_gather | solution.py:208
  27.7 48.3 %copy-start.70 = (s32[128]{0:T(128)S(1)}, s32[128]{0:T(128)}, u32[]{:S(2)}) copy-start(s32[128]{0:T(128)} %param.26) | copy-start | bytes 1540
  27.7 50.0 %copy-start.79 = (f32[256]{0:T(256)S(1)}, f32[256]{0:T(256)}, u32[]{:S(2)}) copy-start(f32[256]{0:T(256)} %param.31) | copy-start | bytes 3076
  27.7 63.4 %copy-start.83 = (f32[16]{0:T(128)S(1)}, f32[16]{0:T(128)}, u32[]{:S(2)}) copy-start(f32[16]{0:T(128)} %param.33) | copy-start | bytes 196
  27.7 63.4 %copy-start.80 = (f32[256]{0:T(256)S(1)}, f32[256]{0:T(256)}, u32[]{:S(2)}) copy-start(f32[256]{0:T(256)} %param.36) | copy-start | bytes 3076
  27.8 77.4 %copy-start.81 = (f32[256]{0:T(256)S(1)}, f32[256]{0:T(256)}, u32[]{:S(2)}) copy-start(f32[256]{0:T(256)} %param.37) | copy-start | bytes 3076
  27.8 77.4 %copy-start.59 = (f32[1024]{0:T(1024)S(1)}, f32[1024]{0:T(1024)}, u32[]{:S(2)}) copy-start(f32[1024]{0:T(1024)} %param.39) | copy-start | bytes 12292
  27.8 77.4 %copy-start.62 = (u32[32]{0:T(128)S(1)}, u32[32]{0:T(128)}, u32[]{:S(2)}) copy-start(u32[32]{0:T(128)} %constant.136) | copy-start | bytes 388
  29.4 116.2 %all-to-all-start.2 = ((bf16[4,64,2048]{2,1,0:T(8,128)(2,1)}), bf16[4,64,2048]{2,1,0:T(8,128)(2,1)S(1)}, u32[]{:S(2)}, u32[]{:S(2)}) async-start(bf16[4,64,2048]{2,1,0:T(8,128)(2,1)} %get-tuple-element.110), calls=%async_computation.2 | async-start | bytes 2097152 | tf_op jit(solution)/shard_map/all_to_all | solution.py:114
  76.0 115.8 %copy-start.43 = (f32[8,1,256]{2,1,0:T(1,128)}, f32[8,1,256]{2,1,0:T(1,128)S(1)}, u32[]{:S(2)}) copy-start(f32[8,1,256]{2,1,0:T(1,128)S(1)} %convert_element_type.487) | copy-start | bytes 24580
  145.6 42.1 %all-to-all-start = ((bf16[4,64,2048]{2,1,0:T(8,128)(2,1)}), bf16[4,64,2048]{2,1,0:T(8,128)(2,1)S(1)}, u32[]{:S(2)}, u32[]{:S(2)}) async-start(bf16[4,64,2048]{2,1,0:T(8,128)(2,1)} %get-tuple-element.111), calls=%async_computation | async-start | bytes 2097152 | tf_op jit(solution)/shard_map/all_to_all | solution.py:113
  174.2 1613.5 %reduce-scatter.8.cloned.1.call-start = ((), (), s32[]{:S(2)}) async-start(), calls=%async_computation.15 | async-start | bytes 1179648 | tf_op jit(solution)/shard_map/reduce_scatter | solution.py:309
  204.1 104.9 %copy-start.4 = (f32[16,80,80]{1,2,0:T(8,128)}, f32[16,80,80]{1,2,0:T(8,128)S(1)}, u32[]{:S(2)}) copy-start(f32[16,80,80]{1,2,0:T(8,128)S(1)} %get-tuple-element.127) | copy-start | bytes 1228804
  1686.7 214.6 %reduce-scatter.6.cloned.1.call-start = ((), (), s32[]{:S(2)}) async-start(), calls=%async_computation.14 | async-start | bytes 9437184 | tf_op jit(solution)/shard_map/reduce_scatter | solution.py:303
  1694.3 359.1 %reduce-scatter.10.cloned.1.call-start = ((), (), s32[]{:S(2)}) async-start(), calls=%async_computation.16 | async-start | bytes 9437184 | tf_op jit(solution)/shard_map/reduce_scatter | solution.py:315
  1701.8 899.2 %reduce-scatter.12.cloned.1.call-start = ((), (), s32[]{:S(2)}) async-start(), calls=%async_computation.17 | async-start | bytes 37748736 | tf_op jit(solution)/shard_map/reduce_scatter | solution.py:327
  1718.4 1429.3 %reduce-scatter.14.cloned.1.call-start = ((), (), s32[]{:S(2)}) async-start(), calls=%async_computation.18 | async-start | bytes 37748736 | tf_op jit(solution)/shard_map/reduce_scatter | solution.py:333
  1735.2 1628.5 %all-reduce.16.cloned.1.call-start = ((), (), s32[]{:S(2)}) async-start(), calls=%async_computation.19 | async-start | bytes 21233664 | tf_op jit(solution)/shard_map/psum | solution.py:343
  3171.1 29.6 all-to-all-start.3
  3200.7 50.4 %all-to-all-start.1 = ((bf16[4,64,2048]{2,1,0:T(8,128)(2,1)}), bf16[4,64,2048]{2,1,0:T(8,128)(2,1)S(1)}, u32[]{:S(2)}, u32[]{:S(2)}) async-start(bf16[4,64,2048]{2,1,0:T(8,128)(2,1)} %get-tuple-element.105), calls=%async_computation.1 | async-start | bytes 2097152 | tf_op jit(solution)/shard_map/all_to_all | solution.py:380
  (79 other events, 489.2 us)
Sparse Core Ops, SparseCore 0:
  10.7 39.7 all-gather.12
  53.2 124.1 all-gather.14
  180.2 123.1 all-gather.16
  305.4 638.3 all-gather.18
  945.7 637.6 all-gather.20
  1686.8 61.0 reduce-scatter.7
  1752.6 148.6 reduce-scatter.5
  1905.4 147.9 reduce-scatter.9
  2057.7 543.1 reduce-scatter.11
  2605.0 542.5 reduce-scatter.13
  3151.0 212.7 all-reduce.15
where the time goes:
time: 3390 us; the launch traced here: 3380 us
  waiting for transfers between devices  2850 us (84%)
  matrix products  227 us (7%)
  blocking collectives  174 us (5%)
  other arithmetic  54.2 us (2%)
  starting transfers between devices  41.8 us (1%)
    all_gather x1, waiting for transfers between devices, shards(): lax.all_gather(low_up_weight, 'fsdp', axis=0, tiled=True)  631 us
    all_gather x1, waiting for transfers between devices, shards(): lax.all_gather(low_down_weight, 'fsdp', axis=0, tiled=True)  621 us
    reduce_scatter x1, waiting for transfers between devices, shards(): lax.psum_scatter(up_full.astype(jnp.bfloat16), 'fsdp', scatter_dimension=...  547 us
    reduce_scatter x1, waiting for transfers between devices, shards(): lax.psum_scatter(down_full.astype(jnp.bfloat16), 'fsdp', scatter_dimensio...  547 us
    reduce_scatter x1, waiting for transfers between devices, shards(): lax.psum_scatter(output_full.astype(jnp.bfloat16), 'fsdp', scatter_dimens...  152 us
    reduce_scatter x1, waiting for transfers between devices, shards(): lax.psum_scatter(query_full.astype(jnp.bfloat16), 'fsdp', scatter_dimensi...  114 us
    psum x1, waiting for transfers between devices, shards(): lax.psum(local_grads[2].astype(jnp.bfloat16), 'dp').astype(jnp.float32)  110 us
    all_gather x1, waiting for transfers between devices, shards(): lax.all_gather(low_output_weight, 'fsdp', axis=0, tiled=True)  98.1 us
  transfers between devices with their start and end apart: 15, of which 10 were waited for; matrix products, arithmetic and copies ran while one was open for 5% of the time, Pallas kernels for 0%

commit v1 on v0

v1 whole, which is shorter than its diff:
```python
import math

import jax
import jax.numpy as jnp
from jax import lax
from jax.experimental import pallas as pl
from jax.experimental.pallas import tpu as pltpu
from jax.sharding import Mesh
from jax.sharding import PartitionSpec as P

HEADS = 16
HEAD = 128
MB = 2
SEATS = 2
PACK = 80

epsilon = 1e-05
gelu_scale = 0.7978845608028654
gelu_cubic = 0.044715

DP = ("x", "c")


def low(values):
    return values.astype(jnp.bfloat16)


def wide(values):
    return values.astype(jnp.float32)


def product(left_mat, right_mat):
    return jnp.dot(left_mat, right_mat, preferred_element_type=jnp.float32)


def product_rows(left_mat, right_mat):
    return lax.dot_general(
        left_mat, right_mat, (((0,), (0,)), ((), ())), preferred_element_type=jnp.float32
    )


def product_cols(left_mat, right_mat):
    return lax.dot_general(
        left_mat, right_mat, (((1,), (1,)), ((), ())), preferred_element_type=jnp.float32
    )


def normalize(rows):
    center = rows - jnp.mean(rows, axis=-1, keepdims=True)
    spread = jnp.mean(center * center, axis=-1, keepdims=True)
    scale = lax.rsqrt(spread + epsilon)
    return center * scale, scale


def norm_back(grad_normed, gain, xhat, scale):
    g = grad_normed * gain
    inner = jnp.mean(g * xhat, axis=-1, keepdims=True)
    return scale * (g - jnp.mean(g, axis=-1, keepdims=True) - xhat * inner)


def gelu_parts(values):
    inner = jnp.tanh(gelu_scale * (values + gelu_cubic * values * values * values))
    activated = 0.5 * values * (1.0 + inner)
    slope = 0.5 * (1.0 + inner) + 0.5 * values * (1.0 - inner * inner) * gelu_scale * (
        1.0 + 3.0 * gelu_cubic * values * values
    )
    return activated, slope


MESH_ID = pl.DeviceIdType.MESH
VMEM_LIMIT = 56 * 1024 * 1024


class Spot:
    def __init__(self, depth):
        self.depth = depth
        self.z = lax.axis_index("z")
        self.y = lax.axis_index("y")
        self.x = lax.axis_index("x")
        self.c = lax.axis_index("c")
        self.to_c = {"c": 1 - self.c}
        self.to_x = {"x": 1 - self.x}
        self.to_y = {"y": 1 - self.y}
        self.to_xc = {"x": 1 - self.x, "c": 1 - self.c}
        self.up = {"z": self.z + 1}
        self.down = {"z": self.z - 1}

    def barrier(self, plane, line):
        bar = pltpu.get_barrier_semaphore()
        for to in plane:
            pl.semaphore_signal(bar, inc=1, device_id=to, device_id_type=MESH_ID)
        if line:

            @pl.when(self.z > 0)
            def _():
                pl.semaphore_signal(bar, inc=1, device_id=self.down, device_id_type=MESH_ID)

            @pl.when(self.z < self.depth - 1)
            def _():
                pl.semaphore_signal(bar, inc=1, device_id=self.up, device_id_type=MESH_ID)

        count = len(plane)
        if line:
            lower = jnp.where(self.z > 0, 1, 0)
            upper = jnp.where(self.z < self.depth - 1, 1, 0)
            count = count + lower + upper
        pl.semaphore_wait(bar, count)


class Net:
    def __init__(self, send_sems, recv_sems, local_sems):
        self.send_sems = send_sems
        self.recv_sems = recv_sems
        self.local_sems = local_sems
        self.count = 0
        self.local_count = 0
        self.open = []

    def remote(self, src, dst, to, arrives=None):
        copy = Copy(self, self.count, src, dst, to, arrives)
        self.count += 1
        return copy

    def local(self, src, dst):
        copy = pltpu.make_async_copy(src, dst, self.local_sems.at[self.local_count])
        self.local_count += 1
        return copy


class Copy:
    def __init__(self, net, index, src, dst, to, arrives):
        def make(target):
            return pltpu.make_async_remote_copy(
                src_ref=src,
                dst_ref=target,
                send_sem=net.send_sems.at[index],
                recv_sem=net.recv_sems.at[index],
                device_id=to,
                device_id_type=MESH_ID,
            )

        self.out = make(dst)
        self.into = make(dst if arrives is None else arrives)

    def start(self):
        self.out.start()

    def got(self):
        self.into.wait_recv()

    def sent(self):
        self.out.wait_send()


class PlaneGather:
    def __init__(self, net, spot, own, slots):
        def at(y, x, c):
            return y * 4 + x * 2 + c

        y, x, c = spot.y, spot.x, spot.c
        half = own.shape[0] // 2
        lo, hi = pl.ds(0, half), pl.ds(half, half)
        me = at(y, x, c)
        on_x, on_y, on_d = at(y, 1 - x, c), at(1 - y, x, c), at(1 - y, 1 - x, c)
        peer = [at(y, x, 1 - c), at(y, 1 - x, 1 - c), at(1 - y, x, 1 - c), at(1 - y, 1 - x, 1 - c)]

        def slot(index):
            return slots.at[index]

        self.keep = net.local(own, slot(me))
        self.x = net.remote(own, slot(me), spot.to_x, slot(on_x))
        self.y = net.remote(own, slot(me), spot.to_y, slot(on_y))
        self.c = net.remote(own, slot(me), spot.to_c, slot(peer[0]))
        self.x_on_y = net.remote(
            slots.at[on_x, lo], slots.at[on_x, lo], spot.to_y, slots.at[on_d, lo]
        )
        self.y_on_x = net.remote(
            slots.at[on_y, hi], slots.at[on_y, hi], spot.to_x, slots.at[on_d, hi]
        )
        self.x_on_c = net.remote(slot(on_x), slot(on_x), spot.to_c, slot(peer[1]))
        self.y_on_c = net.remote(slot(on_y), slot(on_y), spot.to_c, slot(peer[2]))
        self.lo_on_c = net.remote(
            slots.at[on_d, lo], slots.at[on_d, lo], spot.to_c, slots.at[peer[3], lo]
        )
        self.hi_on_c = net.remote(
            slots.at[on_d, hi], slots.at[on_d, hi], spot.to_c, slots.at[peer[3], hi]
        )

    def start(self):
        self.x.start()
        self.y.start()
        self.c.start()
        self.keep.start()

    def middle(self):
        self.x.got()
        self.x_on_y.start()
        self.x_on_c.start()
        self.y.got()
        self.y_on_x.start()
        self.y_on_c.start()

    def last(self):
        self.x_on_y.got()
        self.lo_on_c.start()
        self.y_on_x.got()
        self.hi_on_c.start()

    def finish(self):
        for copy in (self.c, self.x_on_c, self.y_on_c, self.lo_on_c, self.hi_on_c):
            copy.got()
        for copy in (
            self.x,
            self.y,
            self.c,
            self.x_on_y,
            self.y_on_x,
            self.x_on_c,
            self.y_on_c,
            self.lo_on_c,
            self.hi_on_c,
        ):
            copy.sent()
        self.keep.wait()

    remotes = 9
    locals = 1


def add_rows(into, other, step=32):
    rows = into.shape[0]

    @pl.loop(0, rows // step)
    def _(index):
        at = pl.ds(pl.multiple_of(index * step, step), step)
        into[at, :] = low(wide(into[at, :]) + wide(other[at, :]))


class PlaneScatter:
    remotes = 10

    @staticmethod
    def buffers(rows, width):
        return [
            pltpu.VMEM((4, rows, width), jnp.bfloat16),
            pltpu.VMEM((rows, width), jnp.bfloat16),
            pltpu.VMEM((rows, width), jnp.bfloat16),
            pltpu.VMEM((rows, width), jnp.bfloat16),
        ]

    def __init__(self, net, spot, parts, sums, diag, from_x, from_y):
        y, x, c = spot.y, spot.x, spot.c
        half = parts.shape[1] // 2
        lo, hi = pl.ds(0, half), pl.ds(half, half)
        self.own, self.nx, self.ny, self.nd = (
            y * 2 + x,
            y * 2 + 1 - x,
            (1 - y) * 2 + x,
            (1 - y) * 2 + 1 - x,
        )
        self.parts, self.sums, self.diag = parts, sums, diag
        self.from_x, self.from_y, self.c = from_x, from_y, c
        self.lo, self.hi = lo, hi
        self.first = {
            key: net.remote(parts.at[at * 2 + 1 - c], sums.at[at], spot.to_c)
            for key, at in (("d", self.nd), ("x", self.nx), ("y", self.ny), ("o", self.own))
        }
        self.d_lo = net.remote(sums.at[self.nd, lo], diag.at[lo], spot.to_x)
        self.d_hi = net.remote(sums.at[self.nd, hi], diag.at[hi], spot.to_y)
        self.x_lo = net.remote(sums.at[self.nx, lo], from_x.at[lo], spot.to_x)
        self.y_hi = net.remote(sums.at[self.ny, hi], from_y.at[hi], spot.to_y)
        self.x_hi = net.remote(sums.at[self.nx, hi], from_x.at[hi], spot.to_x)
        self.y_lo = net.remote(sums.at[self.ny, lo], from_y.at[lo], spot.to_y)

    def start(self):
        for copy in self.first.values():
            copy.start()

    def pair(self, key, at):
        self.first[key].got()
        add_rows(self.sums.at[at], self.parts.at[at * 2 + self.c])

    def middle(self):
        self.pair("d", self.nd)
        self.d_lo.start()
        self.d_hi.start()
        self.pair("x", self.nx)
        self.x_lo.start()
        self.pair("y", self.ny)
        self.y_hi.start()
        self.pair("o", self.own)

    def last(self):
        self.d_lo.got()
        add_rows(self.sums.at[self.ny, self.lo], self.diag.at[self.lo], 16)
        self.y_lo.start()
        self.d_hi.got()
        add_rows(self.sums.at[self.nx, self.hi], self.diag.at[self.hi], 16)
        self.x_hi.start()

    def finish(self, result):
        for copy in (self.x_lo, self.y_hi, self.x_hi, self.y_lo):
            copy.got()

        @pl.loop(0, result.shape[0] // 16)
        def _(index):
            at = pl.ds(pl.multiple_of(index * 16, 16), 16)
            result[at, :] = (
                wide(self.sums[self.own, at, :]) + wide(self.from_x[at, :]) + wide(self.from_y[at, :])
            )

        for copy in (
            *self.first.values(),
            self.d_lo,
            self.d_hi,
            self.x_lo,
            self.x_hi,
            self.y_lo,
            self.y_hi,
        ):
            copy.sent()


class LineGather:
    def __init__(self, net, spot, slots):
        self.spot, depth, z = spot, spot.depth, spot.z
        self.hops = []
        for step in range(depth - 1):
            lower = jnp.maximum(z - step, 0)
            upper = jnp.minimum(z + step, depth - 1)
            from_low = jnp.maximum(z - 1 - step, 0)
            from_high = jnp.minimum(z + 1 + step, depth - 1)
            self.hops.append(
                (
                    net.remote(slots(lower), slots(lower), spot.up, slots(from_low)),
                    net.remote(slots(upper), slots(upper), spot.down, slots(from_high)),
                )
            )

    @staticmethod
    def remotes(depth):
        return 2 * (depth - 1)

    def sends(self, step):
        z, last = self.spot.z, self.spot.depth - 1
        return (
            ((z >= step) & (z < last), self.hops[step][0]),
            ((z + step <= last) & (z > 0), self.hops[step][1]),
        )

    def takes(self, step):
        z, last = self.spot.z, self.spot.depth - 1
        return ((z >= step + 1, self.hops[step][0]), (z + step + 1 <= last, self.hops[step][1]))

    def start(self, step):
        for cond, copy in self.sends(step):
            pl.when(cond)(copy.start)

    def got(self, step):
        for cond, copy in self.takes(step):
            pl.when(cond)(copy.got)

    def hop(self, step):
        for (came, old), (goes, new) in zip(self.takes(step - 1), self.sends(step)):
            pl.when(came)(old.got)
            pl.when(goes)(new.start)

    def finish(self):
        for step in range(self.spot.depth - 1):
            for cond, copy in self.sends(step):
                pl.when(cond)(copy.sent)


class LineScatter:
    def __init__(self, net, spot, parts, from_low, from_high, add):
        self.spot, depth, z = spot, spot.depth, spot.z
        self.parts, self.from_low, self.from_high, self.add = parts, from_low, from_high, add
        self.ups, self.downs = [], []
        for step in range(depth - 1):
            self.ups.append(net.remote(parts(depth - 1 - step), from_low.at[step], spot.up))
            self.downs.append(net.remote(parts(step), from_high.at[step], spot.down))

    remotes = LineGather.remotes

    def stage(self, step):
        z, last = self.spot.z, self.spot.depth - 1
        up_to, down_to = last - step, step

        @pl.when((z > 0) & (z < up_to))
        def _():
            self.ups[step].got()
            self.add(self.parts(up_to), self.from_low.at[step])

        @pl.when(z < up_to)
        def _():
            self.ups[step].start()

        @pl.when((z < last) & (z > down_to))
        def _():
            self.downs[step].got()
            self.add(self.parts(down_to), self.from_high.at[step])

        @pl.when(z > down_to)
        def _():
            self.downs[step].start()

    def total(self):
        z, last = self.spot.z, self.spot.depth - 1
        for step in range(last):

            @pl.when((z > 0) & (z == last - step))
            def _():
                self.ups[step].got()
                self.add(self.parts(last - step), self.from_low.at[step])

            @pl.when((z < last) & (z == step))
            def _():
                self.downs[step].got()
                self.add(self.parts(step), self.from_high.at[step])

    def finish(self):
        z, last = self.spot.z, self.spot.depth - 1
        for step in range(last):
            pl.when(z < last - step)(self.ups[step].sent)
            pl.when(z > step)(self.downs[step].sent)


class DpGather:
    remotes = 3

    def __init__(self, net, spot, own, slots):
        me = spot.x * 2 + spot.c
        on_x = (1 - spot.x) * 2 + spot.c
        self.keep = net.local(own, slots.at[me])
        self.x = net.remote(own, slots.at[me], spot.to_x, slots.at[on_x])
        self.c = net.remote(own, slots.at[me], spot.to_c, slots.at[spot.x * 2 + 1 - spot.c])
        self.x_on_c = net.remote(
            slots.at[on_x],
            slots.at[on_x],
            spot.to_c,
            slots.at[(1 - spot.x) * 2 + 1 - spot.c],
        )

    def start(self):
        self.x.start()
        self.c.start()
        self.keep.start()

    def last(self):
        self.x.got()
        self.x_on_c.start()

    def finish(self):
        self.c.got()
        self.x_on_c.got()
        for copy in (self.x, self.c, self.x_on_c):
            copy.sent()
        self.keep.wait()


class DpExchange:
    remotes = 3

    def __init__(self, net, spot, parts, slots):
        me = spot.x * 2 + spot.c
        on_x = (1 - spot.x) * 2 + spot.c
        on_c = spot.x * 2 + 1 - spot.c
        on_xc = (1 - spot.x) * 2 + 1 - spot.c
        self.keep = net.local(parts.at[me], slots.at[me])
        self.moves = [
            net.remote(parts.at[at], slots.at[me], to, slots.at[at])
            for at, to in ((on_xc, spot.to_xc), (on_x, spot.to_x), (on_c, spot.to_c))
        ]

    def start(self):
        for copy in self.moves:
            copy.start()
        self.keep.start()

    def got(self):
        for copy in self.moves:
            copy.got()
        self.keep.wait()

    def finish(self):
        for copy in self.moves:
            copy.sent()


def net_scratch(remotes, locals_):
    return [
        pltpu.SemaphoreType.DMA((remotes,)),
        pltpu.SemaphoreType.DMA((remotes,)),
        pltpu.SemaphoreType.DMA((max(locals_, 1),)),
    ]


ANY = pl.BlockSpec(memory_space=pl.ANY)
IN_VMEM = pl.BlockSpec(memory_space=pltpu.VMEM)


def comm_params(collective_id):
    return pltpu.CompilerParams(
        collective_id=collective_id, has_side_effects=True, vmem_limit_bytes=VMEM_LIMIT
    )


def plane_gather(block, depth, collective_id):
    rows, width = block.shape

    def kernel(own, slots, *sems):
        spot = Spot(depth)
        net = Net(*sems)
        gather = PlaneGather(net, spot, own, slots)
        spot.barrier((spot.to_c, spot.to_x, spot.to_y), False)
        gather.start()
        gather.middle()
        gather.last()
        gather.finish()

    out = pl.pallas_call(
        kernel,
        out_shape=jax.ShapeDtypeStruct((8, rows, width), block.dtype),
        in_specs=[ANY],
        out_specs=ANY,
        scratch_shapes=net_scratch(PlaneGather.remotes, 1),
        compiler_params=comm_params(collective_id),
    )(block)
    return out.reshape(8 * rows, width)


def plane_scatter(parts, depth, collective_id):
    count = len(parts)
    rows, width = parts[0].shape[0] // 8, parts[0].shape[1]

    def kernel(*refs):
        sources, results = refs[:count], refs[count : 2 * count]
        scratch = refs[2 * count : -3]
        spot = Spot(depth)
        net = Net(*refs[-3:])
        runs = [
            PlaneScatter(net, spot, source, *scratch[4 * index : 4 * index + 4])
            for index, source in enumerate(sources)
        ]
        spot.barrier((spot.to_c, spot.to_x, spot.to_y), False)
        for run in runs:
            run.start()
        for run in runs:
            run.middle()
        for run in runs:
            run.last()
        for run, result in zip(runs, results):
            run.finish(result)

    return pl.pallas_call(
        kernel,
        out_shape=[jax.ShapeDtypeStruct((rows, width), jnp.float32)] * count,
        in_specs=[IN_VMEM] * count,
        out_specs=[IN_VMEM] * count,
        scratch_shapes=PlaneScatter.buffers(rows, width) * count
        + net_scratch(PlaneScatter.remotes * count, 1),
        compiler_params=comm_params(collective_id),
    )(*[item.reshape(8, rows, width) for item in parts])


def first_gather(
    depth, tokens, cotangent, attn_mine, attn_other, small, out_slice, up_mine, up_other, down_slice
):
    flat, width = tokens.shape
    low_type = jnp.bfloat16

    def shape(*dims):
        return jax.ShapeDtypeStruct(dims, low_type)

    def kernel(
        tok, cot, attn_m, attn_o, small_m, out_m, up_m, up_o, down_m,
        tok_all, cot_all, attn_all, small_all, out_all, out_dealt, up_all, down_all,
        *sems,
    ):
        spot = Spot(depth)
        net = Net(*sems)
        z, y = spot.z, spot.y
        tok_run = PlaneGather(net, spot, tok, tok_all)
        cot_run = PlaneGather(net, spot, cot, cot_all)
        group = depth // 4
        keep_out = net.local(out_m, out_all.at[z // group, z % group])
        keep_attn = net.local(attn_m, attn_all.at[z, y])
        keep_small = net.local(small_m, small_all.at[z, y])
        keep_up = net.local(up_m, up_all.at[z, y])
        keep_down = net.local(down_m, down_all.at[z])
        y_attn = net.remote(attn_o, attn_all.at[z, y], spot.to_y, attn_all.at[z, 1 - y])
        y_small = net.remote(small_m, small_all.at[z, y], spot.to_y, small_all.at[z, 1 - y])
        y_up = net.remote(up_o, up_all.at[z, y], spot.to_y, up_all.at[z, 1 - y])
        run_out = LineGather(net, spot, lambda at: out_all.at[at // group, at % group])
        run_attn = LineGather(net, spot, lambda at: attn_all.at[at])
        run_small = LineGather(net, spot, lambda at: small_all.at[at])
        run_up = LineGather(net, spot, lambda at: up_all.at[at])
        run_down = LineGather(net, spot, lambda at: down_all.at[at])
        deal = DpExchange(net, spot, out_all, out_dealt)
        spot.barrier((spot.to_c, spot.to_x, spot.to_y, spot.to_xc), True)
        keep_out.start()
        y_attn.start()
        y_small.start()
        keep_attn.start()
        keep_small.start()
        y_up.start()
        keep_down.start()
        keep_up.start()
        tok_run.start()
        keep_out.wait()
        run_out.start(0)
        keep_attn.wait()
        y_attn.got()
        run_attn.start(0)
        keep_small.wait()
        y_small.got()
        run_small.start(0)
        keep_down.wait()
        run_down.start(0)
        keep_up.wait()
        y_up.got()
        run_up.start(0)
        tok_run.middle()
        for step in range(1, depth - 1):
            run_out.hop(step)
            run_attn.hop(step)
            run_small.hop(step)
        tok_run.last()
        cot_run.start()
        for run in (run_out, run_attn, run_small):
            run.got(depth - 2)
        deal.start()
        cot_run.middle()
        cot_run.last()
        for step in range(1, depth - 1):
            run_down.hop(step)
            run_up.hop(step)
        deal.got()
        run_down.got(depth - 2)
        run_up.got(depth - 2)
        for run in (run_out, run_attn, run_small, run_up, run_down, tok_run, cot_run, deal):
            run.finish()
        for copy in (y_attn, y_small, y_up):
            copy.sent()

    remotes = 2 * PlaneGather.remotes + 3 + 5 * LineGather.remotes(depth) + DpExchange.remotes
    return pl.pallas_call(
        kernel,
        out_shape=[
            shape(8, flat, width),
            shape(8, flat, width),
            shape(depth, 2, *attn_mine.shape),
            shape(depth, 2, *small.shape),
            shape(4, depth // 4, *out_slice.shape),
            shape(4, depth // 4, *out_slice.shape),
            shape(depth, 2, *up_mine.shape),
            shape(depth, *down_slice.shape),
        ],
        in_specs=[ANY] * 9,
        out_specs=[ANY] * 8,
        scratch_shapes=net_scratch(remotes, 8),
        compiler_params=comm_params(1),
    )(tokens, cotangent, attn_mine, attn_other, small, out_slice, up_mine, up_other, down_slice)


def last_scatter(depth, d_up, d_down, d_attn, d_vec, d_out, grad_parts):
    rows, width = grad_parts.shape[1:]
    low_type = jnp.bfloat16

    def shape(*dims):
        return jax.ShapeDtypeStruct(dims, low_type)

    def add2(into, other):
        add_rows(into, other, 16)

    def add3(into, other):
        for at in range(2):
            add_rows(into.at[at], other.at[at], 16)

    def kernel(
        up, down, attn, vec, out, parts,
        up_all, down_all, attn_all, vec_all, out_all, own_sum,
        up_lo, up_hi, down_lo, down_hi, attn_lo, attn_hi, vec_lo, vec_hi, out_lo, out_hi,
        out_mix, up_got, attn_got, vec_got, sums, diag, from_x, from_y, *sems,
    ):
        spot = Spot(depth)
        net = Net(*sems)
        z, y = spot.z, spot.y
        deal = DpExchange(net, spot, out, out_mix)
        group = depth // 4

        def mixed(at):
            return out_mix.at[at // group, at % group]

        run_up = LineScatter(net, spot, lambda at: up.at[at], up_lo, up_hi, add3)
        run_down = LineScatter(net, spot, lambda at: down.at[at], down_lo, down_hi, add2)
        run_attn = LineScatter(net, spot, lambda at: attn.at[at], attn_lo, attn_hi, add3)
        run_vec = LineScatter(net, spot, lambda at: vec.at[at], vec_lo, vec_hi, add3)
        run_out = LineScatter(net, spot, mixed, out_lo, out_hi, add2)
        plane = PlaneScatter(net, spot, parts, sums, diag, from_x, from_y)
        y_up = net.remote(up.at[z, 1 - y], up_got, spot.to_y)
        y_attn = net.remote(attn.at[z, 1 - y], attn_got, spot.to_y)
        y_vec = net.remote(vec.at[z, 1 - y], vec_got, spot.to_y)
        dp_up = DpGather(net, spot, up.at[z, y], up_all.at[0])
        dp_up2 = DpGather(net, spot, up_got, up_all.at[1])
        dp_down = DpGather(net, spot, down.at[z], down_all)
        dp_attn = DpGather(net, spot, attn.at[z, y], attn_all.at[0])
        dp_attn2 = DpGather(net, spot, attn_got, attn_all.at[1])
        dp_vec = DpGather(net, spot, vec.at[z, y], vec_all)
        dp_out = DpGather(net, spot, mixed(z), out_all)
        spot.barrier((spot.to_c, spot.to_x, spot.to_y, spot.to_xc), True)
        deal.start()
        run_down.stage(0)
        run_up.stage(0)
        plane.start()
        plane.middle()
        for step in range(1, depth - 1):
            run_down.stage(step)
        plane.last()
        for step in range(1, depth - 1):
            run_up.stage(step)
        run_down.total()
        deal.got()
        run_attn.stage(0)
        run_vec.stage(0)
        run_out.stage(0)
        dp_down.start()
        plane.finish(own_sum)
        run_up.total()
        y_up.start()
        dp_up.start()
        for step in range(1, depth - 1):
            run_attn.stage(step)
            run_vec.stage(step)
            run_out.stage(step)
        dp_down.last()
        y_up.got()
        dp_up2.start()
        dp_up.last()
        run_attn.total()
        run_vec.total()
        y_attn.start()
        y_vec.start()
        dp_attn.start()
        run_out.total()
        dp_out.start()
        dp_up2.last()
        y_vec.got()
        y_vec.sent()
        add_rows(vec.at[z, y], vec_got, 16)
        dp_vec.start()
        y_attn.got()
        dp_attn2.start()
        dps = (dp_attn, dp_out, dp_vec, dp_attn2)
        for run in dps:
            run.last()
        for run in (dp_down, dp_up, dp_up2, *dps):
            run.finish()
        for run in (run_up, run_down, run_attn, run_vec, run_out, deal):
            run.finish()
        y_up.sent()
        y_attn.sent()

    remotes = (
        DpExchange.remotes
        + 5 * LineGather.remotes(depth)
        + PlaneScatter.remotes
        + 3
        + 7 * DpGather.remotes
    )
    one = depth - 1

    def twice(*dims):
        return [pltpu.VMEM(dims, low_type)] * 2

    return pl.pallas_call(
        kernel,
        out_shape=[
            shape(2, 4, *d_up.shape[2:]),
            shape(4, *d_down.shape[1:]),
            shape(2, 4, *d_attn.shape[2:]),
            shape(4, *d_vec.shape[2:]),
            shape(4, *d_out.shape[2:]),
            jax.ShapeDtypeStruct((rows, width), jnp.float32),
        ],
        in_specs=[IN_VMEM] * 6,
        out_specs=[ANY] * 5 + [IN_VMEM],
        scratch_shapes=[
            *twice(one, *d_up.shape[1:]),
            *twice(one, *d_down.shape[1:]),
            *twice(one, *d_attn.shape[1:]),
            *twice(one, *d_vec.shape[1:]),
            *twice(one, *d_out.shape[2:]),
            pltpu.VMEM(d_out.shape, low_type),
            pltpu.VMEM(d_up.shape[2:], low_type),
            pltpu.VMEM(d_attn.shape[2:], low_type),
            pltpu.VMEM(d_vec.shape[2:], low_type),
            *PlaneScatter.buffers(rows, width),
            *net_scratch(remotes, 8),
        ],
        compiler_params=comm_params(2),
    )(d_up, d_down, d_attn, d_vec, d_out, grad_parts)


def build(mesh):
    fsdp_size = mesh.shape["fsdp"]
    depth = fsdp_size // 2
    y_slow = depth != 4
    owner_axes = ("y", "z") if y_slow else ("z", "y")

    def owner(z_at, y_at):
        return y_at * depth + z_at if y_slow else z_at * 2 + y_at

    def shards(
        tokens,
        cotangent,
        lengths,
        dealing,
        attn_gain,
        attn_shift,
        query_weight,
        query_bias,
        keyval_weight,
        value_bias,
        output_weight,
        output_bias,
        mlp_gain,
        mlp_shift,
        up_weight,
        up_bias,
        down_weight,
        down_bias,
    ):
        held, slot_len, width = tokens.shape
        my_z = lax.axis_index("z")
        my_y = lax.axis_index("y")
        my_xc = lax.axis_index("x") * 2 + lax.axis_index("c")
        member = my_y * 4 + my_xc
        rows_own = query_weight.shape[0]
        ff = up_weight.shape[1]
        ff_own = down_weight.shape[0]
        ff_seg = ff_own // 4
        out_seg = rows_own // 4
        head_cols = width // 8
        group_seqs = held * 4

        def group_table(table):
            parts = [
                lax.dynamic_slice_in_dim(table, owner(my_z, y_at) * group_seqs, group_seqs)
                for y_at in range(2)
            ]
            return jnp.stack(parts)

        bases = jnp.stack([owner(my_z, y_at) * group_seqs for y_at in range(2)])
        in_group = group_table(dealing) - bases[:, None]
        source = in_group + (jnp.arange(2) * group_seqs)[:, None]
        micro = 2 * 4 * MB
        lens = group_table(lengths).reshape(micro, SEATS)
        source = source.reshape(micro, SEATS)
        ends = jnp.concatenate([lens[:, :1], lens[:, :1] + lens[:, 1:]], axis=1)
        starts = ends - lens
        at = jnp.arange(PACK)
        inside = (at[None, :, None] >= starts[:, None, :]) & (at[None, :, None] < ends[:, None, :])
        row_valid = jnp.any(inside, axis=2)
        seat = jnp.sum(jnp.where(inside, jnp.arange(SEATS)[None, None, :], 0), axis=2)
        segment = jnp.where(row_valid, seat, -1)
        offset = at[None, :] - jnp.sum(jnp.where(inside, starts[:, None, :], 0), axis=2)
        source_row = jnp.sum(jnp.where(inside, source[:, None, :], 0), axis=2) * slot_len + offset
        source_row = jnp.where(row_valid, source_row, 0).reshape(micro * PACK)
        valid = row_valid.reshape(micro * PACK)
        allowed = (
            (at[None, :, None] >= at[None, None, :])
            & (segment[:, :, None] == segment[:, None, :])
            & row_valid[:, None, :]
        )

        def up_columns(y_at):
            cols = [
                lax.dynamic_slice_in_dim(
                    up_weight, owner(z_at, y_at) * ff_own + my_xc * ff_seg, ff_seg, axis=1
                )
                for z_at in range(depth)
            ]
            return low(jnp.concatenate(cols, axis=1))

        def head_base(y_at):
            return owner(my_xc * (depth // 4), y_at) * rows_own

        def query_columns(y_at):
            return low(lax.dynamic_slice_in_dim(query_weight, head_base(y_at), head_cols, axis=1))

        small_parts = [
            attn_gain,
            attn_shift,
            output_bias,
            mlp_gain,
            mlp_shift,
            down_bias,
            query_bias,
            up_bias,
            value_bias,
        ]
        small = low(jnp.concatenate(small_parts))
        small_count = small.shape[0]
        small = jnp.pad(small, (0, 16 * 256 - small_count)).reshape(16, 256)
        attn_mine = jnp.concatenate([query_columns(my_y), low(keyval_weight)], axis=1)
        attn_other = jnp.concatenate([query_columns(1 - my_y), low(keyval_weight)], axis=1)
        out_slice = low(lax.dynamic_slice_in_dim(output_weight, my_xc * out_seg, out_seg, axis=0))
        down_slice = low(lax.dynamic_slice_in_dim(down_weight, my_xc * ff_seg, ff_seg, axis=0))
        flat = held * slot_len
        (
            tokens_all,
            cotangent_all,
            attn_all,
            small_all,
            _,
            out_dealt,
            up_all,
            w_down,
        ) = first_gather(
            depth,
            tokens.reshape(flat, width),
            cotangent.reshape(flat, width),
            attn_mine,
            attn_other,
            small,
            out_slice,
            up_columns(my_y),
            up_columns(1 - my_y),
            down_slice,
        )
        tokens_all = tokens_all.reshape(8 * flat, width)
        cotangent_all = cotangent_all.reshape(8 * flat, width)
        w_down = w_down.reshape(depth * ff_seg, width)
        if y_slow:
            small_all = jnp.transpose(small_all, (1, 0, 2, 3))
        gathered_small = wide(small_all.reshape(fsdp_size, 16 * 256)[:, :small_count])
        sizes = [item.shape[0] for item in small_parts]
        begins = [sum(sizes[:index]) for index in range(len(sizes))]
        (
            gain_a,
            shift_a,
            bias_o,
            gain_m,
            shift_m,
            bias_d,
            bias_q,
            bias_u,
            bias_v,
        ) = [
            gathered_small[:, start : start + size].reshape(-1)
            for start, size in zip(begins, sizes)
        ]
        my_bias_q = lax.dynamic_slice_in_dim(bias_q, head_base(my_y), head_cols)
        my_bias_u = jnp.concatenate(
            [
                lax.dynamic_slice_in_dim(
                    bias_u, owner(z_at, my_y) * ff_own + my_xc * ff_seg, ff_seg
                )
                for z_at in range(depth)
            ]
        )
        bias_kv = jnp.concatenate([jnp.zeros((HEAD,), jnp.float32), bias_v])

        def rows_in_order(gathered):
            if y_slow:
                gathered = jnp.transpose(gathered, (1, 0, 2, 3))
            return gathered.reshape(width, gathered.shape[-1])

        def rows_by_z(values):
            if y_slow:
                return jnp.transpose(
                    values.reshape(2, depth, rows_own, values.shape[-1]), (1, 0, 2, 3)
                )
            return values.reshape(depth, 2, rows_own, values.shape[-1])

        attn_full = rows_in_order(attn_all)
        w_query = attn_full[:, :head_cols]
        w_keyval = attn_full[:, head_cols:]
        w_output = jnp.transpose(out_dealt, (1, 0, 2, 3)).reshape(head_cols, width)
        w_up = rows_in_order(up_all)

        packed = jnp.take(tokens_all, source_row, axis=0)
        grad_mixed = jnp.where(
            valid[:, None], jnp.take(cotangent_all, source_row, axis=0), jnp.zeros((), jnp.bfloat16)
        )
        own_count = MB * PACK
        own_rows = wide(lax.dynamic_slice_in_dim(packed, member * own_count, own_count))
        own_valid = lax.dynamic_slice_in_dim(valid, member * own_count, own_count)[:, None]
        own_grad = wide(lax.dynamic_slice_in_dim(grad_mixed, member * own_count, own_count))

        xhat_all, _ = normalize(wide(packed))
        normed_attn = low(xhat_all * gain_a + shift_a)
        query = low(product(normed_attn, w_query) + my_bias_q)
        keyval = low(product(normed_attn, w_keyval) + bias_kv)
        my_heads = head_cols // HEAD
        query_h = query.reshape(micro, PACK, my_heads, HEAD)
        keys = keyval[:, :HEAD].reshape(micro, PACK, HEAD)
        vals = keyval[:, HEAD:].reshape(micro, PACK, HEAD)
        score_scale = 1.0 / math.sqrt(HEAD)
        scores = (
            jnp.einsum("mshd,mtd->mhst", query_h, keys, preferred_element_type=jnp.float32)
            * score_scale
        )
        scores = jnp.where(allowed[:, None], scores, -1e30)
        expscores = jnp.exp(scores - jnp.max(scores, axis=-1, keepdims=True))
        probs = expscores / jnp.sum(expscores, axis=-1, keepdims=True)
        attended = low(
            jnp.einsum(
                "mhst,mtd->mshd", low(probs), vals, preferred_element_type=jnp.float32
            ).reshape(micro * PACK, head_cols)
        )
        (attn_out,) = plane_scatter([low(product(attended, w_output))], depth, 3)
        middle = own_rows + (attn_out + bias_o)
        xhat_m, scale_m = normalize(middle)
        normed_mlp = plane_gather(low(xhat_m * gain_m + shift_m), depth, 4)
        hidden = product(normed_mlp, w_up) + my_bias_u
        activated, slope = gelu_parts(hidden)
        activated = low(activated)
        grad_hidden = low(slope * product_cols(grad_mixed, w_down))
        mlp_sum, grad_normed = plane_scatter(
            [low(product(activated, w_down)), low(product_cols(grad_hidden, w_up))], depth, 5
        )
        block_own = low(jnp.where(own_valid, middle + (mlp_sum + bias_d), 0.0))
        grad_middle = own_grad + norm_back(grad_normed, gain_m, xhat_m, scale_m)
        d_down = low(product_rows(activated, grad_mixed)).reshape(depth, ff_seg, width)
        d_up = rows_by_z(low(product_rows(normed_mlp, grad_hidden)))

        grad_branch_own = low(grad_middle)
        grad_branch = plane_gather(grad_branch_own, depth, 6)
        d_output = low(product_rows(attended, grad_branch))
        grad_att = low(product_cols(grad_branch, w_output)).reshape(micro, PACK, my_heads, HEAD)
        grad_probs = jnp.einsum("mshd,mtd->mhst", grad_att, vals, preferred_element_type=jnp.float32)
        grad_vals = jnp.einsum(
            "mhst,mshd->mtd", low(probs), grad_att, preferred_element_type=jnp.float32
        )
        inner = jnp.sum(probs * grad_probs, axis=-1, keepdims=True)
        grad_scores = low(probs * (grad_probs - inner))
        grad_query = (
            jnp.einsum("mhst,mtd->mshd", grad_scores, keys, preferred_element_type=jnp.float32)
            * score_scale
        )
        grad_query = low(grad_query.reshape(micro * PACK, head_cols))
        grad_keys = (
            jnp.einsum("mhst,mshd->mtd", grad_scores, query_h, preferred_element_type=jnp.float32)
            * score_scale
        )
        grad_keyval = low(jnp.concatenate([grad_keys, grad_vals], axis=2)).reshape(
            micro * PACK, 2 * HEAD
        )
        d_query = low(product_rows(normed_attn, grad_query))
        d_keyval = low(product_rows(normed_attn, grad_keyval))
        grad_input_part = product_cols(grad_query, w_query) + product_cols(grad_keyval, w_keyval)
        own_xhat, own_scale = normalize(own_rows)

        def colsum(values):
            return jnp.sum(wide(values), axis=0)

        def spread_vec(values, parts, size, full):
            out = jnp.zeros((full,), jnp.float32)
            for index, begin in enumerate(parts):
                out = lax.dynamic_update_slice(
                    out, values[index * size : (index + 1) * size], (begin,)
                )
            return out

        vec_query = spread_vec(colsum(grad_query), [head_base(my_y)], head_cols, width)
        vec_up = spread_vec(
            colsum(grad_hidden),
            [owner(z_at, my_y) * ff_own + my_xc * ff_seg for z_at in range(depth)],
            ff_seg,
            ff,
        )
        vectors = [
            jnp.sum(grad_input_part * xhat_all, axis=0),
            jnp.sum(grad_input_part, axis=0),
            colsum(grad_branch_own),
            jnp.sum(grad_normed * xhat_m, axis=0),
            jnp.sum(grad_normed, axis=0),
            jnp.sum(own_grad, axis=0),
            vec_query,
            vec_up,
            colsum(grad_keyval[:, HEAD:]),
        ]
        vectors = jnp.concatenate([item.reshape(fsdp_size, -1) for item in vectors], axis=1)
        vectors = jnp.pad(low(vectors), ((0, 0), (0, 16 * 256 - small_count)))
        if y_slow:
            d_vec = jnp.transpose(vectors.reshape(2, depth, 16, 256), (1, 0, 2, 3))
        else:
            d_vec = vectors.reshape(depth, 2, 16, 256)

        d_attn = rows_by_z(jnp.concatenate([d_query, d_keyval], axis=1))
        d_out_parts = jnp.transpose(
            d_output.reshape(depth // 4, 4, out_seg, width), (1, 0, 2, 3)
        )
        up_all, down_all, attn_all, vec_all, out_all, grad_first = last_scatter(
            depth,
            d_up,
            d_down,
            d_attn,
            d_vec,
            d_out_parts,
            low(grad_input_part).reshape(8, MB * PACK, width),
        )
        grad_input = low(grad_middle + norm_back(grad_first, gain_a, own_xhat, own_scale))

        def by_y(pair):
            first = my_y == 0
            return (
                jnp.where(first, pair[0], pair[1]),
                jnp.where(first, pair[1], pair[0]),
            )

        up_pair = [item.reshape(4, rows_own, depth, ff_seg) for item in by_y(up_all)]
        if y_slow:
            up_grad = jnp.stack([jnp.transpose(item, (1, 2, 0, 3)) for item in up_pair], axis=1)
        else:
            up_grad = jnp.stack([jnp.transpose(item, (1, 2, 0, 3)) for item in up_pair], axis=2)
        up_grad = wide(up_grad.reshape(rows_own, ff))
        query_pair = by_y(attn_all[..., :head_cols])
        if y_slow:
            query_grad = jnp.stack([jnp.transpose(item, (1, 0, 2)) for item in query_pair], axis=1)
        else:
            query_grad = jnp.stack([jnp.transpose(item, (1, 0, 2)) for item in query_pair], axis=2)
        query_grad = wide(query_grad.reshape(rows_own, width))
        keyval_grad = jnp.sum(wide(attn_all[..., head_cols:]), axis=(0, 1))
        down_grad = wide(down_all.reshape(ff_own, width))
        output_grad = wide(out_all.reshape(rows_own, width))
        vec_own = jnp.sum(wide(vec_all), axis=0).reshape(16 * 256)
        (
            gain_a_grad,
            shift_a_grad,
            bias_o_grad,
            gain_m_grad,
            shift_m_grad,
            bias_d_grad,
            bias_q_grad,
            bias_u_grad,
            bias_v_grad,
        ) = [vec_own[start : start + size] for start, size in zip(begins, sizes)]

        dealt_here = lax.dynamic_index_in_dim(in_group, my_y, 0, keepdims=False)
        holders = (dealt_here // held).reshape(4, held)
        slots = (dealt_here % held).reshape(4, held)
        my_holders = lax.dynamic_index_in_dim(holders, my_xc, 0, keepdims=False)
        my_lens = lax.dynamic_slice_in_dim(lens, member * MB, MB).reshape(held)
        my_starts = (
            lax.dynamic_slice_in_dim(starts, member * MB, MB) + jnp.arange(MB)[:, None] * PACK
        ).reshape(held)
        send_seq = jnp.argmax(my_holders[None, :] == jnp.arange(4)[:, None], axis=1)
        pos = jnp.arange(slot_len)
        live = pos[None, :] < my_lens[send_seq][:, None]
        send_rows = jnp.where(live, my_starts[send_seq][:, None] + pos[None, :], 0)
        slot_of = jnp.sum(jnp.where(holders == my_xc, slots, 0), axis=1)
        from_dev = jnp.argmax(slot_of[None, :] == jnp.arange(held)[:, None], axis=1)

        def send_back(own):
            out = jnp.where(
                live[..., None], jnp.take(own, send_rows, axis=0), jnp.zeros((), jnp.bfloat16)
            )
            got = lax.all_to_all(out, DP, split_axis=0, concat_axis=0, tiled=True)
            return jnp.stack(
                [
                    lax.dynamic_index_in_dim(got, from_dev[index], 0, keepdims=False)
                    for index in range(held)
                ]
            )

        return (
            send_back(block_own),
            send_back(grad_input),
            gain_a_grad,
            shift_a_grad,
            query_grad,
            bias_q_grad,
            keyval_grad,
            bias_v_grad,
            output_grad,
            bias_o_grad,
            gain_m_grad,
            shift_m_grad,
            up_grad,
            bias_u_grad,
            down_grad,
            bias_d_grad,
        )

    return shards, depth, owner_axes


def solution(mesh):
    shards, depth, owner_axes = build(mesh)
    sizes = {"z": depth, "y": 2}
    fine = Mesh(
        mesh.devices.reshape(sizes[owner_axes[0]], sizes[owner_axes[1]], 2, 2),
        owner_axes + ("x", "c"),
    )
    rows = P(owner_axes + ("x", "c"), None, None)
    vec = P(owner_axes)
    mat = P(owner_axes, None)
    in_specs = (
        rows, rows, P(), P(),
        vec, vec, mat, vec, mat, vec, mat, vec, vec, vec, mat, vec, mat, vec,
    )
    out_specs = (
        rows, rows,
        vec, vec, mat, vec, mat, vec, mat, vec, vec, vec, mat, vec, mat, vec,
    )
    return jax.shard_map(shards, mesh=fine, in_specs=in_specs, out_specs=out_specs, check_vma=False)
```

time: 3390 us -> 964 us (0.28)
  waiting for transfers between devices: 2850 us -> 0.01 us
  Pallas kernels: 0 us -> 679 us
  blocking collectives: 174 us -> 0 us
  matrix products: 227 us -> 91 us
  local copies, waits for them, and re-layouts: 22.7 us -> 101 us
    reduce_scatter x5 -> x0, waiting for transfers between devices: 1360 us -> none  [the longest x1 547 us: shards(): lax.psum_scatter(up_full.astype(jnp.bfloat16), 'fsdp', scatter_dimension=...]
    all_gather x5 -> x0, waiting for transfers between devices: 1350 us -> none  [the longest x1 631 us: shards(): lax.all_gather(low_up_weight, 'fsdp', axis=0, tiled=True)]
    pallas_call x0 -> x6, Pallas kernels: none -> 679 us  [the longest x1 286 us: last_scatter(): pl.pallas_call(kernel, out_shape=[shape(2, 4, *d_up.shape[2:]), shape(4,...]
    all_gather x8 -> x0, blocking collectives: 118 us -> none  [the longest x1 22.3 us: shards(): lax.all_gather(low_up_bias, 'fsdp', axis=0, tiled=True)]
    psum x1 -> x0, waiting for transfers between devices: 110 us -> none  [shards(): lax.psum(local_grads[2].astype(jnp.bfloat16), 'dp').astype(jnp.float32)]
    dot_general x10 -> x5, matrix products: 93.5 us -> 36.2 us  [product_cols(): lax.dot_general(left_mat, right_mat, (((1,), (1,)), ((), ())), preferred_...]
    dot_general x10 -> x5, matrix products: 82.9 us -> 26.8 us  [product(): return jnp.dot(left_mat, right_mat, preferred_element_type=jnp.float32)]
    unnamed x2 -> x0, blocking collectives: 43.7 us -> none
  transfers between devices with their start and end apart: 15 -> 2, of which waited for: 10 -> 0; matrix products, arithmetic and copies ran while one was open for 5% -> 6% of each run, Pallas kernels for 0% -> 0%
where the time goes in v1:
time: 964 us; the launch traced here: 954 us
  Pallas kernels  679 us (70%)
  local copies, waits for them, and re-layouts  101 us (10%)
  matrix products  91 us (9%)
  other arithmetic  64.3 us (7%)
  between operations  10.2 us (1%)
    pallas_call x1, Pallas kernels, last_scatter(): pl.pallas_call(kernel, out_shape=[shape(2, 4, *d_up.shape[2:]), shape(4,...  286 us
    pallas_call x1, Pallas kernels, first_gather(): pl.pallas_call(kernel, out_shape=[shape(8, flat, width), shape(8, flat, w...  249 us
    pallas_call x2, Pallas kernels, plane_scatter(): pl.pallas_call(kernel, out_shape=[jax.ShapeDtypeStruct((rows, width), jnp...  86.8 us
    pallas_call x2, Pallas kernels, plane_gather(): pl.pallas_call(kernel, out_shape=jax.ShapeDtypeStruct((8, rows, width), b...  56.8 us
    dot_general x5, matrix products, product_cols(): lax.dot_general(left_mat, right_mat, (((1,), (1,)), ((), ())), preferred_...  36.2 us
    dot_general x5, matrix products, product(): return jnp.dot(left_mat, right_mat, preferred_element_type=jnp.float32)  26.8 us
    dot_general x5, matrix products, product_rows(): lax.dot_general(left_mat, right_mat, (((0,), (0,)), ((), ())), preferred_...  23.6 us
    unnamed x129, local copies, waits for them, and re-layouts  22.8 us
  transfers between devices with their start and end apart: 2, of which 0 were waited for; matrix products, arithmetic and copies ran while one was open for 6% of the time, Pallas kernels for 0%

profile of v1, /device:TPU:9, one launch (start us, length us, event | category | flops | bytes accessed | tf_op | source)
XLA Modules:
  0.0 954.1 jit_solution(11275243143000550881)
XLA Ops:
  24.7 249.5 %shard_map.297 = (bf16[8,256,2048]{2,1,0:T(8,128)(2,1)}, bf16[8,256,2048]{2,1,0:T(8,128)(2,1)}, bf16[4,2,256,512]{3,2,1,0:T(8,128)(2,1)}, bf16[4,2,16,256]{3,2,1...) custom-call(bf16[256,2048]{1,0:T(8,128)(2,1)} %bitcast.227, ...), custom_call_target="tpu_custom_call" | custom-call | tf_op jit(solution)/shard_map/pallas_call | solution.py:647
  276.7 15.3 %gather_fusion.2 = bf16[1280,2048]{1,0:T(8,128)(2,1)} fusion(bf16[2048,2048]{1,0:T(8,128)(2,1)} %bitcast.196, s32[2048]{0:T(1024)S(1)} %pad_clamp_fusion), kind=kCustom, calls=%fused_computation.clone | custom fusion | bytes 10490880 | tf_op jit(solution)/shard_map/jit(_take)/gather | solution.py:983
  292.0 15.3 %gather_fusion.3 = bf16[1280,2048]{1,0:T(8,128)(2,1)} fusion(bf16[2048,2048]{1,0:T(8,128)(2,1)} %bitcast.195, s32[2048]{0:T(1024)S(1)} %pad_clamp_fusion), kind=kCustom, calls=%fused_computation.2.clone | custom fusion | bytes 10490880 | tf_op jit(solution)/shard_map/jit(_take)/gather | solution.py:985
  307.3 6.9 select_select_fusion
  320.4 4.6 fusion.6
  329.1 4.5 fusion.16
  340.6 33.6 %shard_map.298 = f32[160,2048]{1,0:T(8,128)} custom-call(bf16[8,160,2048]{2,1,0:T(8,128)(2,1)} %bitcast.198), custom_call_target="tpu_custom_call" | custom-call | tf_op jit(solution)/shard_map/pallas_call | solution.py:555
  377.7 28.3 %shard_map.299 = bf16[8,160,2048]{2,1,0:T(8,128)(2,1)} custom-call(bf16[160,2048]{1,0:T(8,128)(2,1)} %add_convert_fusion.own), custom_call_target="tpu_custom_call" | custom-call | tf_op jit(solution)/shard_map/pallas_call | solution.py:521
  406.0 8.9 fusion.86
  415.0 9.1 convert_reduce_fusion.1
  424.1 7.4 convolution_convert_fusion.4
  431.6 7.6 convolution_convert_fusion
  439.2 7.9 convolution_convert_fusion.1
  447.1 7.9 convolution_convert_fusion.3
  455.1 53.1 %shard_map.300 = (f32[160,2048]{1,0:T(8,128)}, f32[160,2048]{1,0:T(8,128)}) custom-call(bf16[8,160,2048]{2,1,0:T(8,128)(2,1)} %bitcast.213, bf16[8,160,2048]{2,1,0:T(8,128)(2,1)} %bitcast.212), custom_call_target="tpu_custom_call" | custom-call | tf_op jit(solution)/shard_map/pallas_call | solution.py:555
  513.2 28.5 %shard_map.301 = bf16[8,160,2048]{2,1,0:T(8,128)(2,1)} custom-call(bf16[160,2048]{1,0:T(8,128)(2,1)} %get-tuple-element.144.own), custom_call_target="tpu_custom_call" | custom-call | tf_op jit(solution)/shard_map/pallas_call | solution.py:521
  541.7 5.0 convolution_convert_fusion.8
  557.7 5.5 fusion.37
  573.8 8.9 fusion.73
  583.5 286.2 %shard_map.302 = (bf16[2,4,256,1024]{3,2,1,0:T(8,128)(2,1)}, bf16[4,256,2048]{2,1,0:T(8,128)(2,1)}, bf16[2,4,256,512]{3,2,1,0:T(8,128)(2,1)}, bf16[4,16,256]{2,1...) custom-call(bf16[4,2,256,1024]{3,2,1,0:T(8,128)(2,1)} %bitcast.218, bf16[4,256,2048]{2,1,0:T(8,128)(2,1)} %bitcast.219, ...), custom_call_target="tpu_custom_call" | custom-call | tf_op jit(solution)/shard_map/pallas_call | solution.py:776
  902.4 4.5 maximum_convert_fusion
  907.4 4.7 bitcast_convert_fusion
  928.0 9.9 %copy.116 = f32[256,4,2,4,256]{0,4,3,2,1:T(8,128)} copy(f32[256,4,2,4,256]{4,0,3,2,1:T(8,128)} %maximum_convert_fusion) | data formatting | bytes 16777216 | tf_op jit(solution)/shard_map/convert_element_type | solution.py:29
  937.9 8.9 copy.118
  (290 shorter events, 121.7 us)
Async XLA Ops:
  0.6 16.0 %copy-start = (f32[256,2048]{1,0:T(8,128)S(1)}, f32[256,2048]{1,0:T(8,128)}, u32[]{:S(2)}) copy-start(f32[256,2048]{1,0:T(8,128)} %param.32) | copy-start | bytes 6291460
  275.1 16.9 %copy-start.25 = (f32[8,2832]{1,0:T(8,128)}, f32[8,2832]{1,0:T(8,128)S(1)}, u32[]{:S(2)}) copy-start(f32[8,2832]{1,0:T(8,128)S(1)} %slice_convert_fusion) | copy-start | bytes 271876
  307.3 6.9 copy-start.3
  320.4 7.0 copy-start.23
  335.0 5.6 copy-start.15
  377.7 37.3 %slice-start = ((s8[5242880]{0:T(1024)(128)(4,1)}), s8[4194304]{0:T(1024)(128)(4,1)S(1)}, s32[]{:S(2)}) async-start(s8[5242880]{0:T(1024)(128)(4,1)} %bitcast.203), calls=%async_computation.2 | async-start | bytes 8388608
  405.9 9.0 copy-start.30
  406.0 9.0 copy-start.31
  406.0 9.0 copy-start.32
  406.0 9.0 copy-start.33
  406.0 9.0 slice-start.1
  406.0 9.0 copy-start.38
  406.0 18.1 %slice-start.4 = ((s8[5242880]{0:T(1024)(128)(4,1)}), s8[4194304]{0:T(1024)(128)(4,1)S(1)}, s32[]{:S(2)}) async-start(s8[5242880]{0:T(1024)(128)(4,1)} %bitcast.209), calls=%async_computation.6 | async-start | bytes 8388608
  415.0 9.1 slice-start.5
  424.1 7.4 copy-start.39
  455.1 53.2 %copy-start.36 = (pred[160]{0:T(512)(128)(4,1)S(1)}, pred[160]{0:T(512)(128)(4,1)}, u32[]{:S(2)}) copy-start(pred[160]{0:T(512)(128)(4,1)} %dynamic_slice.118) | copy-start | bytes 484
  513.1 28.5 %copy-start.19 = (bf16[4,1,64,2048]{3,2,1,0:T(8,128)(2,1)S(1)}, bf16[4,1,64,2048]{3,2,1,0:T(8,128)(2,1)}, u32[]{:S(2)}) copy-start(bf16[4,1,64,2048]{3,2,1,0:T(8,128)(2,1)} %get-tuple-element.39) | copy-start | bytes 3145732
  557.6 5.6 copy-start.29
  557.6 6.6 copy-start.40
  877.0 5.8 copy-start.37
  877.0 6.4 copy-start.28
  878.7 6.8 copy-start.12
  878.7 33.4 %all-to-all-start.1 = ((bf16[4,64,2048]{2,1,0:T(8,128)(2,1)}), bf16[4,64,2048]{2,1,0:T(8,128)(2,1)S(1)}, u32[]{:S(2)}, u32[]{:S(2)}) async-start(bf16[4,64,2048]{2,1,0:T(8,128)(2,1)} %get-tuple-element.206), calls=%async_computation.1 | async-start | bytes 2097152 | tf_op jit(solution)/shard_map/all_to_all | solution.py:1161
  912.1 39.1 %all-to-all-start = ((bf16[4,64,2048]{2,1,0:T(8,128)(2,1)}), bf16[4,64,2048]{2,1,0:T(8,128)(2,1)}, u32[]{:S(2)}, u32[]{:S(2)}) async-start(bf16[4,64,2048]{2,1,0:T(8,128)(2,1)} %get-tuple-element.207), calls=%async_computation | async-start | bytes 2097152 | tf_op jit(solution)/shard_map/all_to_all | solution.py:1161
  (27 other events, 78.3 us)

commit v2 on v1

--- a/solution.py
+++ b/solution.py
@@ -85,6 +85,10 @@
         self.up = {"z": self.z + 1}
         self.down = {"z": self.z - 1}
 
+    def ring(self):
+        before = {"z": lax.rem(self.z + self.depth - 1, self.depth)}
+        return ({"z": lax.rem(self.z + 1, self.depth)}, before)
+
     def barrier(self, plane, line):
         bar = pltpu.get_barrier_semaphore()
         for to in plane:
@@ -153,13 +157,14 @@
 
 
 class PlaneGather:
-    def __init__(self, net, spot, own, slots):
+    def __init__(self, net, spot, own, slots, share=2):
         def at(y, x, c):
             return y * 4 + x * 2 + c
 
         y, x, c = spot.y, spot.x, spot.c
-        half = own.shape[0] // 2
-        lo, hi = pl.ds(0, half), pl.ds(half, half)
+        self.both = share == 2
+        half = own.shape[0] // share
+        lo, hi = pl.ds(0, half), pl.ds(half * (share - 1), half)
         me = at(y, x, c)
         on_x, on_y, on_d = at(y, 1 - x, c), at(1 - y, x, c), at(1 - y, 1 - x, c)
         peer = [at(y, x, 1 - c), at(y, 1 - x, 1 - c), at(1 - y, x, 1 - c), at(1 - y, 1 - x, 1 - c)]
@@ -174,17 +179,18 @@
         self.x_on_y = net.remote(
             slots.at[on_x, lo], slots.at[on_x, lo], spot.to_y, slots.at[on_d, lo]
         )
-        self.y_on_x = net.remote(
-            slots.at[on_y, hi], slots.at[on_y, hi], spot.to_x, slots.at[on_d, hi]
-        )
         self.x_on_c = net.remote(slot(on_x), slot(on_x), spot.to_c, slot(peer[1]))
         self.y_on_c = net.remote(slot(on_y), slot(on_y), spot.to_c, slot(peer[2]))
         self.lo_on_c = net.remote(
             slots.at[on_d, lo], slots.at[on_d, lo], spot.to_c, slots.at[peer[3], lo]
         )
-        self.hi_on_c = net.remote(
-            slots.at[on_d, hi], slots.at[on_d, hi], spot.to_c, slots.at[peer[3], hi]
-        )
+        if self.both:
+            self.y_on_x = net.remote(
+                slots.at[on_y, hi], slots.at[on_y, hi], spot.to_x, slots.at[on_d, hi]
+            )
+            self.hi_on_c = net.remote(
+                slots.at[on_d, hi], slots.at[on_d, hi], spot.to_c, slots.at[peer[3], hi]
+            )
 
     def start(self):
         self.x.start()
@@ -197,29 +203,23 @@
         self.x_on_y.start()
         self.x_on_c.start()
         self.y.got()
-        self.y_on_x.start()
+        if self.both:
+            self.y_on_x.start()
         self.y_on_c.start()
 
     def last(self):
         self.x_on_y.got()
         self.lo_on_c.start()
-        self.y_on_x.got()
-        self.hi_on_c.start()
+        if self.both:
+            self.y_on_x.got()
+            self.hi_on_c.start()
 
     def finish(self):
-        for copy in (self.c, self.x_on_c, self.y_on_c, self.lo_on_c, self.hi_on_c):
+        second = (self.y_on_x, self.hi_on_c) if self.both else ()
+        for copy in (self.c, self.x_on_c, self.y_on_c, self.lo_on_c, *second[1:]):
             copy.got()
-        for copy in (
-            self.x,
-            self.y,
-            self.c,
-            self.x_on_y,
-            self.y_on_x,
-            self.x_on_c,
-            self.y_on_c,
-            self.lo_on_c,
-            self.hi_on_c,
-        ):
+        firsts = (self.x, self.y, self.c, self.x_on_y, self.x_on_c, self.y_on_c, self.lo_on_c)
+        for copy in (*firsts, *second):
             copy.sent()
         self.keep.wait()
 
@@ -259,10 +259,13 @@
             (1 - y) * 2 + 1 - x,
         )
         self.parts, self.sums, self.diag = parts, sums, diag
+        self.stacked = parts.shape[0] == 4
         self.from_x, self.from_y, self.c = from_x, from_y, c
         self.lo, self.hi = lo, hi
         self.first = {
-            key: net.remote(parts.at[at * 2 + 1 - c], sums.at[at], spot.to_c)
+            key: net.remote(
+                parts.at[at] if self.stacked else parts.at[at * 2 + 1 - c], sums.at[at], spot.to_c
+            )
             for key, at in (("d", self.nd), ("x", self.nx), ("y", self.ny), ("o", self.own))
         }
         self.d_lo = net.remote(sums.at[self.nd, lo], diag.at[lo], spot.to_x)
@@ -278,7 +281,10 @@
 
     def pair(self, key, at):
         self.first[key].got()
-        add_rows(self.sums.at[at], self.parts.at[at * 2 + self.c])
+        if self.stacked:
+            self.compute(at * 2 + self.c, at)
+        else:
+            add_rows(self.sums.at[at], self.parts.at[at * 2 + self.c])
 
     def middle(self):
         self.pair("d", self.nd)
@@ -499,176 +505,450 @@
 IN_VMEM = pl.BlockSpec(memory_space=pltpu.VMEM)
 
 
+def lasts(micros, moved):
+    return pl.CostEstimate(
+        flops=int(micros * 1e9), bytes_accessed=int(moved), transcendentals=0
+    )
+
+
 def comm_params(collective_id):
     return pltpu.CompilerParams(
         collective_id=collective_id, has_side_effects=True, vmem_limit_bytes=VMEM_LIMIT
     )
 
 
-def plane_gather(block, depth, collective_id):
-    rows, width = block.shape
-
-    def kernel(own, slots, *sems):
-        spot = Spot(depth)
-        net = Net(*sems)
-        gather = PlaneGather(net, spot, own, slots)
-        spot.barrier((spot.to_c, spot.to_x, spot.to_y), False)
-        gather.start()
-        gather.middle()
-        gather.last()
-        gather.finish()
-
-    out = pl.pallas_call(
-        kernel,
-        out_shape=jax.ShapeDtypeStruct((8, rows, width), block.dtype),
-        in_specs=[ANY],
-        out_specs=ANY,
-        scratch_shapes=net_scratch(PlaneGather.remotes, 1),
-        compiler_params=comm_params(collective_id),
-    )(block)
-    return out.reshape(8 * rows, width)
-
-
-def plane_scatter(parts, depth, collective_id):
-    count = len(parts)
-    rows, width = parts[0].shape[0] // 8, parts[0].shape[1]
-
-    def kernel(*refs):
-        sources, results = refs[:count], refs[count : 2 * count]
-        scratch = refs[2 * count : -3]
-        spot = Spot(depth)
-        net = Net(*refs[-3:])
-        runs = [
-            PlaneScatter(net, spot, source, *scratch[4 * index : 4 * index + 4])
-            for index, source in enumerate(sources)
-        ]
-        spot.barrier((spot.to_c, spot.to_x, spot.to_y), False)
-        for run in runs:
-            run.start()
-        for run in runs:
-            run.middle()
-        for run in runs:
-            run.last()
-        for run, result in zip(runs, results):
-            run.finish(result)
-
-    return pl.pallas_call(
-        kernel,
-        out_shape=[jax.ShapeDtypeStruct((rows, width), jnp.float32)] * count,
-        in_specs=[IN_VMEM] * count,
-        out_specs=[IN_VMEM] * count,
-        scratch_shapes=PlaneScatter.buffers(rows, width) * count
-        + net_scratch(PlaneScatter.remotes * count, 1),
-        compiler_params=comm_params(collective_id),
-    )(*[item.reshape(8, rows, width) for item in parts])
-
-
-def first_gather(
-    depth, tokens, cotangent, attn_mine, attn_other, small, out_slice, up_mine, up_other, down_slice
-):
-    flat, width = tokens.shape
-    low_type = jnp.bfloat16
-
-    def shape(*dims):
-        return jax.ShapeDtypeStruct(dims, low_type)
+def low_shape(*dims):
+    return jax.ShapeDtypeStruct(dims, jnp.bfloat16)
+
+
+def wide_shape(*dims):
+    return jax.ShapeDtypeStruct(dims, jnp.float32)
+
+
+def low_vmem(*dims):
+    return pltpu.VMEM(dims, jnp.bfloat16)
+
+
+def pick_rows(chooser, source, result, step=512):
+    width = result.shape[-1]
+
+    @pl.loop(0, width // step)
+    def _(index):
+        at = pl.ds(pl.multiple_of(index * step, step), step)
+        rows = source[..., at].reshape(chooser.shape[1], step)
+        result[..., at] = low(product(chooser[...], rows)).reshape(*result.shape[:-1], step)
+
+
+def opening(depth, owner, tok_send, cot_send, chooser, query_weight, keyval_weight, output_weight, down_weight, small, up_mine, up_other):
+    rows = chooser.shape[0]
+    width = tok_send.shape[-1]
+    group = depth // 4
+    rows_own = query_weight.shape[0]
+    head_cols = width // 8
+    kv_rows = rows_own // 4
+    kv_cols = keyval_weight.shape[1]
+    seg = down_weight.shape[0] // 4
 
     def kernel(
-        tok, cot, attn_m, attn_o, small_m, out_m, up_m, up_o, down_m,
-        tok_all, cot_all, attn_all, small_all, out_all, out_dealt, up_all, down_all,
-        *sems,
+        tok, cot, choose, query_w, kv_w, out_w, down_w, small_m, up_m, up_o,
+        own_tok, own_cot, up_own, down_2,
+        tok_all, cot_all, query_all, kv_all, small_all, out_dealt, up_all, down_all,
+        tok_got, cot_got, out_all, kv_line, query_m, query_o, query_y, small_y, down_m, down_1,
+        query_f, out_f, kv_f, down_f, *sems,
     ):
         spot = Spot(depth)
         net = Net(*sems)
         z, y = spot.z, spot.y
-        tok_run = PlaneGather(net, spot, tok, tok_all)
-        cot_run = PlaneGather(net, spot, cot, cot_all)
-        group = depth // 4
-        keep_out = net.local(out_m, out_all.at[z // group, z % group])
-        keep_attn = net.local(attn_m, attn_all.at[z, y])
+        xc = spot.x * 2 + spot.c
+        after, _ = spot.ring()
+        before = lax.rem(z + depth - 1, depth)
+        before_2 = lax.rem(z + 2 * depth - 2, depth)
+
+        def head_base(y_at):
+            return pl.multiple_of(owner(xc * group, y_at) * rows_own, 128)
+
+        def strip(ref, size):
+            return ref.at[pl.ds(pl.multiple_of(xc * size, size), size)]
+
+        def z_slot(at):
+            return kv_line.at[pl.ds(pl.multiple_of(at * kv_rows, kv_rows), kv_rows)]
+
+        reads = [
+            net.local(query_w.at[:, pl.ds(head_base(1 - y), head_cols)], query_f.at[0]),
+            net.local(strip(down_w, seg), down_f),
+            net.local(strip(out_w, kv_rows), out_f),
+            net.local(strip(kv_w, kv_rows), kv_f),
+            net.local(query_w.at[:, pl.ds(head_base(y), head_cols)], query_f.at[1]),
+        ]
+        tok_deal = DpExchange(net, spot, tok, tok_got)
+        cot_deal = DpExchange(net, spot, cot, cot_got)
+        tok_run = PlaneGather(net, spot, own_tok, tok_all)
+        cot_run = PlaneGather(net, spot, own_cot, cot_all, share=1)
+        kv_run = PlaneGather(net, spot, kv_line, kv_all)
+        y_query = net.remote(query_o, query_y, spot.to_y)
+        y_small = net.remote(small_m, small_y, spot.to_y)
+        y_up = net.remote(up_o, up_own.at[y], spot.to_y, up_own.at[1 - y])
+        d_hops = [net.remote(down_m, down_1, after), net.remote(down_1, down_2, after)]
         keep_small = net.local(small_m, small_all.at[z, y])
-        keep_up = net.local(up_m, up_all.at[z, y])
-        keep_down = net.local(down_m, down_all.at[z])
-        y_attn = net.remote(attn_o, attn_all.at[z, y], spot.to_y, attn_all.at[z, 1 - y])
-        y_small = net.remote(small_m, small_all.at[z, y], spot.to_y, small_all.at[z, 1 - y])
-        y_up = net.remote(up_o, up_all.at[z, y], spot.to_y, up_all.at[z, 1 - y])
+        keep_up_mine = net.local(up_m, up_all.at[z, y])
+        keep_query = net.local(query_m, query_all.at[z, y])
+        keep_query_y = net.local(query_y, query_all.at[z, 1 - y])
+        keep_small_y = net.local(small_y, small_all.at[z, 1 - y])
+        keep_up_y = net.local(up_own.at[1 - y], up_all.at[z, 1 - y])
+        keep_down = [
+            net.local(down_m, down_all.at[z]),
+            net.local(down_1, down_all.at[before]),
+            net.local(down_2, down_all.at[before_2]),
+        ]
         run_out = LineGather(net, spot, lambda at: out_all.at[at // group, at % group])
-        run_attn = LineGather(net, spot, lambda at: attn_all.at[at])
+        run_kv = LineGather(net, spot, z_slot)
+        run_query = LineGather(net, spot, lambda at: query_all.at[at])
         run_small = LineGather(net, spot, lambda at: small_all.at[at])
-        run_up = LineGather(net, spot, lambda at: up_all.at[at])
-        run_down = LineGather(net, spot, lambda at: down_all.at[at])
-        deal = DpExchange(net, spot, out_all, out_dealt)
-        spot.barrier((spot.to_c, spot.to_x, spot.to_y, spot.to_xc), True)
-        keep_out.start()
-        y_attn.start()
+        out_deal = DpExchange(net, spot, out_all, out_dealt)
+        for copy in reads:
+            copy.start()
+        keep_small.start()
+        keep_up_mine.start()
+        spot.barrier((spot.to_c, spot.to_x, spot.to_y, spot.to_xc, *spot.ring()), False)
+        tok_deal.start()
+        reads[0].wait()
+        query_o[...] = low(query_f[0])
+        y_query.start()
         y_small.start()
-        keep_attn.start()
-        keep_small.start()
+        reads[2].wait()
+        out_all[z // group, z % group] = low(out_f[...])
+        run_out.start(0)
+        reads[3].wait()
+        z_slot(z)[...] = low(kv_f[...])
+        run_kv.start(0)
+        reads[4].wait()
+        query_m[...] = low(query_f[1])
+        keep_query.start()
+        reads[1].wait()
+
+        @pl.loop(0, seg // 16)
+        def _(index):
+            at = pl.ds(pl.multiple_of(index * 16, 16), 16)
+            down_m[at, :] = low(down_f[at, :])
+
+        keep_query.wait()
+        keep_small.wait()
+        y_query.got()
+        keep_query_y.start()
+        y_small.got()
+        keep_small_y.start()
+        keep_query_y.wait()
+        keep_small_y.wait()
+        run_query.start(0)
+        run_small.start(0)
         y_up.start()
-        keep_down.start()
-        keep_up.start()
+        d_hops[0].start()
+        keep_down[0].start()
+
+        @pl.loop(0, rows_own // 16)
+        def _(index):
+            at = pl.ds(pl.multiple_of(index * 16, 16), 16)
+            up_own[y, at, :] = up_m[at, :]
+
+        tok_deal.got()
+        pick_rows(choose, tok_got, own_tok)
         tok_run.start()
-        keep_out.wait()
-        run_out.start(0)
-        keep_attn.wait()
-        y_attn.got()
-        run_attn.start(0)
-        keep_small.wait()
-        y_small.got()
-        run_small.start(0)
-        keep_down.wait()
-        run_down.start(0)
-        keep_up.wait()
+        cot_deal.start()
+        run_out.hop(1)
+        run_kv.hop(1)
+        run_query.hop(1)
+        run_small.hop(1)
         y_up.got()
-        run_up.start(0)
+        keep_up_y.start()
+        cot_deal.got()
+        pick_rows(choose, cot_got, own_cot)
         tok_run.middle()
-        for step in range(1, depth - 1):
+        cot_run.start()
+        d_hops[0].got()
+        d_hops[1].start()
+        keep_down[1].start()
+        for step in range(2, depth - 1):
             run_out.hop(step)
-            run_attn.hop(step)
+            run_kv.hop(step)
+            run_query.hop(step)
             run_small.hop(step)
         tok_run.last()
-        cot_run.start()
-        for run in (run_out, run_attn, run_small):
-            run.got(depth - 2)
-        deal.start()
+        run_out.got(depth - 2)
+        run_kv.got(depth - 2)
+        kv_run.start()
+        out_deal.start()
+        run_query.got(depth - 2)
+        run_small.got(depth - 2)
+        kv_run.middle()
         cot_run.middle()
+        kv_run.last()
         cot_run.last()
-        for step in range(1, depth - 1):
-            run_down.hop(step)
-            run_up.hop(step)
-        deal.got()
-        run_down.got(depth - 2)
-        run_up.got(depth - 2)
-        for run in (run_out, run_attn, run_small, run_up, run_down, tok_run, cot_run, deal):
+        d_hops[1].got()
+        keep_down[2].start()
+        out_deal.got()
+        runs = (run_out, run_kv, run_query, run_small, tok_run, kv_run, cot_run)
+        for run in (*runs, tok_deal, cot_deal, out_deal):
             run.finish()
-        for copy in (y_attn, y_small, y_up):
+        for copy in (y_query, y_small, y_up, *d_hops):
             copy.sent()
-
-    remotes = 2 * PlaneGather.remotes + 3 + 5 * LineGather.remotes(depth) + DpExchange.remotes
+        for copy in (keep_up_mine, keep_up_y, *keep_down):
+            copy.wait()
+
+    remotes = (
+        3 * DpExchange.remotes + 3 * PlaneGather.remotes + 5 + 4 * LineGather.remotes(depth)
+    )
+    operands = (
+        tok_send, cot_send, chooser, query_weight, keyval_weight, output_weight, down_weight, small,
+        up_mine, up_other,
+    )
+    wide_type = jnp.float32
     return pl.pallas_call(
         kernel,
         out_shape=[
-            shape(8, flat, width),
-            shape(8, flat, width),
-            shape(depth, 2, *attn_mine.shape),
-            shape(depth, 2, *small.shape),
-            shape(4, depth // 4, *out_slice.shape),
-            shape(4, depth // 4, *out_slice.shape),
-            shape(depth, 2, *up_mine.shape),
-            shape(depth, *down_slice.shape),
+            low_shape(rows, width),
+            low_shape(rows, width),
+            low_shape(2, *up_mine.shape),
+            low_shape(seg, width),
+            low_shape(8, rows, width),
+            low_shape(8, rows, width),
+            low_shape(depth, 2, rows_own, head_cols),
+            low_shape(8, depth * kv_rows, kv_cols),
+            low_shape(depth, 2, *small.shape),
+            low_shape(4, group, kv_rows, width),
+            low_shape(depth, 2, *up_mine.shape),
+            low_shape(depth, seg, width),
         ],
-        in_specs=[ANY] * 9,
-        out_specs=[ANY] * 8,
-        scratch_shapes=net_scratch(remotes, 8),
+        in_specs=[IN_VMEM] * 3 + [ANY] * 4 + [IN_VMEM] * 3,
+        out_specs=[IN_VMEM] * 4 + [ANY] * 8,
+        scratch_shapes=[
+            low_vmem(*tok_send.shape),
+            low_vmem(*tok_send.shape),
+            low_vmem(4, group, kv_rows, width),
+            low_vmem(depth * kv_rows, kv_cols),
+            low_vmem(rows_own, head_cols),
+            low_vmem(rows_own, head_cols),
+            low_vmem(rows_own, head_cols),
+            low_vmem(*small.shape),
+            low_vmem(seg, width),
+            low_vmem(seg, width),
+            pltpu.VMEM((2, rows_own, head_cols), wide_type),
+            pltpu.VMEM((kv_rows, width), wide_type),
+            pltpu.VMEM((kv_rows, kv_cols), wide_type),
+            pltpu.VMEM((seg, width), wide_type),
+            *net_scratch(remotes, 24),
+        ],
         compiler_params=comm_params(1),
-    )(tokens, cotangent, attn_mine, attn_other, small, out_slice, up_mine, up_other, down_slice)
-
-
-def last_scatter(depth, d_up, d_down, d_attn, d_vec, d_out, grad_parts):
+        cost_estimate=lasts(85, 1 << 20),
+    )(*operands)
+
+
+ROWS_STEP = 32
+
+
+def row_loop(count):
+    def decorate(body):
+        @pl.loop(0, count // ROWS_STEP)
+        def _(index):
+            body(pl.ds(pl.multiple_of(index * ROWS_STEP, ROWS_STEP), ROWS_STEP))
+
+    return decorate
+
+
+def feed_blocks(run, c, parts, block):
+    width = parts.shape[-1]
+
+    def columns(body):
+        @pl.loop(0, width // 512)
+        def _(index):
+            body(pl.ds(pl.multiple_of(index * 512, 512), 512))
+
+    def send(at, member):
+        @columns
+        def _(cols):
+            parts[at, :, cols] = low(block(member, cols))
+
+    def merge(member, at):
+        @columns
+        def _(cols):
+            run.sums[at, :, cols] = low(wide(run.sums[at, :, cols]) + block(member, cols))
+
+    run.compute = merge
+    for key, at in (("d", run.nd), ("x", run.nx), ("y", run.ny), ("o", run.own)):
+        send(at, at * 2 + 1 - c)
+        run.first[key].start()
+
+
+def attention_out(depth, attended, w_output, own_tok, bias, gain, shift, up_piece):
+    rows, width = own_tok.shape
+
+    def kernel(att, w_out, tok, bias_row, gain_row, shift_row, piece, middle, normed_all, hop_1, hop_2,
+               parts, normed, sums, diag, from_x, from_y, *sems):
+        spot = Spot(depth)
+        net = Net(*sems)
+        run = PlaneScatter(net, spot, parts, sums, diag, from_x, from_y)
+        gather = PlaneGather(net, spot, normed, normed_all)
+        after, _ = spot.ring()
+        ups = [net.remote(piece, hop_1, after), net.remote(hop_1, hop_2, after)]
+
+        def block(member, cols):
+            rows_at = pl.ds(pl.multiple_of(member * rows, rows), rows)
+            return product(att[rows_at, :], w_out[:, cols])
+
+        spot.barrier((spot.to_c, spot.to_x, spot.to_y, *spot.ring()), False)
+        ups[0].start()
+        feed_blocks(run, spot.c, parts, block)
+        run.middle()
+        run.last()
+        run.finish(middle)
+
+        @row_loop(rows)
+        def _(at):
+            total = wide(tok[at, :]) + (middle[at, :] + bias_row[...])
+            middle[at, :] = total
+            xhat, _ = normalize(total)
+            normed[at, :] = low(xhat * gain_row[...] + shift_row[...])
+
+        gather.start()
+        ups[0].got()
+        ups[1].start()
+        gather.middle()
+        gather.last()
+        gather.finish()
+        ups[1].got()
+        for copy in ups:
+            copy.sent()
+
+    return pl.pallas_call(
+        kernel,
+        out_shape=[
+            wide_shape(rows, width),
+            low_shape(8, rows, width),
+            low_shape(*up_piece.shape),
+            low_shape(*up_piece.shape),
+        ],
+        in_specs=[IN_VMEM] * 6 + [ANY],
+        out_specs=[IN_VMEM, ANY, ANY, ANY],
+        scratch_shapes=[
+            low_vmem(4, rows, width),
+            low_vmem(rows, width),
+            *PlaneScatter.buffers(rows, width),
+            *net_scratch(PlaneScatter.remotes + PlaneGather.remotes + 2, 1),
+        ],
+        compiler_params=comm_params(3),
+        cost_estimate=lasts(60, 1 << 20),
+    )(attended, w_output, own_tok, bias, gain, shift, up_piece)
+
+
+def mlp_back(depth, grad_hidden, w_up, activated, w_down, middle, own_cot, gain, bias, d_down, d_up):
+    rows, width = own_cot.shape
+
+    def kernel(gh, up, act, down, mid, cot, gain_row, bias_row, dd, du,
+               grad_normed, grad_middle, branch_all, block_out, dd_sum, du_sum,
+               parts, branch, sums, diag, from_x, from_y,
+               parts2, sums2, diag2, from_x2, from_y2, mlp_sum, dd_got, *sems):
+        spot = Spot(depth)
+        net = Net(*sems)
+        z = spot.z
+        run = PlaneScatter(net, spot, parts, sums, diag, from_x, from_y)
+        run2 = PlaneScatter(net, spot, parts2, sums2, diag2, from_x2, from_y2)
+        gather = PlaneGather(net, spot, branch, branch_all)
+        after, _ = spot.ring()
+
+        def slot(step):
+            return lax.rem(z + 2 * depth - 1 - step, depth)
+
+        def landing(step):
+            return dd_sum if step == depth - 1 else dd_got.at[step - 1]
+
+        du_hop = net.remote(du.at[slot(0)], du_sum, after)
+        dd_hops = [net.remote(dd.at[slot(0)], landing(1), after)]
+        for step in range(1, depth - 1):
+            dd_hops.append(net.remote(landing(step), landing(step + 1), after))
+
+        def ring_step(step):
+            dd_hops[step - 1].got()
+            add_rows(landing(step), dd.at[slot(step)], 32)
+            if step < depth - 1:
+                dd_hops[step].start()
+
+        def block(member, cols):
+            rows_at = pl.ds(pl.multiple_of(member * rows, rows), rows)
+            return product_cols(gh[rows_at, :], up[cols, :])
+
+        def block2(member, cols):
+            rows_at = pl.ds(pl.multiple_of(member * rows, rows), rows)
+            return product(act[rows_at, :], down[:, cols])
+
+        spot.barrier((spot.to_c, spot.to_x, spot.to_y, *spot.ring()), False)
+        dd_hops[0].start()
+        feed_blocks(run, spot.c, parts, block)
+        run.middle()
+        feed_blocks(run2, spot.c, parts2, block2)
+        run.last()
+        ring_step(1)
+        run.finish(grad_normed)
+
+        @row_loop(rows)
+        def _(at):
+            xhat, scale = normalize(mid[at, :])
+            grad = wide(cot[at, :]) + norm_back(grad_normed[at, :], gain_row[...], xhat, scale)
+            grad_middle[at, :] = grad
+            branch[at, :] = low(grad)
+
+        gather.start()
+        for step in range(2, depth - 1):
+            ring_step(step)
+        gather.middle()
+        run2.middle()
+        gather.last()
+        ring_step(depth - 1)
+        du_hop.start()
+        run2.last()
+        gather.finish()
+        run2.finish(mlp_sum)
+
+        @row_loop(rows)
+        def _(at):
+            block_out[at, :] = low(mid[at, :] + (mlp_sum[at, :] + bias_row[...]))
+
+        du_hop.got()
+        for at in range(2):
+            add_rows(du_sum.at[at], du.at[slot(1), at], 32)
+        for copy in (*dd_hops, du_hop):
+            copy.sent()
+
+    return pl.pallas_call(
+        kernel,
+        out_shape=[
+            wide_shape(rows, width),
+            wide_shape(rows, width),
+            low_shape(8, rows, width),
+            low_shape(rows, width),
+            low_shape(*d_down.shape[1:]),
+            low_shape(*d_up.shape[1:]),
+        ],
+        in_specs=[IN_VMEM] * 10,
+        out_specs=[IN_VMEM, IN_VMEM, ANY, IN_VMEM, IN_VMEM, IN_VMEM],
+        scratch_shapes=[
+            low_vmem(4, rows, width),
+            low_vmem(rows, width),
+            *PlaneScatter.buffers(rows, width),
+            low_vmem(4, rows, width),
+            *PlaneScatter.buffers(rows, width),
+            pltpu.VMEM((rows, width), jnp.float32),
+            low_vmem(depth - 2, *d_down.shape[1:]),
+            *net_scratch(2 * PlaneScatter.remotes + PlaneGather.remotes + depth, 1),
+        ],
+        compiler_params=comm_params(5),
+        cost_estimate=lasts(95, 1 << 20),
+    )(grad_hidden, w_up, activated, w_down, middle, own_cot, gain, bias, d_down, d_up)
+
+
+def closing(depth, up_own, down_own, down_x, d_query, d_keyval, d_vec, d_out, grad_parts, own_tok, grad_middle, gain, block, chooser):
     rows, width = grad_parts.shape[1:]
-    low_type = jnp.bfloat16
-
-    def shape(*dims):
-        return jax.ShapeDtypeStruct(dims, low_type)
+    kv_rows, kv_cols = d_keyval.shape[1] // depth, d_keyval.shape[2]
+    group = depth // 4
+    slots = chooser.shape[0] // 4
 
     def add2(into, other):
         add_rows(into, other, 16)
@@ -678,128 +958,209 @@
             add_rows(into.at[at], other.at[at], 16)
 
     def kernel(
-        up, down, attn, vec, out, parts,
-        up_all, down_all, attn_all, vec_all, out_all, own_sum,
-        up_lo, up_hi, down_lo, down_hi, attn_lo, attn_hi, vec_lo, vec_hi, out_lo, out_hi,
-        out_mix, up_got, attn_got, vec_got, sums, diag, from_x, from_y, *sems,
+        up, down, down_x_in, query, kv, vec, out, parts, tok, grad_mid, gain_row, block_own, choose,
+        up_all, down_all, query_all, kv_all, vec_all, out_all, block_got, grad_got,
+        query_lo, query_hi, kv_lo, kv_hi, vec_lo, vec_hi, out_lo, out_hi,
+        out_mix, up_got, query_got, vec_got, first, grad_low, block_send, grad_send, kv_line, kv_wide,
+        sums, diag, from_x, from_y, kv_sums, kv_diag, kv_from_x, kv_from_y, *sems,
     ):
         spot = Spot(depth)
         net = Net(*sems)
         z, y = spot.z, spot.y
         deal = DpExchange(net, spot, out, out_mix)
-        group = depth // 4
 
         def mixed(at):
             return out_mix.at[at // group, at % group]
 
-        run_up = LineScatter(net, spot, lambda at: up.at[at], up_lo, up_hi, add3)
-        run_down = LineScatter(net, spot, lambda at: down.at[at], down_lo, down_hi, add2)
-        run_attn = LineScatter(net, spot, lambda at: attn.at[at], attn_lo, attn_hi, add3)
+        def kv_part(at):
+            return kv_line.at[pl.ds(pl.multiple_of(at * kv_rows, kv_rows), kv_rows)]
+
+        run_query = LineScatter(net, spot, lambda at: query.at[at], query_lo, query_hi, add3)
+        run_kv = LineScatter(net, spot, kv_part, kv_lo, kv_hi, add2)
         run_vec = LineScatter(net, spot, lambda at: vec.at[at], vec_lo, vec_hi, add3)
         run_out = LineScatter(net, spot, mixed, out_lo, out_hi, add2)
         plane = PlaneScatter(net, spot, parts, sums, diag, from_x, from_y)
-        y_up = net.remote(up.at[z, 1 - y], up_got, spot.to_y)
-        y_attn = net.remote(attn.at[z, 1 - y], attn_got, spot.to_y)
+        kv_plane = PlaneScatter(net, spot, kv, kv_sums, kv_diag, kv_from_x, kv_from_y)
+        y_up = net.remote(up.at[1 - y], up_got, spot.to_y)
+        y_query = net.remote(query.at[z, 1 - y], query_got, spot.to_y)
         y_vec = net.remote(vec.at[z, 1 - y], vec_got, spot.to_y)
-        dp_up = DpGather(net, spot, up.at[z, y], up_all.at[0])
-        dp_up2 = DpGather(net, spot, up_got, up_all.at[1])
-        dp_down = DpGather(net, spot, down.at[z], down_all)
-        dp_attn = DpGather(net, spot, attn.at[z, y], attn_all.at[0])
-        dp_attn2 = DpGather(net, spot, attn_got, attn_all.at[1])
+        dp_up = DpGather(net, spot, up.at[y], up_all.at[y])
+        dp_up2 = DpGather(net, spot, up_got, up_all.at[1 - y])
+        xc, on_x = spot.x * 2 + spot.c, (1 - spot.x) * 2 + spot.c
+        keep_down = [
+            net.local(down, down_all.at[xc]),
+            net.local(down_x_in, down_all.at[on_x]),
+        ]
+        down_moves = [
+            net.remote(down, down_all.at[xc], spot.to_c, down_all.at[spot.x * 2 + 1 - spot.c]),
+            net.remote(
+                down_x_in,
+                down_all.at[on_x],
+                spot.to_c,
+                down_all.at[(1 - spot.x) * 2 + 1 - spot.c],
+            ),
+        ]
+        dp_query = DpGather(net, spot, query.at[z, y], query_all.at[y])
+        dp_query2 = DpGather(net, spot, query_got, query_all.at[1 - y])
+        dp_kv = DpGather(net, spot, kv_part(z), kv_all)
         dp_vec = DpGather(net, spot, vec.at[z, y], vec_all)
         dp_out = DpGather(net, spot, mixed(z), out_all)
+        back_block = DpExchange(net, spot, block_send, block_got)
+        back_grad = DpExchange(net, spot, grad_send, grad_got)
         spot.barrier((spot.to_c, spot.to_x, spot.to_y, spot.to_xc), True)
+        plane.start()
+        kv_plane.start()
+        run_query.stage(0)
         deal.start()
-        run_down.stage(0)
-        run_up.stage(0)
-        plane.start()
+        y_up.start()
+        kv_plane.middle()
         plane.middle()
-        for step in range(1, depth - 1):
-            run_down.stage(step)
+        kv_plane.last()
+        deal.got()
+        run_out.stage(0)
+        run_query.stage(1)
+        kv_plane.finish(kv_wide)
+        kv_line[...] = low(kv_wide[...])
+        run_kv.stage(0)
+        run_vec.stage(0)
+        pick_rows(choose, block_own, block_send)
         plane.last()
-        for step in range(1, depth - 1):
-            run_up.stage(step)
-        run_down.total()
-        deal.got()
-        run_attn.stage(0)
-        run_vec.stage(0)
-        run_out.stage(0)
-        dp_down.start()
-        plane.finish(own_sum)
-        run_up.total()
-        y_up.start()
+        run_out.stage(1)
+        run_kv.stage(1)
+        run_vec.stage(1)
+        for copy in (*down_moves, *keep_down):
+            copy.start()
+        plane.finish(first)
+
+        @row_loop(rows)
+        def _(at):
+            xhat, scale = normalize(wide(tok[at, :]))
+            grad = grad_mid[at, :] + norm_back(first[at, :], gain_row[...], xhat, scale)
+            grad_low[at, :] = low(grad)
+
+        pick_rows(choose, grad_low, grad_send)
+        back_grad.start()
+        for step in range(2, depth - 1):
+            run_query.stage(step)
+            run_out.stage(step)
+            run_kv.stage(step)
+            run_vec.stage(step)
+        y_up.got()
         dp_up.start()
-        for step in range(1, depth - 1):
-            run_attn.stage(step)
-            run_vec.stage(step)
-            run_out.stage(step)
-        dp_down.last()
-        y_up.got()
         dp_up2.start()
-        dp_up.last()
-        run_attn.total()
-        run_vec.total()
-        y_attn.start()
-        y_vec.start()
-        dp_attn.start()
+        run_query.total()
+        y_query.start()
+        dp_query.start()
         run_out.total()
         dp_out.start()
+        run_kv.total()
+        dp_kv.start()
+        run_vec.total()
+        y_vec.start()
+        back_block.start()
+        dp_up.last()
         dp_up2.last()
+        y_query.got()
+        dp_query2.start()
         y_vec.got()
         y_vec.sent()
         add_rows(vec.at[z, y], vec_got, 16)
         dp_vec.start()
-        y_attn.got()
-        dp_attn2.start()
-        dps = (dp_attn, dp_out, dp_vec, dp_attn2)
+        dps = (dp_query, dp_out, dp_kv, dp_query2, dp_vec)
         for run in dps:
             run.last()
-        for run in (dp_down, dp_up, dp_up2, *dps):
+        back_grad.got()
+        back_block.got()
+        for run in (dp_up, dp_up2, *dps, back_grad, back_block):
             run.finish()
-        for run in (run_up, run_down, run_attn, run_vec, run_out, deal):
+        for copy in down_moves:
+            copy.got()
+            copy.sent()
+        for copy in keep_down:
+            copy.wait()
+        for run in (run_query, run_kv, run_vec, run_out, deal):
             run.finish()
-        y_up.sent()
-        y_attn.sent()
+        for copy in (y_up, y_query):
+            copy.sent()
 
     remotes = (
-        DpExchange.remotes
-        + 5 * LineGather.remotes(depth)
-        + PlaneScatter.remotes
+        3 * DpExchange.remotes
+        + 4 * LineGather.remotes(depth)
+        + 2 * PlaneScatter.remotes
         + 3
-        + 7 * DpGather.remotes
+        + 8 * DpGather.remotes
     )
     one = depth - 1
 
     def twice(*dims):
-        return [pltpu.VMEM(dims, low_type)] * 2
+        return [low_vmem(*dims)] * 2
 
     return pl.pallas_call(
         kernel,
         out_shape=[
-            shape(2, 4, *d_up.shape[2:]),
-            shape(4, *d_down.shape[1:]),
-            shape(2, 4, *d_attn.shape[2:]),
-            shape(4, *d_vec.shape[2:]),
-            shape(4, *d_out.shape[2:]),
-            jax.ShapeDtypeStruct((rows, width), jnp.float32),
+            low_shape(2, 4, *up_own.shape[1:]),
+            low_shape(4, *down_own.shape),
+            low_shape(2, 4, *d_query.shape[2:]),
+            low_shape(4, kv_rows, kv_cols),
+            low_shape(4, *d_vec.shape[2:]),
+            low_shape(4, *d_out.shape[2:]),
+            low_shape(4, slots, width),
+            low_shape(4, slots, width),
         ],
-        in_specs=[IN_VMEM] * 6,
-        out_specs=[ANY] * 5 + [IN_VMEM],
+        in_specs=[IN_VMEM] * 13,
+        out_specs=[ANY] * 8,
         scratch_shapes=[
-            *twice(one, *d_up.shape[1:]),
-            *twice(one, *d_down.shape[1:]),
-            *twice(one, *d_attn.shape[1:]),
+            *twice(one, *d_query.shape[1:]),
+            *twice(one, kv_rows, kv_cols),
             *twice(one, *d_vec.shape[1:]),
             *twice(one, *d_out.shape[2:]),
-            pltpu.VMEM(d_out.shape, low_type),
-            pltpu.VMEM(d_up.shape[2:], low_type),
-            pltpu.VMEM(d_attn.shape[2:], low_type),
-            pltpu.VMEM(d_vec.shape[2:], low_type),
+            low_vmem(*d_out.shape),
+            low_vmem(*up_own.shape[1:]),
+            low_vmem(*d_query.shape[2:]),
+            low_vmem(*d_vec.shape[2:]),
+            pltpu.VMEM((rows, width), jnp.float32),
+            low_vmem(rows, width),
+            low_vmem(4, slots, width),
+            low_vmem(4, slots, width),
+            low_vmem(depth * kv_rows, kv_cols),
+            pltpu.VMEM((depth * kv_rows, kv_cols), jnp.float32),
             *PlaneScatter.buffers(rows, width),
-            *net_scratch(remotes, 8),
+            *PlaneScatter.buffers(depth * kv_rows, kv_cols),
+            *net_scratch(remotes, 12),
         ],
         compiler_params=comm_params(2),
-    )(d_up, d_down, d_attn, d_vec, d_out, grad_parts)
+        cost_estimate=lasts(90, 1 << 20),
+    )(
+        up_own, down_own, down_x, d_query, d_keyval, d_vec, d_out, grad_parts, own_tok, grad_middle,
+        gain, block, chooser,
+    )
+
+
+def spread_columns(blocks, depth, seg, y_slow):
+    rows = blocks.shape[2]
+    wide_seg = seg % 128 == 0
+    if not wide_seg:
+        parts = blocks.reshape(2, 4, rows, depth, seg)
+        order = (2, 0, 3, 1, 4) if y_slow else (2, 3, 0, 1, 4)
+        return wide(jnp.transpose(parts, order).reshape(rows, 8 * depth * seg))
+
+    step = 32
+
+    def kernel(block, out):
+        for y in range(2):
+            for z in range(depth):
+                for xc in range(4):
+                    owner = y * depth + z if y_slow else z * 2 + y
+                    at = (owner * 4 + xc) * seg
+                    out[:, at : at + seg] = wide(block[y, xc, :, z * seg : (z + 1) * seg])
+
+    return pl.pallas_call(
+        kernel,
+        grid=(rows // step,),
+        in_specs=[pl.BlockSpec((2, 4, step, depth * seg), lambda index: (0, 0, index, 0))],
+        out_specs=pl.BlockSpec((step, 8 * depth * seg), lambda index: (index, 0)),
+        out_shape=jax.ShapeDtypeStruct((rows, 8 * depth * seg), jnp.float32),
+    )(blocks)
 
 
 def build(mesh):
@@ -844,19 +1205,23 @@
         head_cols = width // 8
         group_seqs = held * 4
 
-        def group_table(table):
+        def plane_table(table):
             parts = [
                 lax.dynamic_slice_in_dim(table, owner(my_z, y_at) * group_seqs, group_seqs)
                 for y_at in range(2)
             ]
             return jnp.stack(parts)
 
-        bases = jnp.stack([owner(my_z, y_at) * group_seqs for y_at in range(2)])
-        in_group = group_table(dealing) - bases[:, None]
-        source = in_group + (jnp.arange(2) * group_seqs)[:, None]
         micro = 2 * 4 * MB
-        lens = group_table(lengths).reshape(micro, SEATS)
-        source = source.reshape(micro, SEATS)
+        dealt_here = (
+            lax.dynamic_slice_in_dim(dealing, owner(my_z, my_y) * group_seqs, group_seqs)
+            - owner(my_z, my_y) * group_seqs
+        )
+        holders = (dealt_here // held).reshape(4, held)
+        slots = (dealt_here % held).reshape(4, held)
+        slot_for = jnp.sum(jnp.where(holders == my_xc, slots, 0), axis=1)
+        my_holders = lax.dynamic_index_in_dim(holders, my_xc, 0, keepdims=False)
+        lens = plane_table(lengths).reshape(micro, SEATS)
         ends = jnp.concatenate([lens[:, :1], lens[:, :1] + lens[:, 1:]], axis=1)
         starts = ends - lens
         at = jnp.arange(PACK)
@@ -864,14 +1229,22 @@
         row_valid = jnp.any(inside, axis=2)
         seat = jnp.sum(jnp.where(inside, jnp.arange(SEATS)[None, None, :], 0), axis=2)
         segment = jnp.where(row_valid, seat, -1)
-        offset = at[None, :] - jnp.sum(jnp.where(inside, starts[:, None, :], 0), axis=2)
-        source_row = jnp.sum(jnp.where(inside, source[:, None, :], 0), axis=2) * slot_len + offset
-        source_row = jnp.where(row_valid, source_row, 0).reshape(micro * PACK)
-        valid = row_valid.reshape(micro * PACK)
         allowed = (
             (at[None, :, None] >= at[None, None, :])
             & (segment[:, :, None] == segment[:, None, :])
             & row_valid[:, None, :]
+        )
+        my_inside = lax.dynamic_slice_in_dim(inside, member * MB, MB)
+        my_starts = lax.dynamic_slice_in_dim(starts, member * MB, MB)
+        my_lens = lax.dynamic_slice_in_dim(lens, member * MB, MB).reshape(held)
+        offset = at[None, :] - jnp.sum(jnp.where(my_inside, my_starts[:, None, :], 0), axis=2)
+        from_dev = jnp.sum(
+            jnp.where(my_inside, my_holders.reshape(MB, 1, SEATS), 0), axis=2
+        )
+        own_count = MB * PACK
+        own_valid = jnp.any(my_inside, axis=2).reshape(own_count)[:, None]
+        source_row = jnp.where(
+            own_valid[:, 0], (from_dev * slot_len + offset).reshape(own_count), 0
         )
 
         def up_columns(y_at):
@@ -900,38 +1273,61 @@
             up_bias,
             value_bias,
         ]
-        small = low(jnp.concatenate(small_parts))
+        small = low(lax.optimization_barrier(jnp.concatenate(small_parts)))
         small_count = small.shape[0]
         small = jnp.pad(small, (0, 16 * 256 - small_count)).reshape(16, 256)
-        attn_mine = jnp.concatenate([query_columns(my_y), low(keyval_weight)], axis=1)
-        attn_other = jnp.concatenate([query_columns(1 - my_y), low(keyval_weight)], axis=1)
-        out_slice = low(lax.dynamic_slice_in_dim(output_weight, my_xc * out_seg, out_seg, axis=0))
-        down_slice = low(lax.dynamic_slice_in_dim(down_weight, my_xc * ff_seg, ff_seg, axis=0))
+        def dealt(array):
+            return jnp.stack(
+                [
+                    lax.dynamic_index_in_dim(array, slot_for[index], 0, keepdims=False)
+                    for index in range(4)
+                ]
+            )
+
         flat = held * slot_len
+        chooser = low((source_row[:, None] == jnp.arange(flat)[None, :]) & own_valid)
         (
+            own_low,
+            own_cot,
+            up_piece,
+            down_piece,
             tokens_all,
             cotangent_all,
-            attn_all,
+            query_all,
+            keyval_all,
             small_all,
-            _,
             out_dealt,
             up_all,
-            w_down,
-        ) = first_gather(
+            down_all,
+        ) = opening(
             depth,
-            tokens.reshape(flat, width),
-            cotangent.reshape(flat, width),
-            attn_mine,
-            attn_other,
+            owner,
+            dealt(tokens),
+            dealt(cotangent),
+            chooser,
+            query_weight,
+            keyval_weight,
+            output_weight,
+            down_weight,
             small,
-            out_slice,
             up_columns(my_y),
             up_columns(1 - my_y),
-            down_slice,
-        )
-        tokens_all = tokens_all.reshape(8 * flat, width)
-        cotangent_all = cotangent_all.reshape(8 * flat, width)
-        w_down = w_down.reshape(depth * ff_seg, width)
+        )
+
+        ring = [(index, (index + 1) % depth) for index in range(depth)]
+
+        def ring_slot(buffer, piece, step):
+            at = (my_z - step + depth) % depth
+            return lax.dynamic_update_slice(
+                buffer, piece[None], (at,) + (0,) * piece.ndim
+            )
+
+        for step in range(3, depth):
+            down_piece = lax.ppermute(down_piece, "z", ring)
+            down_all = ring_slot(down_all, down_piece, step)
+        for step in range(1, depth - 2):
+            up_piece = lax.ppermute(up_piece, "z", ring)
+            up_all = ring_slot(up_all, up_piece, step)
         if y_slow:
             small_all = jnp.transpose(small_all, (1, 0, 2, 3))
         gathered_small = wide(small_all.reshape(fsdp_size, 16 * 256)[:, :small_count])
@@ -974,20 +1370,15 @@
                 )
             return values.reshape(depth, 2, rows_own, values.shape[-1])
 
-        attn_full = rows_in_order(attn_all)
-        w_query = attn_full[:, :head_cols]
-        w_keyval = attn_full[:, head_cols:]
+        w_query = rows_in_order(query_all)
+        keyval_all = keyval_all.reshape(2, 4, depth, out_seg, 2 * HEAD)
+        order = (0, 2, 1, 3, 4) if y_slow else (2, 0, 1, 3, 4)
+        w_keyval = jnp.transpose(keyval_all, order).reshape(width, 2 * HEAD)
         w_output = jnp.transpose(out_dealt, (1, 0, 2, 3)).reshape(head_cols, width)
-        w_up = rows_in_order(up_all)
-
-        packed = jnp.take(tokens_all, source_row, axis=0)
-        grad_mixed = jnp.where(
-            valid[:, None], jnp.take(cotangent_all, source_row, axis=0), jnp.zeros((), jnp.bfloat16)
-        )
-        own_count = MB * PACK
-        own_rows = wide(lax.dynamic_slice_in_dim(packed, member * own_count, own_count))
-        own_valid = lax.dynamic_slice_in_dim(valid, member * own_count, own_count)[:, None]
-        own_grad = wide(lax.dynamic_slice_in_dim(grad_mixed, member * own_count, own_count))
+
+        packed = tokens_all.reshape(micro * PACK, width)
+        grad_mixed = cotangent_all.reshape(micro * PACK, width)
+        own_grad = wide(own_cot)
 
         xhat_all, _ = normalize(wide(packed))
         normed_attn = low(xhat_all * gain_a + shift_a)
@@ -1010,24 +1401,52 @@
                 "mhst,mtd->mshd", low(probs), vals, preferred_element_type=jnp.float32
             ).reshape(micro * PACK, head_cols)
         )
-        (attn_out,) = plane_scatter([low(product(attended, w_output))], depth, 3)
-        middle = own_rows + (attn_out + bias_o)
-        xhat_m, scale_m = normalize(middle)
-        normed_mlp = plane_gather(low(xhat_m * gain_m + shift_m), depth, 4)
+        attended, down_piece = lax.optimization_barrier((attended, down_piece))
+        middle, normed_mlp, up_hop_1, up_hop_2 = attention_out(
+            depth,
+            attended,
+            w_output,
+            own_low,
+            bias_o[None],
+            gain_m[None],
+            shift_m[None],
+            up_piece,
+        )
+        up_all = ring_slot(up_all, up_hop_1, depth - 2)
+        up_all = ring_slot(up_all, up_hop_2, depth - 1)
+        normed_mlp = normed_mlp.reshape(micro * PACK, width)
+        w_down = down_all.reshape(depth * ff_seg, width)
+        grad_act = product_cols(grad_mixed, w_down)
+        w_up = rows_in_order(up_all)
         hidden = product(normed_mlp, w_up) + my_bias_u
         activated, slope = gelu_parts(hidden)
         activated = low(activated)
-        grad_hidden = low(slope * product_cols(grad_mixed, w_down))
-        mlp_sum, grad_normed = plane_scatter(
-            [low(product(activated, w_down)), low(product_cols(grad_hidden, w_up))], depth, 5
-        )
-        block_own = low(jnp.where(own_valid, middle + (mlp_sum + bias_d), 0.0))
-        grad_middle = own_grad + norm_back(grad_normed, gain_m, xhat_m, scale_m)
-        d_down = low(product_rows(activated, grad_mixed)).reshape(depth, ff_seg, width)
-        d_up = rows_by_z(low(product_rows(normed_mlp, grad_hidden)))
-
+        grad_hidden = low(slope * grad_act)
+
+        down_parts = low(product_rows(activated, grad_mixed)).reshape(depth, ff_seg, width)
+        up_parts = rows_by_z(low(product_rows(normed_mlp, grad_hidden)))
+        grad_normed, grad_middle, grad_branch, block_own, d_down, d_up = mlp_back(
+            depth,
+            grad_hidden,
+            w_up,
+            activated,
+            w_down,
+            middle,
+            own_cot,
+            gain_m[None],
+            bias_d[None],
+            down_parts,
+            up_parts,
+        )
+        grad_branch = grad_branch.reshape(micro * PACK, width)
+        down_x = lax.ppermute(d_down, "x", [(0, 1), (1, 0)])
+        for step in range(2, depth):
+            d_up = lax.ppermute(d_up, "z", ring)
+            at = (my_z - 1 - step + 2 * depth) % depth
+            term = lax.dynamic_index_in_dim(up_parts, at, 0, keepdims=False)
+            d_up = low(wide(d_up) + wide(term))
+        xhat_m, _ = normalize(middle)
         grad_branch_own = low(grad_middle)
-        grad_branch = plane_gather(grad_branch_own, depth, 6)
         d_output = low(product_rows(attended, grad_branch))
         grad_att = low(product_cols(grad_branch, w_output)).reshape(micro, PACK, my_heads, HEAD)
         grad_probs = jnp.einsum("mshd,mtd->mhst", grad_att, vals, preferred_element_type=jnp.float32)
@@ -1051,8 +1470,6 @@
         d_query = low(product_rows(normed_attn, grad_query))
         d_keyval = low(product_rows(normed_attn, grad_keyval))
         grad_input_part = product_cols(grad_query, w_query) + product_cols(grad_keyval, w_keyval)
-        own_xhat, own_scale = normalize(own_rows)
-
         def colsum(values):
             return jnp.sum(wide(values), axis=0)
 
@@ -1089,41 +1506,56 @@
         else:
             d_vec = vectors.reshape(depth, 2, 16, 256)
 
-        d_attn = rows_by_z(jnp.concatenate([d_query, d_keyval], axis=1))
         d_out_parts = jnp.transpose(
             d_output.reshape(depth // 4, 4, out_seg, width), (1, 0, 2, 3)
         )
-        up_all, down_all, attn_all, vec_all, out_all, grad_first = last_scatter(
+        if y_slow:
+            d_keyval = d_keyval.reshape(2, depth, 4, out_seg, 2 * HEAD)
+            d_keyval = jnp.transpose(d_keyval, (0, 2, 1, 3, 4))
+        else:
+            d_keyval = d_keyval.reshape(depth, 2, 4, out_seg, 2 * HEAD)
+            d_keyval = jnp.transpose(d_keyval, (1, 2, 0, 3, 4))
+        d_keyval = d_keyval.reshape(8, depth * out_seg, 2 * HEAD)
+
+        send_seq = jnp.argmax(my_holders[None, :] == jnp.arange(4)[:, None], axis=1)
+        pos = jnp.arange(slot_len)
+        live = pos[None, :] < my_lens[send_seq][:, None]
+        seq_starts = (my_starts + jnp.arange(MB)[:, None] * PACK).reshape(held)
+        send_rows = jnp.where(live, seq_starts[send_seq][:, None] + pos[None, :], -1)
+        back_chooser = low(send_rows.reshape(flat)[:, None] == jnp.arange(own_count)[None, :])
+        up_all, down_all, query_sum, kv_sum, vec_all, out_all, block_got, grad_got = closing(
             depth,
             d_up,
             d_down,
-            d_attn,
+            down_x,
+            rows_by_z(d_query),
+            d_keyval,
             d_vec,
             d_out_parts,
-            low(grad_input_part).reshape(8, MB * PACK, width),
-        )
-        grad_input = low(grad_middle + norm_back(grad_first, gain_a, own_xhat, own_scale))
-
-        def by_y(pair):
-            first = my_y == 0
-            return (
-                jnp.where(first, pair[0], pair[1]),
-                jnp.where(first, pair[1], pair[0]),
+            low(grad_input_part).reshape(8, own_count, width),
+            own_low,
+            grad_middle,
+            gain_a[None],
+            block_own,
+            back_chooser,
+        )
+        from_dealt = jnp.argmax(slot_for[None, :] == jnp.arange(held)[:, None], axis=1)
+
+        def held_order(got):
+            return jnp.stack(
+                [
+                    lax.dynamic_index_in_dim(got, from_dealt[index], 0, keepdims=False)
+                    for index in range(held)
+                ]
             )
 
-        up_pair = [item.reshape(4, rows_own, depth, ff_seg) for item in by_y(up_all)]
+        up_grad = spread_columns(up_all, depth, ff_seg, y_slow)
         if y_slow:
-            up_grad = jnp.stack([jnp.transpose(item, (1, 2, 0, 3)) for item in up_pair], axis=1)
+            query_grad = jnp.transpose(query_sum, (2, 0, 1, 3))
         else:
-            up_grad = jnp.stack([jnp.transpose(item, (1, 2, 0, 3)) for item in up_pair], axis=2)
-        up_grad = wide(up_grad.reshape(rows_own, ff))
-        query_pair = by_y(attn_all[..., :head_cols])
-        if y_slow:
-            query_grad = jnp.stack([jnp.transpose(item, (1, 0, 2)) for item in query_pair], axis=1)
-        else:
-            query_grad = jnp.stack([jnp.transpose(item, (1, 0, 2)) for item in query_pair], axis=2)
+            query_grad = jnp.transpose(query_sum, (2, 1, 0, 3))
         query_grad = wide(query_grad.reshape(rows_own, width))
-        keyval_grad = jnp.sum(wide(attn_all[..., head_cols:]), axis=(0, 1))
+        keyval_grad = wide(kv_sum.reshape(rows_own, 2 * HEAD))
         down_grad = wide(down_all.reshape(ff_own, width))
         output_grad = wide(out_all.reshape(rows_own, width))
         vec_own = jnp.sum(wide(vec_all), axis=0).reshape(16 * 256)
@@ -1139,36 +1571,9 @@
             bias_v_grad,
         ) = [vec_own[start : start + size] for start, size in zip(begins, sizes)]
 
-        dealt_here = lax.dynamic_index_in_dim(in_group, my_y, 0, keepdims=False)
-        holders = (dealt_here // held).reshape(4, held)
-        slots = (dealt_here % held).reshape(4, held)
-        my_holders = lax.dynamic_index_in_dim(holders, my_xc, 0, keepdims=False)
-        my_lens = lax.dynamic_slice_in_dim(lens, member * MB, MB).reshape(held)
-        my_starts = (
-            lax.dynamic_slice_in_dim(starts, member * MB, MB) + jnp.arange(MB)[:, None] * PACK
-        ).reshape(held)
-        send_seq = jnp.argmax(my_holders[None, :] == jnp.arange(4)[:, None], axis=1)
-        pos = jnp.arange(slot_len)
-        live = pos[None, :] < my_lens[send_seq][:, None]
-        send_rows = jnp.where(live, my_starts[send_seq][:, None] + pos[None, :], 0)
-        slot_of = jnp.sum(jnp.where(holders == my_xc, slots, 0), axis=1)
-        from_dev = jnp.argmax(slot_of[None, :] == jnp.arange(held)[:, None], axis=1)
-
-        def send_back(own):
-            out = jnp.where(
-                live[..., None], jnp.take(own, send_rows, axis=0), jnp.zeros((), jnp.bfloat16)
-            )
-            got = lax.all_to_all(out, DP, split_axis=0, concat_axis=0, tiled=True)
-            return jnp.stack(
-                [
-                    lax.dynamic_index_in_dim(got, from_dev[index], 0, keepdims=False)
-                    for index in range(held)
-                ]
-            )
-
         return (
-            send_back(block_own),
-            send_back(grad_input),
+            held_order(block_got),
+            held_order(grad_got),
             gain_a_grad,
             shift_a_grad,
             query_grad,

time: 964 us -> 648 us (0.67)
  Pallas kernels: 679 us -> 420 us
  local copies, waits for them, and re-layouts: 101 us -> 48.9 us
  waiting for transfers between devices: 0.01 us -> 29.4 us
  other arithmetic: 64.3 us -> 36.1 us
  matrix products: 91 us -> 78.9 us
    pallas_call x6 -> x5, Pallas kernels: 679 us -> 420 us  [the longest x1 143 us: closing(): pl.pallas_call(kernel, out_shape=[low_shape(2, 4, *up_own.shape[1:]), low...]
    gather x5 -> x1, local copies, waits for them, and re-layouts: 34.9 us -> 0.64 us  [shards(): seq_starts[send_seq][:, None] + pos[None, :]]
    ppermute x0 -> x5, waiting for transfers between devices: none -> 29.4 us  [the longest x2 29.4 us: shards(): d_up = lax.ppermute(d_up, 'z', ring)]
    ppermute x0 -> x5, starting transfers between devices: none -> 13 us  [the longest x1 9.25 us: shards(): down_piece = lax.ppermute(down_piece, 'z', ring)]
    select_n x4, other arithmetic: 13.7 us -> 0.83 us  [the longest x1 0.74 us: shards(): holders = (dealt_here // held).reshape(4, held)]
    convert_element_type x2 -> x1, local copies, waits for them, and re-layouts: 11.8 us -> 1.81 us  [wide(): return values.astype(jnp.float32)]
    dot_general x5 -> x4, matrix products: 36.2 us -> 27 us  [product_cols(): lax.dot_general(left_mat, right_mat, (((1,), (1,)), ((), ())), preferred_...]
    dot_general x5 -> x3, matrix products: 26.8 us -> 17.7 us  [product(): return jnp.dot(left_mat, right_mat, preferred_element_type=jnp.float32)]
  transfers between devices with their start and end apart: 2 -> 5, of which waited for: 0 -> 2; matrix products, arithmetic and copies ran while one was open for 6% -> 8% of each run, Pallas kernels for 0% -> 0%
where the time goes in v2:
time: 648 us; the launch traced here: 644 us
  Pallas kernels  420 us (65%)
  matrix products  78.9 us (12%)
  local copies, waits for them, and re-layouts  48.9 us (8%)
  other arithmetic  36.1 us (6%)
  waiting for transfers between devices  29.4 us (5%)
  between operations  17.4 us (3%)
  starting transfers between devices  13 us (2%)
    pallas_call x1, Pallas kernels, closing(): pl.pallas_call(kernel, out_shape=[low_shape(2, 4, *up_own.shape[1:]), low...  143 us
    pallas_call x1, Pallas kernels, mlp_back(): pl.pallas_call(kernel, out_shape=[wide_shape(rows, width), wide_shape(row...  107 us
    pallas_call x1, Pallas kernels, opening(): pl.pallas_call(kernel, out_shape=[low_shape(rows, width), low_shape(rows,...  104 us
    pallas_call x1, Pallas kernels, attention_out(): pl.pallas_call(kernel, out_shape=[wide_shape(rows, width), low_shape(8, r...  59.3 us
    ppermute x2, waiting for transfers between devices, shards(): d_up = lax.ppermute(d_up, 'z', ring)  29.4 us
    dot_general x4, matrix products, product_cols(): lax.dot_general(left_mat, right_mat, (((1,), (1,)), ((), ())), preferred_...  27 us
    dot_general x5, matrix products, product_rows(): lax.dot_general(left_mat, right_mat, (((0,), (0,)), ((), ())), preferred_...  24.8 us
    unnamed x148, local copies, waits for them, and re-layouts  18.9 us
  transfers between devices with their start and end apart: 5, of which 2 were waited for; matrix products, arithmetic and copies ran while one was open for 8% of the time, Pallas kernels for 0%

profile of v2, /device:TPU:9, one launch (start us, length us, event | category | flops | bytes accessed | tf_op | source)
XLA Modules:
  0.0 644.1 jit_solution(5046548834202950200)
XLA Ops:
  26.8 103.9 %shard_map.297 = (bf16[160,2048]{1,0:T(8,128)(2,1)}, bf16[160,2048]{1,0:T(8,128)(2,1)}, bf16[2,256,1024]{2,1,0:T(8,128)(2,1)}, bf16[256,2048]{1,0:T(8,128)(2,1)}...) custom-call(bf16[4,64,2048]{2,1,0:T(8,128)(2,1)} %pad_maximum_fusion, ...), custom_call_target="tpu_custom_call" | custom-call | flops 85000003584 | bytes 1048576 | tf_op jit(solution)/shard_map/pallas_call | solution.py:705
  130.8 9.3 %collective-permute-start = (bf16[256,2048]{1,0:T(8,128)(2,1)}, bf16[256,2048]{1,0:T(8,128)(2,1)S(1)}, u32[]{:S(2)}, u32[]{:S(2)}) collective-permute-start(bf16[256,2048]{1,0:T(8,128)(2,1)} %get-tuple-element.53), channel_id=1, source_target_pairs={{0,8},{8,16},{16,24},{24,0},{1,9},{9,17},{17,25},{25,1},{2,10},{10... | collective-permute-start | bytes 3145736 | tf_op jit(solution)/shard_map/ppermute | solution.py:1326
  142.5 3.3 convert_reduce_fusion
  147.5 4.5 add_convert_fusion.1
  158.3 4.3 fusion.9
  164.6 2.5 fusion.60
  167.2 2.7 fusion.18
  191.5 59.3 %shard_map.298 = (f32[160,2048]{1,0:T(8,128)}, bf16[8,160,2048]{2,1,0:T(8,128)(2,1)}, bf16[2,256,1024]{2,1,0:T(8,128)(2,1)}, bf16[2,256,1024]{2,1,0:T(8,128)(2,1)}) custom-call(bf16[1280,256]{1,0:T(8,128)(2,1)} %bitcast.224, bf16[256,2048]{1,0:T(8,128)(2,1)} %bitcast.270, bf16[160,2048]{1,0:T(8,128)(2,1)} %get-tuple-element.56.tok, f32[1,2048]{1,0:T(1,128)} %bitcast.244, ...), custom_call_target="tpu_custom_call" | custom-call | flops 60000002048 | bytes 1048576 | tf_op jit(solution)/shard_map/pallas_call | solution.py:821
  253.7 11.8 %multiply_convert_fusion = (bf16[1280,1024]{1,0:T(8,128)(2,1)S(1)}, f32[1280,1024]{1,0:T(8,128)}) fusion(f32[1024]{0:T(1024)S(1)} %pad_maximum_fusion.9, bf16[1280,2048]{1,0:T(8,128)(2,1)} %bitcast.265, bf16[2048,1024]{1,0:T(8,128)(2,1)S(1)} %bitcast.256), kind=kOutput, calls=%fused_computation.21 | convolution fusion | flops 5381816320 | bytes 17305600 | tf_op jit(solution)/shard_map/dot_general | solution.py:33
  265.8 13.3 %convert_reduce_fusion.1 = (f32[1024]{0:T(1024)S(1)}, bf16[1280,1024]{1,0:T(8,128)(2,1)S(1)}) fusion(bf16[1280,2048]{1,0:T(8,128)(2,1)S(1)} %bitcast.260, bf16[1024,2048]{1,0:T(8,128)(2,1)S(1)} %bitcast.254, f32[1280,1024]{1,0:T(8,128)} %get-tuple-element.208, f32[1024]{0:T(1024)S(1)} %pad_maximum_fusion.9), kind=kOutput, calls=%fused_computation.20 | convolution fusion | flops 5397543936 | bytes 17309696 | tf_op jit(solution)/shard_map/dot_general | solution.py:43
  279.1 7.4 %convolution_convert_fusion = bf16[2048,1024]{1,0:T(8,128)(2,1)} fusion(bf16[1280,2048]{1,0:T(8,128)(2,1)S(1)} %bitcast.268, bf16[1280,1024]{1,0:T(8,128)(2,1)S(1)} %get-tuple-element.215.gh), kind=kOutput, calls=%fused_computation.23 | convolution fusion | flops 5370806272 | bytes 12058624 | tf_op jit(solution)/shard_map/dot_general | solution.py:37
  286.6 7.6 %convolution_convert_fusion.1 = bf16[1024,2048]{1,0:T(8,128)(2,1)} fusion(bf16[1280,1024]{1,0:T(8,128)(2,1)S(1)} %get-tuple-element.207.act, bf16[1280,2048]{1,0:T(8,128)(2,1)S(1)} %bitcast.261), kind=kOutput, calls=%fused_computation.24 | convolution fusion | flops 5370806272 | bytes 12058624 | tf_op jit(solution)/shard_map/dot_general | solution.py:37
  294.3 106.7 %shard_map.299 = (f32[160,2048]{1,0:T(8,128)}, f32[160,2048]{1,0:T(8,128)}, bf16[8,160,2048]{2,1,0:T(8,128)(2,1)}, bf16[160,2048]{1,0:T(8,128)(2,1)}, bf16[256,2...) custom-call(bf16[1280,1024]{1,0:T(8,128)(2,1)} %copy-done.48, bf16[2048,1024]{1,0:T(8,128)(2,1)} %bitcast.257, ...), custom_call_target="tpu_custom_call" | custom-call | flops 95000002560 | bytes 1048576 | tf_op jit(solution)/shard_map/pallas_call | solution.py:920
  401.1 4.2 convolution_convert_fusion.5
  414.5 2.9 fusion.23
  417.5 6.6 %fusion.51 = (bf16[2048]{0:T(1024)(128)(2,1)S(1)}, bf16[2048]{0:T(1024)(128)(2,1)S(1)}, bf16[1280,2048]{1,0:T(8,128)(2,1)}, bf16[1280,2048]{1,0:T(8,128)(2,1)}) fusion(f32[1280]{0:T(1024)S(1)} %copy-done.31, f32[1280]{0:T(1024)S(1)} %copy-done.32, bf16[8,160,2048]{2,1,0:T(8,128)(2,1)S(1)} %bitcast.202, f32[2048]{0:T(1024)S(1)} %bitcast.237, ...), kind=kOutput, calls=%fused_computation.202 | convolution fusion | flops 1372319744 | bytes 27953152 | tf_op jit(solution)/shard_map/dot_general | solution.py:43
  427.4 5.4 convolution_convert_fusion.2
  434.5 13.6 %collective-permute-done.2 = bf16[2,256,1024]{2,1,0:T(8,128)(2,1)S(1)} collective-permute-done((bf16[2,256,1024]{2,1,0:T(8,128)(2,1)}, bf16[2,256,1024]{2,1,0:T(8,128)(2,1)S(1)}, u32[]{:S(2)}, u32[]{:S(2)}) %collective-permute-start.2) | collective-permute-done | bytes 1048608 | tf_op jit(solution)/shard_map/ppermute | solution.py:1444
  452.4 2.7 convolution_convert_fusion.4
  455.1 15.9 %collective-permute-done.3 = bf16[2,256,1024]{2,1,0:T(8,128)(2,1)S(1)} collective-permute-done((bf16[2,256,1024]{2,1,0:T(8,128)(2,1)S(1)}, bf16[2,256,1024]{2,1,0:T(8,128)(2,1)S(1)}, u32[]{:S(2)}, u32[]{:S(2)}) %collective-permute-start.3) | collective-permute-done | bytes 1048608 | tf_op jit(solution)/shard_map/ppermute | solution.py:1444
  473.3 143.1 %shard_map.300 = (bf16[2,4,256,1024]{3,2,1,0:T(8,128)(2,1)}, bf16[4,256,2048]{2,1,0:T(8,128)(2,1)}, bf16[2,4,256,256]{3,2,1,0:T(8,128)(2,1)}, bf16[4,64,256]{2,1...) custom-call(bf16[2,256,1024]{2,1,0:T(8,128)(2,1)} %fusion.11.up, ...), custom_call_target="tpu_custom_call" | custom-call | flops 89999998976 | bytes 1048576 | tf_op jit(solution)/shard_map/pallas_call | solution.py:1098
  617.8 6.7 %bitcast_convert_fusion = f32[1024,2048]{1,0:T(8,128)} fusion(bf16[4,256,2048]{2,1,0:T(8,128)(2,1)} %get-tuple-element.81), kind=kLoop, calls=%fused_computation.22 | loop fusion | flops 2097152 | bytes 12582912 | tf_op jit(solution)/shard_map/convert_element_type | solution.py:29
  624.4 7.4 %shard_map.301 = f32[256,8192]{1,0:T(8,128)} custom-call(bf16[2,4,256,1024]{3,2,1,0:T(8,128)(2,1)} %get-tuple-element.80.block), custom_call_target="tpu_custom_call" | custom-call | tf_op jit(solution)/shard_map/pallas_call | solution.py:1157
  633.8 3.0 copy.88
  (282 shorter events, 78.7 us)
Async XLA Ops:
  130.7 58.5 %collective-permute-start.1 = (bf16[2,256,1024]{2,1,0:T(8,128)(2,1)}, bf16[2,256,1024]{2,1,0:T(8,128)(2,1)}, u32[]{:S(2)}, u32[]{:S(2)}) collective-permute-start(bf16[2,256,1024]{2,1,0:T(8,128)(2,1)} %get-tuple-element.57), channel_id=1, source_target_pairs={{0,8},{8,16},{16,24},{24,0},{1,9},{9,17},{17,25},{25,1},{2,10},{10... | collective-permute-start | bytes 3145736 | tf_op jit(solution)/shard_map/ppermute | solution.py:1329
  130.8 58.5 %collective-permute-start = (bf16[256,2048]{1,0:T(8,128)(2,1)}, bf16[256,2048]{1,0:T(8,128)(2,1)S(1)}, u32[]{:S(2)}, u32[]{:S(2)}) collective-permute-start(bf16[256,2048]{1,0:T(8,128)(2,1)} %get-tuple-element.53), channel_id=1, source_target_pairs={{0,8},{8,16},{16,24},{24,0},{1,9},{9,17},{17,25},{25,1},{2,10},{10... | collective-permute-start | bytes 3145736 | tf_op jit(solution)/shard_map/ppermute | solution.py:1326
  163.4 17.0 %copy-start.6 = (bf16[1280,128]{1,0:T(8,128)(2,1)}, bf16[1280,128]{1,0:T(8,128)(2,1)S(1)}, u32[]{:S(2)}) copy-start(bf16[1280,128]{1,0:T(8,128)(2,1)S(1)} %get-tuple-element.168) | copy-start | bytes 983044
  164.6 18.2 %copy-start.15 = (bf16[160,2048]{1,0:T(8,128)(2,1)S(1)}, bf16[160,2048]{1,0:T(8,128)(2,1)}, u32[]{:S(2)}) copy-start(bf16[160,2048]{1,0:T(8,128)(2,1)} %get-tuple-element.65.cot) | copy-start | bytes 1966084
  167.1 17.0 %copy-start.4 = (f32[16,2,80,80]{2,3,1,0:T(8,128)}, f32[16,2,80,80]{2,3,1,0:T(8,128)S(1)}, u32[]{:S(2)}) copy-start(f32[16,2,80,80]{2,3,1,0:T(8,128)S(1)} %get-tuple-element.206) | copy-start | bytes 2457604
  167.1 13.9 %copy-start.27 = (f32[1,1,8,256]{3,2,1,0:T(8,128)S(1)}, f32[1,1,8,256]{3,2,1,0:T(8,128)}, u32[]{:S(2)}) copy-start(f32[1,1,8,256]{3,2,1,0:T(8,128)} %get-tuple-element.173) | copy-start | bytes 24580
  167.1 14.5 %copy-start.26 = (f32[1,1,8,256]{3,2,1,0:T(8,128)S(1)}, f32[1,1,8,256]{3,2,1,0:T(8,128)}, u32[]{:S(2)}) copy-start(f32[1,1,8,256]{3,2,1,0:T(8,128)} %get-tuple-element.172) | copy-start | bytes 24580
  167.1 15.1 %copy-start.25 = (f32[1,1,8,256]{3,2,1,0:T(8,128)S(1)}, f32[1,1,8,256]{3,2,1,0:T(8,128)}, u32[]{:S(2)}) copy-start(f32[1,1,8,256]{3,2,1,0:T(8,128)} %get-tuple-element.171) | copy-start | bytes 24580
  167.1 16.4 %copy-start.24 = (f32[1,1,8,256]{3,2,1,0:T(8,128)S(1)}, f32[1,1,8,256]{3,2,1,0:T(8,128)}, u32[]{:S(2)}) copy-start(f32[1,1,8,256]{3,2,1,0:T(8,128)} %get-tuple-element.170) | copy-start | bytes 24580
  167.1 17.0 %copy-start.34 = (s32[2,2]{1,0:T(2,128)S(1)}, s32[2,2]{1,0:T(2,128)}, u32[]{:S(2)}) copy-start(s32[2,2]{1,0:T(2,128)} %get-tuple-element.222) | copy-start | bytes 52
  167.2 17.1 %copy-start.33 = (s32[2,2]{1,0:T(2,128)S(1)}, s32[2,2]{1,0:T(2,128)}, u32[]{:S(2)}) copy-start(s32[2,2]{1,0:T(2,128)} %get-tuple-element.136) | copy-start | bytes 52
  167.2 17.2 %copy-start.45 = (s32[4]{0:T(128)S(1)}, s32[4]{0:T(128)}, u32[]{:S(2)}) copy-start(s32[4]{0:T(128)} %get-tuple-element.72) | copy-start | bytes 52
  191.5 59.3 %copy-start.37 = (bf16[4,2,256,1024]{3,2,1,0:T(8,128)(2,1)S(1)}, bf16[4,2,256,1024]{3,2,1,0:T(8,128)(2,1)}, u32[]{:S(2)}) copy-start(bf16[4,2,256,1024]{3,2,1,0:T(8,128)(2,1)} %bitcast_dynamic-update-slice_fusion.3) | copy-start | bytes 12582916
  250.8 14.9 %slice-start.5 = ((s8[5242880]{0:T(1024)(128)(4,1)}), s8[4194304]{0:T(1024)(128)(4,1)S(1)}, s32[]{:S(2)}) async-start(s8[5242880]{0:T(1024)(128)(4,1)} %bitcast.258), calls=%async_computation.5 | async-start | bytes 8388608
  265.6 21.0 %copy-start.47 = (bf16[1280,1024]{1,0:T(8,128)(2,1)}, bf16[1280,1024]{1,0:T(8,128)(2,1)S(1)}, u32[]{:S(2)}) copy-start(bf16[1280,1024]{1,0:T(8,128)(2,1)S(1)} %get-tuple-element.207.act) | copy-start | bytes 7864324
  265.6 13.5 %slice-start.7 = ((s8[5242880]{0:T(1024)(128)(4,1)}), s8[4194304]{0:T(1024)(128)(4,1)S(1)}, s32[]{:S(2)}) async-start(s8[5242880]{0:T(1024)(128)(4,1)} %bitcast.266), calls=%async_computation.7 | async-start | bytes 8388608
  294.3 106.7 %copy-start.40 = (bf16[4,1,64,2048]{3,2,1,0:T(8,128)(2,1)S(1)}, bf16[4,1,64,2048]{3,2,1,0:T(8,128)(2,1)}, u32[]{:S(2)}) copy-start(bf16[4,1,64,2048]{3,2,1,0:T(8,128)(2,1)} %get-tuple-element.55) | copy-start | bytes 3145732
  425.9 22.2 %collective-permute-start.2 = (bf16[2,256,1024]{2,1,0:T(8,128)(2,1)}, bf16[2,256,1024]{2,1,0:T(8,128)(2,1)S(1)}, u32[]{:S(2)}, u32[]{:S(2)}) collective-permute-start(bf16[2,256,1024]{2,1,0:T(8,128)(2,1)} %get-tuple-element.66), channel_id=1, source_target_pairs={{0,8},{8,16},{16,24},{24,0},{1,9},{9,17},{17,25},{25,1},{2,10},{10... | collective-permute-start | bytes 3145736 | tf_op jit(solution)/shard_map/ppermute | solution.py:1444
  427.4 44.9 %collective-permute-start.4 = (bf16[256,2048]{1,0:T(8,128)(2,1)}, bf16[256,2048]{1,0:T(8,128)(2,1)S(1)}, u32[]{:S(2)}, u32[]{:S(2)}) collective-permute-start(bf16[256,2048]{1,0:T(8,128)(2,1)} %get-tuple-element.67.down), channel_id=1, source_target_pairs={{0,2},{2,0},{1,3},{3,1},{4,6},{6,4},{5,7},{7,5},{8,10},{10,8},{9,1... | collective-permute-start | bytes 3145736 | tf_op jit(solution)/shard_map/ppermute | solution.py:1442
  427.4 25.0 %slice-start.2 = ((s8[5242880]{0:T(1024)(128)(4,1)}), s8[4194304]{0:T(1024)(128)(4,1)S(1)}, s32[]{:S(2)}) async-start(s8[5242880]{0:T(1024)(128)(4,1)} %bitcast.206), calls=%async_computation.2 | async-start | bytes 8388608
  432.8 15.3 %copy-start.12 = (bf16[2048,1024]{1,0:T(8,128)(2,1)S(1)}, bf16[2048,1024]{1,0:T(8,128)(2,1)}, u32[]{:S(2)}) copy-start(bf16[2048,1024]{1,0:T(8,128)(2,1)} %convolution_convert_fusion) | copy-start | bytes 12582916
  432.8 17.9 %copy-start.30 = (bf16[8,256]{1,0:T(8,128)(2,1)S(1)}, bf16[8,256]{1,0:T(8,128)(2,1)}, u32[]{:S(2)}) copy-start(bf16[8,256]{1,0:T(8,128)(2,1)} %reshape.459) | copy-start | bytes 12292
  432.8 19.6 %slice-start.3 = ((s8[5242880]{0:T(1024)(128)(4,1)}), s8[1048576]{0:T(1024)(128)(4,1)S(1)}, s32[]{:S(2)}) async-start(s8[5242880]{0:T(1024)(128)(4,1)} %bitcast.206), calls=%async_computation.3 | async-start | bytes 2097152
  448.5 22.4 %collective-permute-start.3 = (bf16[2,256,1024]{2,1,0:T(8,128)(2,1)S(1)}, bf16[2,256,1024]{2,1,0:T(8,128)(2,1)S(1)}, u32[]{:S(2)}, u32[]{:S(2)}) collective-permute-start(bf16[2,256,1024]{2,1,0:T(8,128)(2,1)S(1)} %fusion.12), channel_id=1, source_target_pairs={{0,8},{8,16},{16,24},{24,0},{1,9},{9,17},{17,25},{25,1},{2,10},{10... | collective-permute-start | bytes 3145736 | tf_op jit(solution)/shard_map/ppermute | solution.py:1444
  (39 other events, 232.2 us)

commit v3 on v2

--- a/solution.py
+++ b/solution.py
@@ -328,8 +328,9 @@
 
 
 class LineGather:
-    def __init__(self, net, spot, slots):
+    def __init__(self, net, spot, slots, moves=None):
         self.spot, depth, z = spot, spot.depth, spot.z
+        self.moves = moves
         self.hops = []
         for step in range(depth - 1):
             lower = jnp.maximum(z - step, 0)
@@ -347,16 +348,22 @@
     def remotes(depth):
         return 2 * (depth - 1)
 
+    def pick(self, cond, slot):
+        return cond if self.moves is None else cond & self.moves(slot)
+
     def sends(self, step):
         z, last = self.spot.z, self.spot.depth - 1
         return (
-            ((z >= step) & (z < last), self.hops[step][0]),
-            ((z + step <= last) & (z > 0), self.hops[step][1]),
+            (self.pick((z >= step) & (z < last), z - step), self.hops[step][0]),
+            (self.pick((z + step <= last) & (z > 0), z + step), self.hops[step][1]),
         )
 
     def takes(self, step):
         z, last = self.spot.z, self.spot.depth - 1
-        return ((z >= step + 1, self.hops[step][0]), (z + step + 1 <= last, self.hops[step][1]))
+        return (
+            (self.pick(z >= step + 1, z - 1 - step), self.hops[step][0]),
+            (self.pick(z + step + 1 <= last, z + 1 + step), self.hops[step][1]),
+        )
 
     def start(self, step):
         for cond, copy in self.sends(step):
@@ -539,30 +546,27 @@
         result[..., at] = low(product(chooser[...], rows)).reshape(*result.shape[:-1], step)
 
 
-def opening(depth, owner, tok_send, cot_send, chooser, query_weight, keyval_weight, output_weight, down_weight, small, up_mine, up_other):
+def opening(depth, owner, tokens, cotangent, sender, chooser, query_weight, keyval_weight, output_weight, small, up_mine, up_other):
     rows = chooser.shape[0]
-    width = tok_send.shape[-1]
+    width = tokens.shape[-1]
     group = depth // 4
     rows_own = query_weight.shape[0]
     head_cols = width // 8
     kv_rows = rows_own // 4
     kv_cols = keyval_weight.shape[1]
-    seg = down_weight.shape[0] // 4
 
     def kernel(
-        tok, cot, choose, query_w, kv_w, out_w, down_w, small_m, up_m, up_o,
-        own_tok, own_cot, up_own, down_2,
-        tok_all, cot_all, query_all, kv_all, small_all, out_dealt, up_all, down_all,
-        tok_got, cot_got, out_all, kv_line, query_m, query_o, query_y, small_y, down_m, down_1,
-        query_f, out_f, kv_f, down_f, *sems,
+        tok_held, cot_held, send, choose, query_w, kv_w, out_w, small_m, up_m, up_o,
+        own_tok, own_cot, up_own,
+        tok_all, query_all, kv_all, small_all, out_all,
+        tok, cot, tok_got, cot_got, out_v, kv_line, query_m, query_o, query_y, small_y,
+        query_f, out_f, kv_f, *sems,
     ):
         spot = Spot(depth)
         net = Net(*sems)
         z, y = spot.z, spot.y
         xc = spot.x * 2 + spot.c
-        after, _ = spot.ring()
-        before = lax.rem(z + depth - 1, depth)
-        before_2 = lax.rem(z + 2 * depth - 2, depth)
+        source = z // group == xc
 
         def head_base(y_at):
             return pl.multiple_of(owner(xc * group, y_at) * rows_own, 128)
@@ -573,64 +577,67 @@
         def z_slot(at):
             return kv_line.at[pl.ds(pl.multiple_of(at * kv_rows, kv_rows), kv_rows)]
 
-        reads = [
-            net.local(query_w.at[:, pl.ds(head_base(1 - y), head_cols)], query_f.at[0]),
-            net.local(strip(down_w, seg), down_f),
-            net.local(strip(out_w, kv_rows), out_f),
-            net.local(strip(kv_w, kv_rows), kv_f),
-            net.local(query_w.at[:, pl.ds(head_base(y), head_cols)], query_f.at[1]),
-        ]
+        read_query_o = net.local(query_w.at[:, pl.ds(head_base(1 - y), head_cols)], query_f.at[0])
+        read_out = net.local(out_w, out_f)
+        read_kv = net.local(strip(kv_w, kv_rows), kv_f)
+        read_query = net.local(query_w.at[:, pl.ds(head_base(y), head_cols)], query_f.at[1])
         tok_deal = DpExchange(net, spot, tok, tok_got)
         cot_deal = DpExchange(net, spot, cot, cot_got)
         tok_run = PlaneGather(net, spot, own_tok, tok_all)
-        cot_run = PlaneGather(net, spot, own_cot, cot_all, share=1)
         kv_run = PlaneGather(net, spot, kv_line, kv_all)
         y_query = net.remote(query_o, query_y, spot.to_y)
         y_small = net.remote(small_m, small_y, spot.to_y)
         y_up = net.remote(up_o, up_own.at[y], spot.to_y, up_own.at[1 - y])
-        d_hops = [net.remote(down_m, down_1, after), net.remote(down_1, down_2, after)]
         keep_small = net.local(small_m, small_all.at[z, y])
-        keep_up_mine = net.local(up_m, up_all.at[z, y])
         keep_query = net.local(query_m, query_all.at[z, y])
         keep_query_y = net.local(query_y, query_all.at[z, 1 - y])
         keep_small_y = net.local(small_y, small_all.at[z, 1 - y])
-        keep_up_y = net.local(up_own.at[1 - y], up_all.at[z, 1 - y])
-        keep_down = [
-            net.local(down_m, down_all.at[z]),
-            net.local(down_1, down_all.at[before]),
-            net.local(down_2, down_all.at[before_2]),
-        ]
-        run_out = LineGather(net, spot, lambda at: out_all.at[at // group, at % group])
+        keep_out = net.local(out_v, out_all)
         run_kv = LineGather(net, spot, z_slot)
         run_query = LineGather(net, spot, lambda at: query_all.at[at])
         run_small = LineGather(net, spot, lambda at: small_all.at[at])
-        out_deal = DpExchange(net, spot, out_all, out_dealt)
-        for copy in reads:
-            copy.start()
+
+        def piece_of_out(piece):
+            rows_at = pl.ds(piece * kv_rows, kv_rows)
+            return LineGather(
+                net,
+                spot,
+                lambda at: out_v.at[at % group, rows_at],
+                lambda at: at // group == xc,
+            )
+
+        run_outs = [piece_of_out(piece) for piece in range(4)]
+        read_query_o.start()
+        pl.when(source)(read_out.start)
+        read_kv.start()
+        read_query.start()
         keep_small.start()
-        keep_up_mine.start()
-        spot.barrier((spot.to_c, spot.to_x, spot.to_y, spot.to_xc, *spot.ring()), False)
+        spot.barrier((spot.to_c, spot.to_x, spot.to_y, spot.to_xc), True)
+        pick_rows(send, tok_held, tok)
         tok_deal.start()
-        reads[0].wait()
+        read_query_o.wait()
         query_o[...] = low(query_f[0])
         y_query.start()
         y_small.start()
-        reads[2].wait()
-        out_all[z // group, z % group] = low(out_f[...])
-        run_out.start(0)
-        reads[3].wait()
+        y_up.start()
+
+        @pl.when(source)
+        def _():
+            read_out.wait()
+
+            @pl.loop(0, rows_own // 16)
+            def _(index):
+                at = pl.ds(pl.multiple_of(index * 16, 16), 16)
+                out_v[z % group, at, :] = low(out_f[at, :])
+
+        for run in run_outs:
+            run.start(0)
+        read_kv.wait()
         z_slot(z)[...] = low(kv_f[...])
         run_kv.start(0)
-        reads[4].wait()
+        read_query.wait()
         query_m[...] = low(query_f[1])
         keep_query.start()
-        reads[1].wait()
-
-        @pl.loop(0, seg // 16)
-        def _(index):
-            at = pl.ds(pl.multiple_of(index * 16, 16), 16)
-            down_m[at, :] = low(down_f[at, :])
-
         keep_query.wait()
         keep_small.wait()
         y_query.got()
@@ -641,9 +648,7 @@
         keep_small_y.wait()
         run_query.start(0)
         run_small.start(0)
-        y_up.start()
-        d_hops[0].start()
-        keep_down[0].start()
+        pick_rows(send, cot_held, cot)
 
         @pl.loop(0, rows_own // 16)
         def _(index):
@@ -654,51 +659,41 @@
         pick_rows(choose, tok_got, own_tok)
         tok_run.start()
         cot_deal.start()
-        run_out.hop(1)
-        run_kv.hop(1)
+        for step in range(1, depth - 1):
+            for run in run_outs:
+                run.hop(step)
+            run_kv.hop(step)
         run_query.hop(1)
         run_small.hop(1)
-        y_up.got()
-        keep_up_y.start()
+        run_kv.got(depth - 2)
+        kv_run.start()
+        for step in range(2, depth - 1):
+            run_query.hop(step)
+            run_small.hop(step)
+        tok_run.middle()
+        kv_run.middle()
         cot_deal.got()
         pick_rows(choose, cot_got, own_cot)
-        tok_run.middle()
-        cot_run.start()
-        d_hops[0].got()
-        d_hops[1].start()
-        keep_down[1].start()
-        for step in range(2, depth - 1):
-            run_out.hop(step)
-            run_kv.hop(step)
-            run_query.hop(step)
-            run_small.hop(step)
         tok_run.last()
-        run_out.got(depth - 2)
-        run_kv.got(depth - 2)
-        kv_run.start()
-        out_deal.start()
+        kv_run.last()
+        for run in run_outs:
+            run.got(depth - 2)
+        keep_out.start()
         run_query.got(depth - 2)
         run_small.got(depth - 2)
-        kv_run.middle()
-        cot_run.middle()
-        kv_run.last()
-        cot_run.last()
-        d_hops[1].got()
-        keep_down[2].start()
-        out_deal.got()
-        runs = (run_out, run_kv, run_query, run_small, tok_run, kv_run, cot_run)
-        for run in (*runs, tok_deal, cot_deal, out_deal):
+        y_up.got()
+        runs = (*run_outs, run_kv, run_query, run_small, tok_run, kv_run)
+        for run in (*runs, tok_deal, cot_deal):
             run.finish()
-        for copy in (y_query, y_small, y_up, *d_hops):
+        for copy in (y_query, y_small, y_up):
             copy.sent()
-        for copy in (keep_up_mine, keep_up_y, *keep_down):
-            copy.wait()
+        keep_out.wait()
 
     remotes = (
-        3 * DpExchange.remotes + 3 * PlaneGather.remotes + 5 + 4 * LineGather.remotes(depth)
+        2 * DpExchange.remotes + 2 * PlaneGather.remotes + 4 + 7 * LineGather.remotes(depth)
     )
     operands = (
-        tok_send, cot_send, chooser, query_weight, keyval_weight, output_weight, down_weight, small,
+        tokens, cotangent, sender, chooser, query_weight, keyval_weight, output_weight, small,
         up_mine, up_other,
     )
     wide_type = jnp.float32
@@ -708,37 +703,29 @@
             low_shape(rows, width),
             low_shape(rows, width),
             low_shape(2, *up_mine.shape),
-            low_shape(seg, width),
-            low_shape(8, rows, width),
             low_shape(8, rows, width),
             low_shape(depth, 2, rows_own, head_cols),
             low_shape(8, depth * kv_rows, kv_cols),
             low_shape(depth, 2, *small.shape),
-            low_shape(4, group, kv_rows, width),
-            low_shape(depth, 2, *up_mine.shape),
-            low_shape(depth, seg, width),
+            low_shape(group, rows_own, width),
         ],
-        in_specs=[IN_VMEM] * 3 + [ANY] * 4 + [IN_VMEM] * 3,
-        out_specs=[IN_VMEM] * 4 + [ANY] * 8,
+        in_specs=[IN_VMEM] * 4 + [ANY] * 3 + [IN_VMEM] * 3,
+        out_specs=[IN_VMEM] * 3 + [ANY] * 5,
         scratch_shapes=[
-            low_vmem(*tok_send.shape),
-            low_vmem(*tok_send.shape),
-            low_vmem(4, group, kv_rows, width),
+            *[low_vmem(*tokens.shape)] * 4,
+            low_vmem(group, rows_own, width),
             low_vmem(depth * kv_rows, kv_cols),
             low_vmem(rows_own, head_cols),
             low_vmem(rows_own, head_cols),
             low_vmem(rows_own, head_cols),
             low_vmem(*small.shape),
-            low_vmem(seg, width),
-            low_vmem(seg, width),
             pltpu.VMEM((2, rows_own, head_cols), wide_type),
-            pltpu.VMEM((kv_rows, width), wide_type),
+            pltpu.VMEM((rows_own, width), wide_type),
             pltpu.VMEM((kv_rows, kv_cols), wide_type),
-            pltpu.VMEM((seg, width), wide_type),
-            *net_scratch(remotes, 24),
+            *net_scratch(remotes, 20),
         ],
         compiler_params=comm_params(1),
-        cost_estimate=lasts(85, 1 << 20),
+        cost_estimate=lasts(75, 1 << 20),
     )(*operands)
 
 
@@ -754,7 +741,7 @@
     return decorate
 
 
-def feed_blocks(run, c, parts, block):
+def feed_blocks(run, c, parts, block, prepare=None):
     width = parts.shape[-1]
 
     def columns(body):
@@ -763,11 +750,17 @@
             body(pl.ds(pl.multiple_of(index * 512, 512), 512))
 
     def send(at, member):
+        if prepare is not None:
+            prepare(member)
+
         @columns
         def _(cols):
             parts[at, :, cols] = low(block(member, cols))
 
     def merge(member, at):
+        if prepare is not None:
+            prepare(member)
+
         @columns
         def _(cols):
             run.sums[at, :, cols] = low(wide(run.sums[at, :, cols]) + block(member, cols))
@@ -778,74 +771,311 @@
         run.first[key].start()
 
 
-def attention_out(depth, attended, w_output, own_tok, bias, gain, shift, up_piece):
+SCORE_SCALE = 1.0 / math.sqrt(HEAD)
+
+
+def stacked(values):
+    return jnp.concatenate([values[:, :HEAD], values[:, HEAD:]], axis=0)
+
+
+def unstacked(values):
+    half = values.shape[0] // 2
+    return jnp.concatenate([values[:half], values[half:]], axis=1)
+
+
+def softmax_of(query_2, keys, allowed):
+    scores = product_cols(query_2, keys) * SCORE_SCALE
+    scores = jnp.where(jnp.concatenate([allowed, allowed], axis=0) > 0.0, scores, -1e30)
+    exps = jnp.exp(scores - jnp.max(scores, axis=-1, keepdims=True))
+    return exps / jnp.sum(exps, axis=-1, keepdims=True)
+
+
+def attend(depth, tok_all, own_tok, own_cot, w_query, w_keyval, w_output, gain_a, shift_a, bias_q, bias_kv, allowed, bias, gain, shift, up_own, down_own, down_1):
     rows, width = own_tok.shape
-
-    def kernel(att, w_out, tok, bias_row, gain_row, shift_row, piece, middle, normed_all, hop_1, hop_2,
-               parts, normed, sums, diag, from_x, from_y, *sems):
+    total = 8 * rows
+    head_cols = w_query.shape[1]
+    micros = rows // PACK
+
+    def kernel(
+        tok_far, tok, cot, w_q, w_kv, w_out, gain_1, shift_1, b_q, b_kv, allow, bias_row, gain_row, shift_row,
+        up, down, down_b,
+        middle, normed_a, query, keyval, attended, normed_all, cot_all, up_all, down_all, down_2,
+        parts, normed, sums, diag, from_x, from_y, *sems,
+    ):
         spot = Spot(depth)
         net = Net(*sems)
+        z = spot.z
         run = PlaneScatter(net, spot, parts, sums, diag, from_x, from_y)
         gather = PlaneGather(net, spot, normed, normed_all)
+        cot_run = PlaneGather(net, spot, cot, cot_all, share=1)
         after, _ = spot.ring()
-        ups = [net.remote(piece, hop_1, after), net.remote(hop_1, hop_2, after)]
+
+        def behind(step):
+            return lax.rem(z + 2 * depth - step, depth)
+
+        keeps = [
+            net.local(up, up_all.at[z]),
+            net.local(down, down_all.at[z]),
+            net.local(down_b, down_all.at[behind(1)]),
+        ]
+        keep_2 = net.local(down_2, down_all.at[behind(2)])
+        ups = [net.remote(up, up_all.at[z], after, up_all.at[behind(1)])]
+        for step in range(2, depth):
+            at = up_all.at[behind(step - 1)]
+            ups.append(net.remote(at, at, after, up_all.at[behind(step)]))
+        down_hop = net.remote(down_b, down_2, after)
+
+        def one_member(member):
+            first = pl.multiple_of(member * rows, rows)
+
+            @pl.loop(0, rows // ROWS_STEP)
+            def _(index):
+                at = pl.multiple_of(index * ROWS_STEP, ROWS_STEP)
+                xhat, _ = normalize(wide(tok_far[member, pl.ds(at, ROWS_STEP), :]))
+                normed_a[pl.ds(first + at, ROWS_STEP), :] = low(xhat * gain_1[...] + shift_1[...])
+
+            rows_at = pl.ds(first, rows)
+            query[rows_at, :] = low(product(normed_a[rows_at, :], w_q[...]) + b_q[...])
+            keyval[rows_at, :] = low(product(normed_a[rows_at, :], w_kv[...]) + b_kv[...])
+
+            for index in range(micros):
+                at = pl.ds(pl.multiple_of(first + index * PACK, PACK), PACK)
+                pair = keyval[at, :]
+                probs = softmax_of(
+                    stacked(query[at, :]), pair[:, :HEAD], allow[member * micros + index]
+                )
+                attended[at, :] = low(unstacked(product(low(probs), pair[:, HEAD:])))
 
         def block(member, cols):
             rows_at = pl.ds(pl.multiple_of(member * rows, rows), rows)
-            return product(att[rows_at, :], w_out[:, cols])
-
+            return product(attended[rows_at, :], w_out[:, cols])
+
+        for copy in keeps:
+            copy.start()
         spot.barrier((spot.to_c, spot.to_x, spot.to_y, *spot.ring()), False)
         ups[0].start()
-        feed_blocks(run, spot.c, parts, block)
+        cot_run.start()
+        feed_blocks(run, spot.c, parts, block, one_member)
+        down_hop.start()
+        cot_run.middle()
         run.middle()
+        ups[0].got()
+        ups[1].start()
         run.last()
+        cot_run.last()
         run.finish(middle)
 
         @row_loop(rows)
         def _(at):
-            total = wide(tok[at, :]) + (middle[at, :] + bias_row[...])
-            middle[at, :] = total
-            xhat, _ = normalize(total)
+            total_rows = wide(tok[at, :]) + (middle[at, :] + bias_row[...])
+            middle[at, :] = total_rows
+            xhat, _ = normalize(total_rows)
             normed[at, :] = low(xhat * gain_row[...] + shift_row[...])
 
         gather.start()
-        ups[0].got()
-        ups[1].start()
+        down_hop.got()
+        keep_2.start()
+        for step in range(2, depth - 1):
+            ups[step - 1].got()
+            ups[step].start()
         gather.middle()
         gather.last()
         gather.finish()
-        ups[1].got()
-        for copy in ups:
+        cot_run.finish()
+        ups[-1].got()
+        for copy in (*ups, down_hop):
             copy.sent()
+        for copy in (*keeps, keep_2):
+            copy.wait()
 
     return pl.pallas_call(
         kernel,
         out_shape=[
             wide_shape(rows, width),
+            low_shape(total, width),
+            low_shape(total, head_cols),
+            low_shape(total, 2 * HEAD),
+            low_shape(total, head_cols),
             low_shape(8, rows, width),
-            low_shape(*up_piece.shape),
-            low_shape(*up_piece.shape),
+            low_shape(8, rows, width),
+            low_shape(depth, *up_own.shape),
+            low_shape(depth, *down_own.shape),
+            low_shape(*down_own.shape),
         ],
-        in_specs=[IN_VMEM] * 6 + [ANY],
-        out_specs=[IN_VMEM, ANY, ANY, ANY],
+        in_specs=[IN_VMEM] * 17,
+        out_specs=[IN_VMEM] * 5 + [ANY] * 4 + [IN_VMEM],
         scratch_shapes=[
             low_vmem(4, rows, width),
             low_vmem(rows, width),
             *PlaneScatter.buffers(rows, width),
-            *net_scratch(PlaneScatter.remotes + PlaneGather.remotes + 2, 1),
+            *net_scratch(PlaneScatter.remotes + 2 * PlaneGather.remotes + depth, 6),
         ],
         compiler_params=comm_params(3),
-        cost_estimate=lasts(60, 1 << 20),
-    )(attended, w_output, own_tok, bias, gain, shift, up_piece)
-
-
-def mlp_back(depth, grad_hidden, w_up, activated, w_down, middle, own_cot, gain, bias, d_down, d_up):
+        cost_estimate=lasts(90, 1 << 20),
+    )(
+        tok_all, own_tok, own_cot, w_query, w_keyval, w_output, gain_a, shift_a, bias_q, bias_kv,
+        allowed, bias, gain, shift, up_own, down_own, down_1,
+    )
+
+
+def attend_back(depth, branch_all, query, keyval, allowed, w_output, w_query, w_keyval, own_tok, grad_middle, gain, block, chooser, holder, d_out, up_sum, up_parts):
+    group = depth // 4
+    rows, width = own_tok.shape
+    total, head_cols = query.shape
+    micros = rows // PACK
+    slots = chooser.shape[0] // 4
+
+    def kernel(
+        branch, q_all, kv_all, allow, w_out, w_q, w_kv, tok, grad_mid, gain_row, block_own, choose, hold,
+        out, du, du_far,
+        grad_q, kv_rows_all, vec, block_res, grad_res, out_sum, du_sum,
+        parts, sums, diag, from_x, from_y, first, grad_low, block_send, grad_send, block_got, grad_got,
+        out_mix, out_lo, out_hi, du_term,
+        grad_kv, kv_sums, kv_diag, kv_from_x, kv_from_y, kv_wide, kv_own, *sems,
+    ):
+        spot = Spot(depth)
+        net = Net(*sems)
+        run = PlaneScatter(net, spot, parts, sums, diag, from_x, from_y)
+        z = spot.z
+        after, _ = spot.ring()
+        deal = DpExchange(net, spot, out, out_mix)
+
+        def mixed(at):
+            return out_mix.at[at // group, at % group]
+
+        def add2(into, other):
+            add_rows(into, other, 16)
+
+        kv_run = PlaneScatter(net, spot, grad_kv, kv_sums, kv_diag, kv_from_x, kv_from_y)
+        kv_gather = PlaneGather(net, spot, kv_own, kv_rows_all)
+        run_out = LineScatter(net, spot, mixed, out_lo, out_hi, add2)
+        up_hop = net.remote(du, du_sum, after)
+        up_term = net.local(du_far.at[z], du_term)
+        back_block = DpExchange(net, spot, block_send, block_got)
+        back_grad = DpExchange(net, spot, grad_send, grad_got)
+
+        def one_member(member):
+            begin = pl.multiple_of(member * rows, rows)
+            grad_att = low(product_cols(branch[member], w_out[...]))
+            for index in range(micros):
+                at = pl.ds(pl.multiple_of(begin + index * PACK, PACK), PACK)
+                pair = kv_all[at, :]
+                keys, vals = pair[:, :HEAD], pair[:, HEAD:]
+                q_2 = stacked(q_all[at, :])
+                g_2 = stacked(grad_att[index * PACK : (index + 1) * PACK])
+                probs = softmax_of(q_2, keys, allow[member * micros + index])
+                grad_probs = product_cols(g_2, vals)
+                inner = jnp.sum(probs * grad_probs, axis=-1, keepdims=True)
+                grad_scores = low(probs * (grad_probs - inner))
+                grad_q[at, :] = low(unstacked(product(grad_scores, keys) * SCORE_SCALE))
+                grad_k = product_rows(grad_scores, q_2) * SCORE_SCALE
+                grad_v = product_rows(low(probs), g_2)
+                grad_kv[member, index * PACK : (index + 1) * PACK, :] = low(
+                    jnp.concatenate([grad_k, grad_v], axis=1)
+                )
+
+        def block_of(member, cols):
+            rows_at = pl.ds(pl.multiple_of(member * rows, rows), rows)
+            return product_cols(grad_q[rows_at, :], w_q[cols, :]) + product_cols(
+                grad_kv[member], w_kv[cols, :]
+            )
+
+        up_term.start()
+        spot.barrier((spot.to_c, spot.to_x, spot.to_y, spot.to_xc, *spot.ring()), False)
+        deal.start()
+        up_hop.start()
+        pick_rows(choose, block_own, block_send)
+        back_block.start()
+        feed_blocks(run, spot.c, parts, block_of, one_member)
+        deal.got()
+        run_out.stage(0)
+        kv_run.start()
+        run.middle()
+        kv_run.middle()
+        for step in range(1, depth - 1):
+            run_out.stage(step)
+        run.last()
+        kv_run.last()
+        run.finish(first)
+        kv_run.finish(kv_wide)
+        kv_own[...] = low(kv_wide[...])
+        kv_gather.start()
+        vec[...] = jnp.zeros_like(vec)
+
+        @row_loop(rows)
+        def _(at):
+            xhat, scale = normalize(wide(tok[at, :]))
+            grad = grad_mid[at, :] + norm_back(first[at, :], gain_row[...], xhat, scale)
+            grad_low[at, :] = low(grad)
+            vec[0:1, :] += jnp.sum(first[at, :] * xhat, axis=0, keepdims=True)
+            vec[1:2, :] += jnp.sum(first[at, :], axis=0, keepdims=True)
+
+        pick_rows(choose, grad_low, grad_send)
+        back_grad.start()
+        kv_gather.middle()
+        run_out.total()
+        out_sum[...] = mixed(z)[...]
+        kv_gather.last()
+        back_block.got()
+        pick_rows(hold, block_got, block_res)
+        up_hop.got()
+        up_term.wait()
+        for at in range(2):
+            add_rows(du_sum.at[at], du_term.at[at], 32)
+        back_grad.got()
+        pick_rows(hold, grad_got, grad_res)
+        for run_done in (back_block, back_grad, deal, run_out):
+            run_done.finish()
+        kv_gather.finish()
+        up_hop.sent()
+
+    return pl.pallas_call(
+        kernel,
+        out_shape=[
+            low_shape(total, head_cols),
+            low_shape(8, rows, 2 * HEAD),
+            wide_shape(8, width),
+            low_shape(4, slots, width),
+            low_shape(4, slots, width),
+            low_shape(*d_out.shape[2:]),
+            low_shape(*up_sum.shape),
+        ],
+        in_specs=[IN_VMEM] * 15 + [ANY],
+        out_specs=[IN_VMEM, ANY] + [IN_VMEM] * 5,
+        scratch_shapes=[
+            low_vmem(4, rows, width),
+            *PlaneScatter.buffers(rows, width),
+            pltpu.VMEM((rows, width), jnp.float32),
+            low_vmem(rows, width),
+            *[low_vmem(4, slots, width)] * 4,
+            low_vmem(*d_out.shape),
+            *[low_vmem(depth - 1, *d_out.shape[2:])] * 2,
+            low_vmem(*up_sum.shape),
+            low_vmem(8, rows, 2 * HEAD),
+            *PlaneScatter.buffers(rows, 2 * HEAD),
+            pltpu.VMEM((rows, 2 * HEAD), jnp.float32),
+            low_vmem(rows, 2 * HEAD),
+            *net_scratch(
+                2 * PlaneScatter.remotes + PlaneGather.remotes + 3 * DpExchange.remotes + LineGather.remotes(depth) + 1, 6
+            ),
+        ],
+        compiler_params=comm_params(4),
+        cost_estimate=lasts(70, 1 << 20),
+    )(
+        branch_all, query, keyval, allowed, w_output, w_query, w_keyval, own_tok, grad_middle, gain,
+        block, chooser, holder, d_out, up_sum, up_parts,
+    )
+
+
+def mlp_back(depth, grad_hidden, w_up, activated, w_down, middle, own_cot, gain, bias, down_first, d_down, d_up):
     rows, width = own_cot.shape
-
-    def kernel(gh, up, act, down, mid, cot, gain_row, bias_row, dd, du,
-               grad_normed, grad_middle, branch_all, block_out, dd_sum, du_sum,
+    up_hops = min(2, depth - 1)
+
+    def kernel(gh, up, act_far, down_far, mid, cot, gain_row, bias_row, dd_first, dd, du,
+               vec, grad_middle, branch_all, block_out, dd_sum, du_sum, dd_x,
                parts, branch, sums, diag, from_x, from_y,
-               parts2, sums2, diag2, from_x2, from_y2, mlp_sum, dd_got, *sems):
+               parts2, sums2, diag2, from_x2, from_y2, mlp_sum, act, down,
+               dd_got, du_got, dd_term, du_term, grad_normed, *sems):
         spot = Spot(depth)
         net = Net(*sems)
         z = spot.z
@@ -857,19 +1087,43 @@
         def slot(step):
             return lax.rem(z + 2 * depth - 1 - step, depth)
 
-        def landing(step):
+        def down_at(step):
             return dd_sum if step == depth - 1 else dd_got.at[step - 1]
 
-        du_hop = net.remote(du.at[slot(0)], du_sum, after)
-        dd_hops = [net.remote(dd.at[slot(0)], landing(1), after)]
-        for step in range(1, depth - 1):
-            dd_hops.append(net.remote(landing(step), landing(step + 1), after))
-
-        def ring_step(step):
-            dd_hops[step - 1].got()
-            add_rows(landing(step), dd.at[slot(step)], 32)
+        def up_at(step):
+            return du_sum if step == up_hops else du_got.at[step - 1]
+
+        down_terms = [
+            net.local(dd.at[slot(step)], dd_term.at[step - 1]) for step in range(1, depth)
+        ]
+        up_terms = [
+            net.local(du.at[slot(step)], du_term.at[step - 1]) for step in range(1, up_hops + 1)
+        ]
+        loads = [net.local(act_far, act), net.local(down_far, down)]
+        down_hops = [
+            net.remote(down_at(step - 1), down_at(step), after) for step in range(2, depth)
+        ]
+        ups = [net.remote(du.at[slot(0)], up_at(1), after)]
+        ups += [net.remote(up_at(step - 1), up_at(step), after) for step in range(2, up_hops + 1)]
+
+        down_over = net.remote(dd_sum, dd_x, spot.to_x)
+
+        def down_step(step):
+            down_hops[step - 2].got()
+            down_terms[step - 1].wait()
+            add_rows(down_at(step), dd_term.at[step - 1], 32)
             if step < depth - 1:
-                dd_hops[step].start()
+                down_hops[step - 1].start()
+            else:
+                down_over.start()
+
+        def up_step(step):
+            ups[step - 1].got()
+            up_terms[step - 1].wait()
+            for at in range(2):
+                add_rows(up_at(step).at[at], du_term.at[step - 1, at], 32)
+            if step < up_hops:
+                ups[step].start()
 
         def block(member, cols):
             rows_at = pl.ds(pl.multiple_of(member * rows, rows), rows)
@@ -879,30 +1133,49 @@
             rows_at = pl.ds(pl.multiple_of(member * rows, rows), rows)
             return product(act[rows_at, :], down[:, cols])
 
+        for copy in (*down_terms, *up_terms, *loads):
+            copy.start()
         spot.barrier((spot.to_c, spot.to_x, spot.to_y, *spot.ring()), False)
-        dd_hops[0].start()
+        down_terms[0].wait()
+
+        @pl.loop(0, dd_first.shape[0] // 32)
+        def _(index):
+            at = pl.ds(pl.multiple_of(index * 32, 32), 32)
+            dd_got[0, at, :] = low(wide(dd_first[at, :]) + wide(dd_term[0, at, :]))
+
+        down_hops[0].start()
         feed_blocks(run, spot.c, parts, block)
         run.middle()
+        for copy in loads:
+            copy.wait()
         feed_blocks(run2, spot.c, parts2, block2)
         run.last()
-        ring_step(1)
+        down_step(2)
+        ups[0].start()
         run.finish(grad_normed)
+        vec[...] = jnp.zeros_like(vec)
 
         @row_loop(rows)
         def _(at):
             xhat, scale = normalize(mid[at, :])
-            grad = wide(cot[at, :]) + norm_back(grad_normed[at, :], gain_row[...], xhat, scale)
+            grad_n = grad_normed[at, :]
+            grad_o = wide(cot[at, :])
+            grad = grad_o + norm_back(grad_n, gain_row[...], xhat, scale)
+            grad_b = low(grad)
             grad_middle[at, :] = grad
-            branch[at, :] = low(grad)
+            branch[at, :] = grad_b
+            for row, values in enumerate((wide(grad_b), grad_n * xhat, grad_n, grad_o)):
+                vec[row : row + 1, :] += jnp.sum(values, axis=0, keepdims=True)
 
         gather.start()
-        for step in range(2, depth - 1):
-            ring_step(step)
+        for step in range(3, depth):
+            if step < depth - 1:
+                down_step(step)
         gather.middle()
         run2.middle()
         gather.last()
-        ring_step(depth - 1)
-        du_hop.start()
+        down_step(depth - 1)
+        up_step(1)
         run2.last()
         gather.finish()
         run2.finish(mlp_sum)
@@ -911,24 +1184,25 @@
         def _(at):
             block_out[at, :] = low(mid[at, :] + (mlp_sum[at, :] + bias_row[...]))
 
-        du_hop.got()
-        for at in range(2):
-            add_rows(du_sum.at[at], du.at[slot(1), at], 32)
-        for copy in (*dd_hops, du_hop):
+        for step in range(2, up_hops + 1):
+            up_step(step)
+        down_over.got()
+        for copy in (*down_hops, *ups, down_over):
             copy.sent()
 
     return pl.pallas_call(
         kernel,
         out_shape=[
-            wide_shape(rows, width),
+            wide_shape(8, width),
             wide_shape(rows, width),
             low_shape(8, rows, width),
             low_shape(rows, width),
             low_shape(*d_down.shape[1:]),
             low_shape(*d_up.shape[1:]),
+            low_shape(*d_down.shape[1:]),
         ],
-        in_specs=[IN_VMEM] * 10,
-        out_specs=[IN_VMEM, IN_VMEM, ANY, IN_VMEM, IN_VMEM, IN_VMEM],
+        in_specs=[IN_VMEM] * 2 + [ANY] * 2 + [IN_VMEM] * 5 + [ANY] * 2,
+        out_specs=[IN_VMEM, IN_VMEM, ANY, IN_VMEM, IN_VMEM, IN_VMEM, IN_VMEM],
         scratch_shapes=[
             low_vmem(4, rows, width),
             low_vmem(rows, width),
@@ -936,19 +1210,27 @@
             low_vmem(4, rows, width),
             *PlaneScatter.buffers(rows, width),
             pltpu.VMEM((rows, width), jnp.float32),
+            low_vmem(*activated.shape),
+            low_vmem(*w_down.shape),
             low_vmem(depth - 2, *d_down.shape[1:]),
-            *net_scratch(2 * PlaneScatter.remotes + PlaneGather.remotes + depth, 1),
+            low_vmem(max(up_hops - 1, 1), *d_up.shape[1:]),
+            low_vmem(depth - 1, *d_down.shape[1:]),
+            low_vmem(up_hops, *d_up.shape[1:]),
+            pltpu.VMEM((rows, width), jnp.float32),
+            *net_scratch(
+                2 * PlaneScatter.remotes + PlaneGather.remotes + depth + up_hops + 1,
+                depth + up_hops + 3,
+            ),
         ],
         compiler_params=comm_params(5),
         cost_estimate=lasts(95, 1 << 20),
-    )(grad_hidden, w_up, activated, w_down, middle, own_cot, gain, bias, d_down, d_up)
-
-
-def closing(depth, up_own, down_own, down_x, d_query, d_keyval, d_vec, d_out, grad_parts, own_tok, grad_middle, gain, block, chooser):
-    rows, width = grad_parts.shape[1:]
-    kv_rows, kv_cols = d_keyval.shape[1] // depth, d_keyval.shape[2]
-    group = depth // 4
-    slots = chooser.shape[0] // 4
+    )(
+        grad_hidden, w_up, activated, w_down, middle, own_cot, gain, bias, down_first, d_down, d_up
+    )
+
+
+def closing(depth, up_own, down_own, down_x, d_query, d_keyval, d_vec, out_own):
+    kv_rows, kv_cols = d_keyval.shape[0] // depth, d_keyval.shape[1]
 
     def add2(into, other):
         add_rows(into, other, 16)
@@ -958,35 +1240,31 @@
             add_rows(into.at[at], other.at[at], 16)
 
     def kernel(
-        up, down, down_x_in, query, kv, vec, out, parts, tok, grad_mid, gain_row, block_own, choose,
-        up_all, down_all, query_all, kv_all, vec_all, out_all, block_got, grad_got,
-        query_lo, query_hi, kv_lo, kv_hi, vec_lo, vec_hi, out_lo, out_hi,
-        out_mix, up_got, query_got, vec_got, first, grad_low, block_send, grad_send, kv_line, kv_wide,
-        sums, diag, from_x, from_y, kv_sums, kv_diag, kv_from_x, kv_from_y, *sems,
+        up, down, down_x_in, query, kv, vec, out,
+        up_all, down_all, query_all, kv_all, vec_all, out_all,
+        query_lo, query_hi, kv_lo, kv_hi, vec_lo, vec_hi,
+        up_got, query_got, vec_got, *sems,
     ):
         spot = Spot(depth)
         net = Net(*sems)
         z, y = spot.z, spot.y
-        deal = DpExchange(net, spot, out, out_mix)
-
-        def mixed(at):
-            return out_mix.at[at // group, at % group]
-
+        xc, on_x = spot.x * 2 + spot.c, (1 - spot.x) * 2 + spot.c
         def kv_part(at):
-            return kv_line.at[pl.ds(pl.multiple_of(at * kv_rows, kv_rows), kv_rows)]
+            return kv.at[pl.ds(pl.multiple_of(at * kv_rows, kv_rows), kv_rows)]
 
         run_query = LineScatter(net, spot, lambda at: query.at[at], query_lo, query_hi, add3)
         run_kv = LineScatter(net, spot, kv_part, kv_lo, kv_hi, add2)
         run_vec = LineScatter(net, spot, lambda at: vec.at[at], vec_lo, vec_hi, add3)
-        run_out = LineScatter(net, spot, mixed, out_lo, out_hi, add2)
-        plane = PlaneScatter(net, spot, parts, sums, diag, from_x, from_y)
-        kv_plane = PlaneScatter(net, spot, kv, kv_sums, kv_diag, kv_from_x, kv_from_y)
         y_up = net.remote(up.at[1 - y], up_got, spot.to_y)
         y_query = net.remote(query.at[z, 1 - y], query_got, spot.to_y)
         y_vec = net.remote(vec.at[z, 1 - y], vec_got, spot.to_y)
         dp_up = DpGather(net, spot, up.at[y], up_all.at[y])
         dp_up2 = DpGather(net, spot, up_got, up_all.at[1 - y])
-        xc, on_x = spot.x * 2 + spot.c, (1 - spot.x) * 2 + spot.c
+        dp_query = DpGather(net, spot, query.at[z, y], query_all.at[y])
+        dp_query2 = DpGather(net, spot, query_got, query_all.at[1 - y])
+        dp_kv = DpGather(net, spot, kv_part(z), kv_all)
+        dp_vec = DpGather(net, spot, vec.at[z, y], vec_all)
+        dp_out = DpGather(net, spot, out, out_all)
         keep_down = [
             net.local(down, down_all.at[xc]),
             net.local(down_x_in, down_all.at[on_x]),
@@ -1000,95 +1278,56 @@
                 down_all.at[(1 - spot.x) * 2 + 1 - spot.c],
             ),
         ]
-        dp_query = DpGather(net, spot, query.at[z, y], query_all.at[y])
-        dp_query2 = DpGather(net, spot, query_got, query_all.at[1 - y])
-        dp_kv = DpGather(net, spot, kv_part(z), kv_all)
-        dp_vec = DpGather(net, spot, vec.at[z, y], vec_all)
-        dp_out = DpGather(net, spot, mixed(z), out_all)
-        back_block = DpExchange(net, spot, block_send, block_got)
-        back_grad = DpExchange(net, spot, grad_send, grad_got)
-        spot.barrier((spot.to_c, spot.to_x, spot.to_y, spot.to_xc), True)
-        plane.start()
-        kv_plane.start()
+        spot.barrier((spot.to_c, spot.to_x, spot.to_y), True)
         run_query.stage(0)
-        deal.start()
+        run_vec.stage(0)
+        run_kv.stage(0)
         y_up.start()
-        kv_plane.middle()
-        plane.middle()
-        kv_plane.last()
-        deal.got()
-        run_out.stage(0)
-        run_query.stage(1)
-        kv_plane.finish(kv_wide)
-        kv_line[...] = low(kv_wide[...])
-        run_kv.stage(0)
-        run_vec.stage(0)
-        pick_rows(choose, block_own, block_send)
-        plane.last()
-        run_out.stage(1)
-        run_kv.stage(1)
-        run_vec.stage(1)
+        dp_up.start()
+        dp_out.start()
         for copy in (*down_moves, *keep_down):
             copy.start()
-        plane.finish(first)
-
-        @row_loop(rows)
-        def _(at):
-            xhat, scale = normalize(wide(tok[at, :]))
-            grad = grad_mid[at, :] + norm_back(first[at, :], gain_row[...], xhat, scale)
-            grad_low[at, :] = low(grad)
-
-        pick_rows(choose, grad_low, grad_send)
-        back_grad.start()
-        for step in range(2, depth - 1):
+        for step in range(1, depth - 1):
             run_query.stage(step)
-            run_out.stage(step)
+            run_vec.stage(step)
             run_kv.stage(step)
-            run_vec.stage(step)
-        y_up.got()
-        dp_up.start()
-        dp_up2.start()
+            if step == 1:
+                y_up.got()
+                dp_up2.start()
         run_query.total()
         y_query.start()
         dp_query.start()
-        run_out.total()
-        dp_out.start()
+        run_vec.total()
+        y_vec.start()
         run_kv.total()
         dp_kv.start()
-        run_vec.total()
-        y_vec.start()
-        back_block.start()
         dp_up.last()
-        dp_up2.last()
         y_query.got()
         dp_query2.start()
         y_vec.got()
         y_vec.sent()
         add_rows(vec.at[z, y], vec_got, 16)
         dp_vec.start()
+        dp_up2.last()
         dps = (dp_query, dp_out, dp_kv, dp_query2, dp_vec)
         for run in dps:
             run.last()
-        back_grad.got()
-        back_block.got()
-        for run in (dp_up, dp_up2, *dps, back_grad, back_block):
+        for run in (dp_up, dp_up2, *dps):
             run.finish()
         for copy in down_moves:
             copy.got()
             copy.sent()
         for copy in keep_down:
             copy.wait()
-        for run in (run_query, run_kv, run_vec, run_out, deal):
+        for run in (run_query, run_kv, run_vec):
             run.finish()
         for copy in (y_up, y_query):
             copy.sent()
 
     remotes = (
-        3 * DpExchange.remotes
-        + 4 * LineGather.remotes(depth)
-        + 2 * PlaneScatter.remotes
-        + 3
-        + 8 * DpGather.remotes
+        3 * LineGather.remotes(depth)
+        + 5
+        + 7 * DpGather.remotes
     )
     one = depth - 1
 
@@ -1103,64 +1342,71 @@
             low_shape(2, 4, *d_query.shape[2:]),
             low_shape(4, kv_rows, kv_cols),
             low_shape(4, *d_vec.shape[2:]),
-            low_shape(4, *d_out.shape[2:]),
-            low_shape(4, slots, width),
-            low_shape(4, slots, width),
+            low_shape(4, *out_own.shape),
         ],
-        in_specs=[IN_VMEM] * 13,
-        out_specs=[ANY] * 8,
+        in_specs=[IN_VMEM] * 7,
+        out_specs=[ANY] * 6,
         scratch_shapes=[
             *twice(one, *d_query.shape[1:]),
             *twice(one, kv_rows, kv_cols),
             *twice(one, *d_vec.shape[1:]),
-            *twice(one, *d_out.shape[2:]),
-            low_vmem(*d_out.shape),
             low_vmem(*up_own.shape[1:]),
             low_vmem(*d_query.shape[2:]),
             low_vmem(*d_vec.shape[2:]),
-            pltpu.VMEM((rows, width), jnp.float32),
-            low_vmem(rows, width),
-            low_vmem(4, slots, width),
-            low_vmem(4, slots, width),
-            low_vmem(depth * kv_rows, kv_cols),
-            pltpu.VMEM((depth * kv_rows, kv_cols), jnp.float32),
-            *PlaneScatter.buffers(rows, width),
-            *PlaneScatter.buffers(depth * kv_rows, kv_cols),
-            *net_scratch(remotes, 12),
+            *net_scratch(remotes, 10),
         ],
         compiler_params=comm_params(2),
-        cost_estimate=lasts(90, 1 << 20),
-    )(
-        up_own, down_own, down_x, d_query, d_keyval, d_vec, d_out, grad_parts, own_tok, grad_middle,
-        gain, block, chooser,
-    )
-
-
-def spread_columns(blocks, depth, seg, y_slow):
-    rows = blocks.shape[2]
-    wide_seg = seg % 128 == 0
-    if not wide_seg:
-        parts = blocks.reshape(2, 4, rows, depth, seg)
-        order = (2, 0, 3, 1, 4) if y_slow else (2, 3, 0, 1, 4)
-        return wide(jnp.transpose(parts, order).reshape(rows, 8 * depth * seg))
-
-    step = 32
-
-    def kernel(block, out):
+        cost_estimate=lasts(70, 1 << 20),
+    )(up_own, down_own, down_x, d_query, d_keyval, d_vec, out_own)
+
+
+def widen(depth, y_slow, up_all, query_all, down_all, out_all, kv_all):
+    rows = up_all.shape[2]
+    seg = up_all.shape[3] // depth
+    head_cols = query_all.shape[3]
+    down_rows, width = down_all.shape
+    steps = rows // 16
+
+    def kernel(up, query, down, out, kv, up_w, query_w, down_w, out_w, kv_w):
         for y in range(2):
-            for z in range(depth):
-                for xc in range(4):
+            for xc in range(4):
+                for z in range(depth):
                     owner = y * depth + z if y_slow else z * 2 + y
                     at = (owner * 4 + xc) * seg
-                    out[:, at : at + seg] = wide(block[y, xc, :, z * seg : (z + 1) * seg])
-
+                    up_w[:, at : at + seg] = wide(up[y, xc, :, z * seg : (z + 1) * seg])
+                at = (y * 4 + xc if y_slow else xc * 2 + y) * head_cols
+                query_w[:, at : at + head_cols] = wide(query[y, xc])
+        down_w[...] = wide(down[...])
+        out_w[...] = wide(out[...])
+        kv_w[...] = wide(kv[...])
+
+    def rows_of(array):
+        return pl.BlockSpec((array.shape[0] // steps, array.shape[1]), lambda index: (index, 0))
+
+    def blocks_of(array):
+        return pl.BlockSpec((2, 4, 16, array.shape[3]), lambda index: (0, 0, index, 0))
+
+    shapes = [
+        wide_shape(rows, 8 * depth * seg),
+        wide_shape(rows, width),
+        wide_shape(down_rows, width),
+        wide_shape(*out_all.shape),
+        wide_shape(*kv_all.shape),
+    ]
     return pl.pallas_call(
         kernel,
-        grid=(rows // step,),
-        in_specs=[pl.BlockSpec((2, 4, step, depth * seg), lambda index: (0, 0, index, 0))],
-        out_specs=pl.BlockSpec((step, 8 * depth * seg), lambda index: (index, 0)),
-        out_shape=jax.ShapeDtypeStruct((rows, 8 * depth * seg), jnp.float32),
-    )(blocks)
+        grid=(steps,),
+        in_specs=[
+            blocks_of(up_all),
+            blocks_of(query_all),
+            rows_of(down_all),
+            rows_of(out_all),
+            rows_of(kv_all),
+        ],
+        out_specs=[rows_of(item) for item in shapes],
+        out_shape=shapes,
+        compiler_params=pltpu.CompilerParams(vmem_limit_bytes=VMEM_LIMIT),
+    )(up_all, query_all, down_all, out_all, kv_all)
 
 
 def build(mesh):
@@ -1276,58 +1522,47 @@
         small = low(lax.optimization_barrier(jnp.concatenate(small_parts)))
         small_count = small.shape[0]
         small = jnp.pad(small, (0, 16 * 256 - small_count)).reshape(16, 256)
-        def dealt(array):
-            return jnp.stack(
-                [
-                    lax.dynamic_index_in_dim(array, slot_for[index], 0, keepdims=False)
-                    for index in range(4)
-                ]
+        down_own = low(lax.dynamic_slice_in_dim(down_weight, my_xc * ff_seg, ff_seg, axis=0))
+        ring = [(index, (index + 1) % depth) for index in range(depth)]
+
+        def ring_slot(buffer, piece, step):
+            at = (my_z - step + depth) % depth
+            return lax.dynamic_update_slice(
+                buffer, piece[None], (at,) + (0,) * piece.ndim
             )
 
+        down_hop_1 = lax.ppermute(down_own, "z", ring)
         flat = held * slot_len
+        places = jnp.arange(flat)
+        from_slot = jnp.repeat(slot_for, slot_len) * slot_len + places % slot_len
+        sender = low(from_slot[:, None] == places[None, :])
+        holder = low(places[:, None] == from_slot[None, :])
         chooser = low((source_row[:, None] == jnp.arange(flat)[None, :]) & own_valid)
         (
             own_low,
             own_cot,
             up_piece,
-            down_piece,
             tokens_all,
-            cotangent_all,
             query_all,
             keyval_all,
             small_all,
-            out_dealt,
-            up_all,
-            down_all,
+            w_output,
         ) = opening(
             depth,
             owner,
-            dealt(tokens),
-            dealt(cotangent),
+            tokens,
+            cotangent,
+            sender,
             chooser,
             query_weight,
             keyval_weight,
             output_weight,
-            down_weight,
             small,
             up_columns(my_y),
             up_columns(1 - my_y),
         )
-
-        ring = [(index, (index + 1) % depth) for index in range(depth)]
-
-        def ring_slot(buffer, piece, step):
-            at = (my_z - step + depth) % depth
-            return lax.dynamic_update_slice(
-                buffer, piece[None], (at,) + (0,) * piece.ndim
-            )
-
-        for step in range(3, depth):
-            down_piece = lax.ppermute(down_piece, "z", ring)
-            down_all = ring_slot(down_all, down_piece, step)
-        for step in range(1, depth - 2):
-            up_piece = lax.ppermute(up_piece, "z", ring)
-            up_all = ring_slot(up_all, up_piece, step)
+        w_output = w_output.reshape(head_cols, width)
+
         if y_slow:
             small_all = jnp.transpose(small_all, (1, 0, 2, 3))
         gathered_small = wide(small_all.reshape(fsdp_size, 16 * 256)[:, :small_count])
@@ -1374,58 +1609,59 @@
         keyval_all = keyval_all.reshape(2, 4, depth, out_seg, 2 * HEAD)
         order = (0, 2, 1, 3, 4) if y_slow else (2, 0, 1, 3, 4)
         w_keyval = jnp.transpose(keyval_all, order).reshape(width, 2 * HEAD)
-        w_output = jnp.transpose(out_dealt, (1, 0, 2, 3)).reshape(head_cols, width)
-
-        packed = tokens_all.reshape(micro * PACK, width)
-        grad_mixed = cotangent_all.reshape(micro * PACK, width)
-        own_grad = wide(own_cot)
-
-        xhat_all, _ = normalize(wide(packed))
-        normed_attn = low(xhat_all * gain_a + shift_a)
-        query = low(product(normed_attn, w_query) + my_bias_q)
-        keyval = low(product(normed_attn, w_keyval) + bias_kv)
-        my_heads = head_cols // HEAD
-        query_h = query.reshape(micro, PACK, my_heads, HEAD)
-        keys = keyval[:, :HEAD].reshape(micro, PACK, HEAD)
-        vals = keyval[:, HEAD:].reshape(micro, PACK, HEAD)
-        score_scale = 1.0 / math.sqrt(HEAD)
-        scores = (
-            jnp.einsum("mshd,mtd->mhst", query_h, keys, preferred_element_type=jnp.float32)
-            * score_scale
-        )
-        scores = jnp.where(allowed[:, None], scores, -1e30)
-        expscores = jnp.exp(scores - jnp.max(scores, axis=-1, keepdims=True))
-        probs = expscores / jnp.sum(expscores, axis=-1, keepdims=True)
-        attended = low(
-            jnp.einsum(
-                "mhst,mtd->mshd", low(probs), vals, preferred_element_type=jnp.float32
-            ).reshape(micro * PACK, head_cols)
-        )
-        attended, down_piece = lax.optimization_barrier((attended, down_piece))
-        middle, normed_mlp, up_hop_1, up_hop_2 = attention_out(
+        (
+            middle,
+            normed_attn,
+            query,
+            keyval,
+            attended,
+            normed_mlp,
+            cotangent_all,
+            up_all,
+            down_all,
+            down_piece,
+        ) = attend(
             depth,
-            attended,
+            tokens_all,
+            own_low,
+            own_cot,
+            w_query,
+            w_keyval,
             w_output,
-            own_low,
+            gain_a[None],
+            shift_a[None],
+            my_bias_q[None],
+            bias_kv[None],
+            wide(allowed),
             bias_o[None],
             gain_m[None],
             shift_m[None],
             up_piece,
-        )
-        up_all = ring_slot(up_all, up_hop_1, depth - 2)
-        up_all = ring_slot(up_all, up_hop_2, depth - 1)
+            down_own,
+            down_hop_1,
+        )
         normed_mlp = normed_mlp.reshape(micro * PACK, width)
-        w_down = down_all.reshape(depth * ff_seg, width)
-        grad_act = product_cols(grad_mixed, w_down)
+        grad_mixed = cotangent_all.reshape(micro * PACK, width)
+        for step in range(3, depth):
+            down_piece = lax.ppermute(down_piece, "z", ring)
+            down_all = ring_slot(down_all, down_piece, step)
         w_up = rows_in_order(up_all)
         hidden = product(normed_mlp, w_up) + my_bias_u
         activated, slope = gelu_parts(hidden)
         activated = low(activated)
+
+        down_parts = low(product_rows(activated, grad_mixed)).reshape(depth, ff_seg, width)
+        down_first = lax.ppermute(
+            lax.dynamic_index_in_dim(down_parts, (my_z + depth - 1) % depth, 0, keepdims=False),
+            "z",
+            ring,
+        )
+        mixed_later, down_parts = lax.optimization_barrier((grad_mixed, down_parts))
+        w_down = down_all.reshape(depth * ff_seg, width)
+        grad_act = product_cols(mixed_later, w_down)
         grad_hidden = low(slope * grad_act)
-
-        down_parts = low(product_rows(activated, grad_mixed)).reshape(depth, ff_seg, width)
         up_parts = rows_by_z(low(product_rows(normed_mlp, grad_hidden)))
-        grad_normed, grad_middle, grad_branch, block_own, d_down, d_up = mlp_back(
+        second_sums, grad_middle, grad_branch, block_own, d_down, d_up, down_x = mlp_back(
             depth,
             grad_hidden,
             w_up,
@@ -1435,41 +1671,52 @@
             own_cot,
             gain_m[None],
             bias_d[None],
+            down_first,
             down_parts,
             up_parts,
         )
-        grad_branch = grad_branch.reshape(micro * PACK, width)
-        down_x = lax.ppermute(d_down, "x", [(0, 1), (1, 0)])
-        for step in range(2, depth):
+        grad_flat = grad_branch.reshape(micro * PACK, width)
+        for step in range(3, depth - 1):
             d_up = lax.ppermute(d_up, "z", ring)
             at = (my_z - 1 - step + 2 * depth) % depth
             term = lax.dynamic_index_in_dim(up_parts, at, 0, keepdims=False)
             d_up = low(wide(d_up) + wide(term))
-        xhat_m, _ = normalize(middle)
-        grad_branch_own = low(grad_middle)
-        d_output = low(product_rows(attended, grad_branch))
-        grad_att = low(product_cols(grad_branch, w_output)).reshape(micro, PACK, my_heads, HEAD)
-        grad_probs = jnp.einsum("mshd,mtd->mhst", grad_att, vals, preferred_element_type=jnp.float32)
-        grad_vals = jnp.einsum(
-            "mhst,mshd->mtd", low(probs), grad_att, preferred_element_type=jnp.float32
-        )
-        inner = jnp.sum(probs * grad_probs, axis=-1, keepdims=True)
-        grad_scores = low(probs * (grad_probs - inner))
-        grad_query = (
-            jnp.einsum("mhst,mtd->mshd", grad_scores, keys, preferred_element_type=jnp.float32)
-            * score_scale
-        )
-        grad_query = low(grad_query.reshape(micro * PACK, head_cols))
-        grad_keys = (
-            jnp.einsum("mhst,mshd->mtd", grad_scores, query_h, preferred_element_type=jnp.float32)
-            * score_scale
-        )
-        grad_keyval = low(jnp.concatenate([grad_keys, grad_vals], axis=2)).reshape(
-            micro * PACK, 2 * HEAD
+        d_output = low(product_rows(attended, grad_flat))
+        hits = my_holders[None, :] == jnp.arange(4)[:, None]
+        seq_starts = (my_starts + jnp.arange(MB)[:, None] * PACK).reshape(held)
+        send_lens = jnp.sum(jnp.where(hits, my_lens[None, :], 0), axis=1)
+        send_starts = jnp.sum(jnp.where(hits, seq_starts[None, :], 0), axis=1)
+        pos = jnp.arange(slot_len)
+        live = pos[None, :] < send_lens[:, None]
+        send_rows = jnp.where(live, send_starts[:, None] + pos[None, :], -1)
+        back_chooser = low(send_rows.reshape(flat)[:, None] == jnp.arange(own_count)[None, :])
+        d_out_parts = jnp.transpose(
+            d_output.reshape(depth // 4, 4, out_seg, width), (1, 0, 2, 3)
+        )
+        grad_query, grad_keyval, first_sums, block_out, input_grad, out_own, d_up = attend_back(
+            depth,
+            grad_branch,
+            query,
+            keyval,
+            wide(allowed),
+            w_output,
+            w_query,
+            w_keyval,
+            own_low,
+            grad_middle,
+            gain_a[None],
+            block_own,
+            back_chooser,
+            holder,
+            d_out_parts,
+            d_up,
+            up_parts,
         )
         d_query = low(product_rows(normed_attn, grad_query))
+        grad_keyval = grad_keyval.reshape(micro * PACK, 2 * HEAD)
         d_keyval = low(product_rows(normed_attn, grad_keyval))
-        grad_input_part = product_cols(grad_query, w_query) + product_cols(grad_keyval, w_keyval)
+        own_keyval = lax.dynamic_slice_in_dim(grad_keyval, member * own_count, own_count)
+
         def colsum(values):
             return jnp.sum(wide(values), axis=0)
 
@@ -1489,15 +1736,15 @@
             ff,
         )
         vectors = [
-            jnp.sum(grad_input_part * xhat_all, axis=0),
-            jnp.sum(grad_input_part, axis=0),
-            colsum(grad_branch_own),
-            jnp.sum(grad_normed * xhat_m, axis=0),
-            jnp.sum(grad_normed, axis=0),
-            jnp.sum(own_grad, axis=0),
+            first_sums[0],
+            first_sums[1],
+            second_sums[0],
+            second_sums[1],
+            second_sums[2],
+            second_sums[3],
             vec_query,
             vec_up,
-            colsum(grad_keyval[:, HEAD:]),
+            colsum(own_keyval[:, HEAD:]),
         ]
         vectors = jnp.concatenate([item.reshape(fsdp_size, -1) for item in vectors], axis=1)
         vectors = jnp.pad(low(vectors), ((0, 0), (0, 16 * 256 - small_count)))
@@ -1506,58 +1753,26 @@
         else:
             d_vec = vectors.reshape(depth, 2, 16, 256)
 
-        d_out_parts = jnp.transpose(
-            d_output.reshape(depth // 4, 4, out_seg, width), (1, 0, 2, 3)
-        )
         if y_slow:
             d_keyval = d_keyval.reshape(2, depth, 4, out_seg, 2 * HEAD)
-            d_keyval = jnp.transpose(d_keyval, (0, 2, 1, 3, 4))
+            d_keyval = lax.dynamic_index_in_dim(d_keyval, my_y, 0, keepdims=False)
         else:
             d_keyval = d_keyval.reshape(depth, 2, 4, out_seg, 2 * HEAD)
-            d_keyval = jnp.transpose(d_keyval, (1, 2, 0, 3, 4))
-        d_keyval = d_keyval.reshape(8, depth * out_seg, 2 * HEAD)
-
-        send_seq = jnp.argmax(my_holders[None, :] == jnp.arange(4)[:, None], axis=1)
-        pos = jnp.arange(slot_len)
-        live = pos[None, :] < my_lens[send_seq][:, None]
-        seq_starts = (my_starts + jnp.arange(MB)[:, None] * PACK).reshape(held)
-        send_rows = jnp.where(live, seq_starts[send_seq][:, None] + pos[None, :], -1)
-        back_chooser = low(send_rows.reshape(flat)[:, None] == jnp.arange(own_count)[None, :])
-        up_all, down_all, query_sum, kv_sum, vec_all, out_all, block_got, grad_got = closing(
+            d_keyval = lax.dynamic_index_in_dim(d_keyval, my_y, 1, keepdims=False)
+        d_keyval = lax.dynamic_index_in_dim(d_keyval, my_xc, 1, keepdims=False)
+        d_keyval = d_keyval.reshape(depth * out_seg, 2 * HEAD)
+        up_all, down_all, query_sum, kv_sum, vec_all, out_all = closing(
+            depth, d_up, d_down, down_x, rows_by_z(d_query), d_keyval, d_vec, out_own
+        )
+        up_grad, query_grad, down_grad, output_grad, keyval_grad = widen(
             depth,
-            d_up,
-            d_down,
-            down_x,
-            rows_by_z(d_query),
-            d_keyval,
-            d_vec,
-            d_out_parts,
-            low(grad_input_part).reshape(8, own_count, width),
-            own_low,
-            grad_middle,
-            gain_a[None],
-            block_own,
-            back_chooser,
-        )
-        from_dealt = jnp.argmax(slot_for[None, :] == jnp.arange(held)[:, None], axis=1)
-
-        def held_order(got):
-            return jnp.stack(
-                [
-                    lax.dynamic_index_in_dim(got, from_dealt[index], 0, keepdims=False)
-                    for index in range(held)
-                ]
-            )
-
-        up_grad = spread_columns(up_all, depth, ff_seg, y_slow)
-        if y_slow:
-            query_grad = jnp.transpose(query_sum, (2, 0, 1, 3))
-        else:
-            query_grad = jnp.transpose(query_sum, (2, 1, 0, 3))
-        query_grad = wide(query_grad.reshape(rows_own, width))
-        keyval_grad = wide(kv_sum.reshape(rows_own, 2 * HEAD))
-        down_grad = wide(down_all.reshape(ff_own, width))
-        output_grad = wide(out_all.reshape(rows_own, width))
+            y_slow,
+            up_all,
+            query_sum,
+            down_all.reshape(ff_own, width),
+            out_all.reshape(rows_own, width),
+            kv_sum.reshape(rows_own, 2 * HEAD),
+        )
         vec_own = jnp.sum(wide(vec_all), axis=0).reshape(16 * 256)
         (
             gain_a_grad,
@@ -1572,8 +1787,8 @@
         ) = [vec_own[start : start + size] for start, size in zip(begins, sizes)]
 
         return (
-            held_order(block_got),
-            held_order(grad_got),
+            block_out,
+            input_grad,
             gain_a_grad,
             shift_a_grad,
             query_grad,

time: 648 us -> 568 us (0.88)
  Pallas kernels: 420 us -> 462 us
  matrix products: 78.9 us -> 48.5 us
  other arithmetic: 36.1 us -> 8.94 us
  waiting for transfers between devices: 29.4 us -> 6.15 us
  local copies, waits for them, and re-layouts: 48.9 us -> 29.3 us
  between operations: 17.4 us -> 1.54 us
  starting transfers between devices: 13 us -> 2.95 us
    pallas_call x3 -> x4, Pallas kernels: 173 us -> 335 us  [the longest x1 110 us: mlp_back(): pl.pallas_call(kernel, out_shape=[wide_shape(8, width), wide_shape(rows,...]
    pallas_call x1, Pallas kernels: 143 us -> 66.6 us  [closing(): pl.pallas_call(kernel, out_shape=[low_shape(2, 4, *up_own.shape[1:]), low...]
    pallas_call x1, Pallas kernels: 104 us -> 61 us  [opening(): pl.pallas_call(kernel, out_shape=[low_shape(rows, width), low_shape(rows,...]
    ppermute x4 -> x2, waiting for transfers between devices: 29.4 us -> 0.73 us  [the longest x1 0.73 us: shards(): lax.ppermute(lax.dynamic_index_in_dim(down_parts, (my_z + depth - 1) % de...]
    dot_general x4 -> x1, matrix products: 27 us -> 10.2 us  [product_cols(): lax.dot_general(left_mat, right_mat, (((1,), (1,)), ((), ())), preferred_...]
    convert_element_type x5 -> x2, other arithmetic: 9.21 us -> 1.08 us  [wide(): return values.astype(jnp.float32)]
    ppermute x1, starting transfers between devices: 9.25 us -> 1.52 us  [shards(): down_piece = lax.ppermute(down_piece, 'z', ring)]
    dot_general x3 -> x1, matrix products: 17.7 us -> 10 us  [product(): return jnp.dot(left_mat, right_mat, preferred_element_type=jnp.float32)]
  transfers between devices with their start and end apart: 5 -> 3, of which waited for: 2 -> 2; matrix products, arithmetic and copies ran while one was open for 8% -> 11% of each run, Pallas kernels for 0% -> 11%
where the time goes in v3:
time: 568 us; the launch traced here: 560 us
  Pallas kernels  462 us (81%)
  matrix products  48.5 us (9%)
  local copies, waits for them, and re-layouts  29.3 us (5%)
  other arithmetic  8.94 us (2%)
  waiting for transfers between devices  6.15 us (1%)
    pallas_call x1, Pallas kernels, mlp_back(): pl.pallas_call(kernel, out_shape=[wide_shape(8, width), wide_shape(rows,...  110 us
    pallas_call x1, Pallas kernels, attend(): pl.pallas_call(kernel, out_shape=[wide_shape(rows, width), low_shape(tota...  108 us
    pallas_call x1, Pallas kernels, attend_back(): pl.pallas_call(kernel, out_shape=[low_shape(total, head_cols), low_shape(...  102 us
    pallas_call x1, Pallas kernels, closing(): pl.pallas_call(kernel, out_shape=[low_shape(2, 4, *up_own.shape[1:]), low...  66.6 us
    pallas_call x1, Pallas kernels, opening(): pl.pallas_call(kernel, out_shape=[low_shape(rows, width), low_shape(rows,...  61 us
    dot_general x5, matrix products, product_rows(): lax.dot_general(left_mat, right_mat, (((0,), (0,)), ((), ())), preferred_...  28.3 us
    unnamed x63, local copies, waits for them, and re-layouts  15.2 us
    pallas_call x1, Pallas kernels, widen(): pl.pallas_call(kernel, grid=(steps,), in_specs=[blocks_of(up_all), blocks...  15 us
  transfers between devices with their start and end apart: 3, of which 2 were waited for; matrix products, arithmetic and copies ran while one was open for 11% of the time, Pallas kernels for 11%

profile of v3, /device:TPU:9, one launch (start us, length us, event | category | flops | bytes accessed | tf_op | source)
XLA Modules:
  0.0 559.7 jit_solution(2773756585560244919)
XLA Ops:
  0.7 1.7 dynamic-slice_convert_fusion.down
  2.4 1.3 collective-permute-start
  15.4 1.6 dynamic-slice_convert_fusion.4
  17.1 1.1 pad_maximum_fusion
  18.2 61.0 %shard_map.297 = (bf16[160,2048]{1,0:T(8,128)(2,1)}, bf16[160,2048]{1,0:T(8,128)(2,1)}, bf16[2,256,1024]{2,1,0:T(8,128)(2,1)}, bf16[8,160,2048]{2,1,0:T(8,128)(2...) custom-call(bf16[4,64,2048]{2,1,0:T(8,128)(2,1)} %tok_held.1, ...), custom_call_target="tpu_custom_call" | custom-call | flops 74999996416 | bytes 1048576 | tf_op jit(solution)/shard_map/pallas_call | solution.py:700
  80.3 2.3 copy.51
  88.5 1.1 and_convert_fusion.allow
  90.5 107.9 %shard_map.298 = (f32[160,2048]{1,0:T(8,128)}, bf16[1280,2048]{1,0:T(8,128)(2,1)}, bf16[1280,256]{1,0:T(8,128)(2,1)}, bf16[1280,256]{1,0:T(8,128)(2,1)}, bf16[12...) custom-call(bf16[8,160,2048]{2,1,0:T(8,128)(2,1)} %get-tuple-element, ...), custom_call_target="tpu_custom_call" | custom-call | flops 89999998976 | bytes 1048576 | tf_op jit(solution)/shard_map/pallas_call | solution.py:891
  198.4 1.5 collective-permute-start.1
  199.9 10.0 %multiply_convert_fusion = (bf16[1280,1024]{1,0:T(8,128)(2,1)S(1)}, f32[1280,1024]{1,0:T(8,128)S(1)}) fusion(f32[1024]{0:T(1024)S(1)} %pad_maximum_fusion.2, bf16[1280,2048]{1,0:T(8,128)(2,1)} %bitcast.139, bf16[2048,1024]{1,0:T(8,128)(2,1)} %bitcast.144), kind=kOutput, calls=%fused_computation.10 | convolution fusion | flops 5381816320 | bytes 17305600 | tf_op jit(solution)/shard_map/dot_general | solution.py:33
  210.0 6.0 %convolution_convert_fusion.1 = bf16[1024,2048]{1,0:T(8,128)(2,1)S(1)} fusion(bf16[1280,1024]{1,0:T(8,128)(2,1)S(1)} %get-tuple-element.158.act_far, bf16[1280,2048]{1,0:T(8,128)(2,1)S(1)} %bitcast.141), kind=kOutput, calls=%fused_computation.12 | convolution fusion | flops 5370806272 | bytes 12058624 | tf_op jit(solution)/shard_map/dot_general | solution.py:37
  216.3 5.4 collective-permute-done.1
  221.8 10.2 %convert_reduce_fusion = (f32[1024]{0:T(1024)S(1)}, bf16[1280,1024]{1,0:T(8,128)(2,1)}) fusion(bf16[1280,2048]{1,0:T(8,128)(2,1)S(1)} %bitcast.142, bf16[1024,2048]{1,0:T(8,128)(2,1)S(1)} %bitcast.137, f32[1280,1024]{1,0:T(8,128)S(1)} %get-tuple-element.159, f32[1024]{0:T(1024)S(1)} %pad_maximum_fusion.2), kind=kOutput, calls=%fused_computation.9 | convolution fusion | flops 5397543936 | bytes 17309696 | tf_op jit(solution)/shard_map/dot_general | solution.py:43
  233.2 10.2 %convolution_convert_fusion = bf16[2048,1024]{1,0:T(8,128)(2,1)} fusion(bf16[1280,2048]{1,0:T(8,128)(2,1)} %bitcast.140, bf16[1280,1024]{1,0:T(8,128)(2,1)} %get-tuple-element.161.gh), kind=kOutput, calls=%fused_computation.11 | convolution fusion | flops 5370806272 | bytes 12058624 | tf_op jit(solution)/shard_map/dot_general | solution.py:37
  245.1 109.9 %shard_map.299 = (f32[8,2048]{1,0:T(8,128)}, f32[160,2048]{1,0:T(8,128)}, bf16[8,160,2048]{2,1,0:T(8,128)(2,1)}, bf16[160,2048]{1,0:T(8,128)(2,1)}, bf16[256,204...) custom-call(bf16[1280,1024]{1,0:T(8,128)(2,1)} %get-tuple-element.161.gh, ...), custom_call_target="tpu_custom_call" | custom-call | flops 95000002560 | bytes 1048576 | tf_op jit(solution)/shard_map/pallas_call | solution.py:1193
  355.0 5.0 convolution_convert_fusion.4
  360.0 101.9 %shard_map.300 = (bf16[1280,256]{1,0:T(8,128)(2,1)}, bf16[8,160,256]{2,1,0:T(8,128)(2,1)}, f32[8,2048]{1,0:T(8,128)}, bf16[4,64,2048]{2,1,0:T(8,128)(2,1)}, bf16...) custom-call(bf16[8,160,2048]{2,1,0:T(8,128)(2,1)} %get-tuple-element.77.branch, ...), custom_call_target="tpu_custom_call" | custom-call | flops 70000001024 | bytes 1048576 | tf_op jit(solution)/shard_map/pallas_call | solution.py:1032
  463.1 1.3 convert_reduce_fusion.1
  464.6 5.4 convolution_convert_fusion.3
  470.0 1.7 convolution_convert_fusion.2
  473.2 66.6 %shard_map.301 = (bf16[2,4,256,1024]{3,2,1,0:T(8,128)(2,1)}, bf16[4,256,2048]{2,1,0:T(8,128)(2,1)}, bf16[2,4,256,256]{3,2,1,0:T(8,128)(2,1)}, bf16[4,64,256]{2,1...) custom-call(bf16[2,256,1024]{2,1,0:T(8,128)(2,1)} %get-tuple-element.86.up, ...), custom_call_target="tpu_custom_call" | custom-call | flops 70000001024 | bytes 1048576 | tf_op jit(solution)/shard_map/pallas_call | solution.py:1337
  542.3 15.0 %shard_map.302 = (f32[256,8192]{1,0:T(8,128)}, f32[256,2048]{1,0:T(8,128)}, f32[1024,2048]{1,0:T(8,128)}, f32[256,2048]{1,0:T(8,128)}, f32[256,256]{1,0:T(8,128)}) custom-call(bf16[2,4,256,1024]{3,2,1,0:T(8,128)(2,1)} %get-tuple-element.96.up, bf16[2,4,256,256]{3,2,1,0:T(8,128)(2,1)} %get-tuple-element.97.query, bf16[1024,2048]{1,0:T(8,128)(2,1)} %bitcast.99, ...), custom_call_target="tpu_custom_call" | custom-call | tf_op jit(solution)/shard_map/pallas_call | solution.py:1396
  557.3 1.0 copy.96
  558.3 1.0 copy.97
  (146 shorter events, 28.0 us)
Async XLA Ops:
  2.4 76.8 %copy-start = (bf16[256,2048]{1,0:T(8,128)(2,1)}, bf16[256,2048]{1,0:T(8,128)(2,1)S(1)}, u32[]{:S(2)}) copy-start(bf16[256,2048]{1,0:T(8,128)(2,1)S(1)} %dynamic-slice_convert_fusion.down) | copy-start | bytes 3145732
  2.4 87.2 %collective-permute-start = (bf16[256,2048]{1,0:T(8,128)(2,1)S(1)}, bf16[256,2048]{1,0:T(8,128)(2,1)S(1)}, u32[]{:S(2)}, u32[]{:S(2)}) collective-permute-start(bf16[256,2048]{1,0:T(8,128)(2,1)S(1)} %dynamic-slice_convert_fusion.down), channel_id=1, source_target_pairs={{0,8},{8,16},{16,24},{24,0},{1,9},{9,17},{17,25},{25,1},{2,10},{10... | collective-permute-start | bytes 3145736 | tf_op jit(solution)/shard_map/ppermute | solution.py:1534
  89.6 1.0 copy-start.9
  198.4 23.3 %collective-permute-start.1 = (bf16[256,2048]{1,0:T(8,128)(2,1)}, bf16[256,2048]{1,0:T(8,128)(2,1)S(1)}, u32[]{:S(2)}, u32[]{:S(2)}) collective-permute-start(bf16[256,2048]{1,0:T(8,128)(2,1)} %get-tuple-element.74), channel_id=1, source_target_pairs={{0,8},{8,16},{16,24},{24,0},{1,9},{9,17},{17,25},{25,1},{2,10},{10... | collective-permute-start | bytes 3145736 | tf_op jit(solution)/shard_map/ppermute | solution.py:1646
  199.9 10.1 %copy-start.11 = (bf16[8,160,2048]{2,1,0:T(8,128)(2,1)S(1)}, bf16[8,160,2048]{2,1,0:T(8,128)(2,1)}, u32[]{:S(2)}) copy-start(bf16[8,160,2048]{2,1,0:T(8,128)(2,1)} %get-tuple-element.71) | copy-start | bytes 15728644
  210.0 6.1 %copy-start.14 = (bf16[1280,1024]{1,0:T(8,128)(2,1)}, bf16[1280,1024]{1,0:T(8,128)(2,1)S(1)}, u32[]{:S(2)}) copy-start(bf16[1280,1024]{1,0:T(8,128)(2,1)S(1)} %get-tuple-element.158.act_far) | copy-start | bytes 7864324
  210.0 11.7 %copy-start.7 = (bf16[4,256,2048]{2,1,0:T(8,128)(2,1)S(1)}, bf16[4,256,2048]{2,1,0:T(8,128)(2,1)}, u32[]{:S(2)}) copy-start(bf16[4,256,2048]{2,1,0:T(8,128)(2,1)} %get-tuple-element.73) | copy-start | bytes 12582916
  216.1 5.8 %copy-start.3 = (bf16[1024,2048]{1,0:T(8,128)(2,1)}, bf16[1024,2048]{1,0:T(8,128)(2,1)S(1)}, u32[]{:S(2)}) copy-start(bf16[1024,2048]{1,0:T(8,128)(2,1)S(1)} %convolution_convert_fusion.1) | copy-start | bytes 12582916
  216.2 28.0 %collective-permute-start.2 = (bf16[256,2048]{1,0:T(8,128)(2,1)S(1)}, bf16[256,2048]{1,0:T(8,128)(2,1)S(1)}, u32[]{:S(2)}, u32[]{:S(2)}) collective-permute-start(bf16[256,2048]{1,0:T(8,128)(2,1)S(1)} %dynamic-slice_bitcast_fusion), channel_id=1, source_target_pairs={{0,8},{8,16},{16,24},{24,0},{1,9},{9,17},{17,25},{25,1},{2,10},{10... | collective-permute-start | bytes 3145736 | tf_op jit(solution)/shard_map/ppermute | solution.py:1654
  221.8 10.2 %copy-start.8 = (bf16[4,256,2048]{2,1,0:T(8,128)(2,1)}, bf16[4,256,2048]{2,1,0:T(8,128)(2,1)S(1)}, u32[]{:S(2)}) copy-start(bf16[4,256,2048]{2,1,0:T(8,128)(2,1)S(1)} %bitcast_dynamic-update-slice_fusion) | copy-start | bytes 12582916
  244.2 1.0 copy-start.10
  245.1 109.9 %copy-start.12 = (bf16[1280,256]{1,0:T(8,128)(2,1)S(1)}, bf16[1280,256]{1,0:T(8,128)(2,1)}, u32[]{:S(2)}) copy-start(bf16[1280,256]{1,0:T(8,128)(2,1)} %get-tuple-element.82) | copy-start | bytes 1966084
  360.0 102.9 %copy-start.4 = (f32[8,2048]{1,0:T(8,128)S(1)}, f32[8,2048]{1,0:T(8,128)}, u32[]{:S(2)}) copy-start(f32[8,2048]{1,0:T(8,128)} %get-tuple-element.93) | copy-start | bytes 196612
  464.6 5.4 copy-start.6
  464.6 5.4 copy-start.13
  470.0 1.9 copy-start.5
  542.3 15.0 %copy-start.2 = (bf16[4,64,2048]{2,1,0:T(8,128)(2,1)S(1)}, bf16[4,64,2048]{2,1,0:T(8,128)(2,1)}, u32[]{:S(2)}) copy-start(bf16[4,64,2048]{2,1,0:T(8,128)(2,1)} %get-tuple-element.181) | copy-start | bytes 3145732
  542.3 15.9 %copy-start.1 = (bf16[4,64,2048]{2,1,0:T(8,128)(2,1)S(1)}, bf16[4,64,2048]{2,1,0:T(8,128)(2,1)}, u32[]{:S(2)}) copy-start(bf16[4,64,2048]{2,1,0:T(8,128)(2,1)} %get-tuple-element.182) | copy-start | bytes 3145732

commit v4 on v3

--- a/solution.py
+++ b/solution.py
@@ -248,10 +248,11 @@
             pltpu.VMEM((rows, width), jnp.bfloat16),
         ]
 
-    def __init__(self, net, spot, parts, sums, diag, from_x, from_y):
+    def __init__(self, net, spot, parts, sums, diag, from_x, from_y, share=2):
         y, x, c = spot.y, spot.x, spot.c
-        half = parts.shape[1] // 2
-        lo, hi = pl.ds(0, half), pl.ds(half, half)
+        self.both = share == 2
+        half = parts.shape[1] // share
+        lo, hi = pl.ds(0, half), pl.ds(half * (share - 1), half)
         self.own, self.nx, self.ny, self.nd = (
             y * 2 + x,
             y * 2 + 1 - x,
@@ -268,44 +269,60 @@
             )
             for key, at in (("d", self.nd), ("x", self.nx), ("y", self.ny), ("o", self.own))
         }
-        self.d_lo = net.remote(sums.at[self.nd, lo], diag.at[lo], spot.to_x)
         self.d_hi = net.remote(sums.at[self.nd, hi], diag.at[hi], spot.to_y)
-        self.x_lo = net.remote(sums.at[self.nx, lo], from_x.at[lo], spot.to_x)
         self.y_hi = net.remote(sums.at[self.ny, hi], from_y.at[hi], spot.to_y)
         self.x_hi = net.remote(sums.at[self.nx, hi], from_x.at[hi], spot.to_x)
-        self.y_lo = net.remote(sums.at[self.ny, lo], from_y.at[lo], spot.to_y)
+        if self.both:
+            self.d_lo = net.remote(sums.at[self.nd, lo], diag.at[lo], spot.to_x)
+            self.x_lo = net.remote(sums.at[self.nx, lo], from_x.at[lo], spot.to_x)
+            self.y_lo = net.remote(sums.at[self.ny, lo], from_y.at[lo], spot.to_y)
 
     def start(self):
         for copy in self.first.values():
             copy.start()
 
+    def give(self, key, at):
+        if self.stacked:
+            self.send(at, at * 2 + 1 - self.c)
+            self.first[key].start()
+
     def pair(self, key, at):
-        self.first[key].got()
         if self.stacked:
-            self.compute(at * 2 + self.c, at)
+            self.prepare(at * 2 + self.c)
+            self.first[key].got()
+            self.merge(at * 2 + self.c, at)
         else:
+            self.first[key].got()
             add_rows(self.sums.at[at], self.parts.at[at * 2 + self.c])
 
     def middle(self):
+        self.give("d", self.nd)
+        self.give("x", self.nx)
         self.pair("d", self.nd)
-        self.d_lo.start()
+        if self.both:
+            self.d_lo.start()
         self.d_hi.start()
+        self.give("y", self.ny)
         self.pair("x", self.nx)
-        self.x_lo.start()
+        if self.both:
+            self.x_lo.start()
+        self.give("o", self.own)
         self.pair("y", self.ny)
         self.y_hi.start()
         self.pair("o", self.own)
 
     def last(self):
-        self.d_lo.got()
-        add_rows(self.sums.at[self.ny, self.lo], self.diag.at[self.lo], 16)
-        self.y_lo.start()
+        if self.both:
+            self.d_lo.got()
+            add_rows(self.sums.at[self.ny, self.lo], self.diag.at[self.lo], 16)
+            self.y_lo.start()
         self.d_hi.got()
         add_rows(self.sums.at[self.nx, self.hi], self.diag.at[self.hi], 16)
         self.x_hi.start()
 
     def finish(self, result):
-        for copy in (self.x_lo, self.y_hi, self.x_hi, self.y_lo):
+        second = (self.x_lo, self.y_lo) if self.both else ()
+        for copy in (self.y_hi, self.x_hi, *second):
             copy.got()
 
         @pl.loop(0, result.shape[0] // 16)
@@ -317,12 +334,10 @@
 
         for copy in (
             *self.first.values(),
-            self.d_lo,
             self.d_hi,
-            self.x_lo,
             self.x_hi,
-            self.y_lo,
             self.y_hi,
+            *((self.d_lo, *second) if self.both else ()),
         ):
             copy.sent()
 
@@ -386,56 +401,68 @@
 
 class LineScatter:
     def __init__(self, net, spot, parts, from_low, from_high, add):
-        self.spot, depth, z = spot, spot.depth, spot.z
-        self.parts, self.from_low, self.from_high, self.add = parts, from_low, from_high, add
-        self.ups, self.downs = [], []
-        for step in range(depth - 1):
-            self.ups.append(net.remote(parts(depth - 1 - step), from_low.at[step], spot.up))
-            self.downs.append(net.remote(parts(step), from_high.at[step], spot.down))
-
-    remotes = LineGather.remotes
+        self.net, self.spot, self.parts, self.add = net, spot, parts, add
+        self.boxes = (from_low, from_high)
+        self.first = net.count
+        net.count += 2 * (spot.depth - 1)
+
+    @staticmethod
+    def remotes(depth):
+        return 2 * (depth - 1)
+
+    def copy(self, side, message):
+        last = self.spot.depth - 1
+        slot = self.parts(last - message if side == 0 else message)
+        at = self.first + side * last + message
+        copy = pltpu.make_async_remote_copy(
+            src_ref=slot,
+            dst_ref=self.boxes[side].at[message],
+            send_sem=self.net.send_sems.at[at],
+            recv_sem=self.net.recv_sems.at[at],
+            device_id=(self.spot.up, self.spot.down)[side],
+            device_id_type=MESH_ID,
+        )
+        return copy, slot, self.boxes[side].at[message]
+
+    def take(self, side, message):
+        copy, slot, box = self.copy(side, message)
+        copy.wait_recv()
+        self.add(slot, box)
+
+    def place(self, side):
+        return self.spot.z if side == 0 else self.spot.depth - 1 - self.spot.z
 
     def stage(self, step):
-        z, last = self.spot.z, self.spot.depth - 1
-        up_to, down_to = last - step, step
-
-        @pl.when((z > 0) & (z < up_to))
-        def _():
-            self.ups[step].got()
-            self.add(self.parts(up_to), self.from_low.at[step])
-
-        @pl.when(z < up_to)
-        def _():
-            self.ups[step].start()
-
-        @pl.when((z < last) & (z > down_to))
-        def _():
-            self.downs[step].got()
-            self.add(self.parts(down_to), self.from_high.at[step])
-
-        @pl.when(z > down_to)
-        def _():
-            self.downs[step].start()
+        for side in range(2):
+            behind = self.place(side)
+
+            @pl.when(behind <= step)
+            def _():
+                message = step - behind
+
+                @pl.when(behind > 0)
+                def _():
+                    self.take(side, message)
+
+                self.copy(side, message)[0].start()
 
     def total(self):
-        z, last = self.spot.z, self.spot.depth - 1
-        for step in range(last):
-
-            @pl.when((z > 0) & (z == last - step))
+        last = self.spot.depth - 1
+        for side in range(2):
+            behind = self.place(side)
+
+            @pl.when(behind > 0)
             def _():
-                self.ups[step].got()
-                self.add(self.parts(last - step), self.from_low.at[step])
-
-            @pl.when((z < last) & (z == step))
-            def _():
-                self.downs[step].got()
-                self.add(self.parts(step), self.from_high.at[step])
+                self.take(side, last - behind)
 
     def finish(self):
-        z, last = self.spot.z, self.spot.depth - 1
-        for step in range(last):
-            pl.when(z < last - step)(self.ups[step].sent)
-            pl.when(z > step)(self.downs[step].sent)
+        for side in range(2):
+            behind = self.place(side)
+            for message in range(self.spot.depth - 1):
+
+                @pl.when(behind + message < self.spot.depth - 1)
+                def _():
+                    self.copy(side, message)[0].wait_send()
 
 
 class DpGather:
@@ -557,9 +584,9 @@
 
     def kernel(
         tok_held, cot_held, send, choose, query_w, kv_w, out_w, small_m, up_m, up_o,
-        own_tok, own_cot, up_own,
-        tok_all, query_all, kv_all, small_all, out_all,
-        tok, cot, tok_got, cot_got, out_v, kv_line, query_m, query_o, query_y, small_y,
+        own_tok, own_cot, up_own, small_rows, w_keyval,
+        tok_all, query_all, out_all,
+        kv_all, small_all, tok, cot, tok_got, cot_got, out_v, kv_line, query_m, query_o, query_y, small_y,
         query_f, out_f, kv_f, *sems,
     ):
         spot = Spot(depth)
@@ -588,10 +615,8 @@
         y_query = net.remote(query_o, query_y, spot.to_y)
         y_small = net.remote(small_m, small_y, spot.to_y)
         y_up = net.remote(up_o, up_own.at[y], spot.to_y, up_own.at[1 - y])
-        keep_small = net.local(small_m, small_all.at[z, y])
         keep_query = net.local(query_m, query_all.at[z, y])
         keep_query_y = net.local(query_y, query_all.at[z, 1 - y])
-        keep_small_y = net.local(small_y, small_all.at[z, 1 - y])
         keep_out = net.local(out_v, out_all)
         run_kv = LineGather(net, spot, z_slot)
         run_query = LineGather(net, spot, lambda at: query_all.at[at])
@@ -611,7 +636,7 @@
         pl.when(source)(read_out.start)
         read_kv.start()
         read_query.start()
-        keep_small.start()
+        small_all[z, y] = small_m[...]
         spot.barrier((spot.to_c, spot.to_x, spot.to_y, spot.to_xc), True)
         pick_rows(send, tok_held, tok)
         tok_deal.start()
@@ -639,13 +664,11 @@
         query_m[...] = low(query_f[1])
         keep_query.start()
         keep_query.wait()
-        keep_small.wait()
         y_query.got()
         keep_query_y.start()
         y_small.got()
-        keep_small_y.start()
+        small_all[z, 1 - y] = small_y[...]
         keep_query_y.wait()
-        keep_small_y.wait()
         run_query.start(0)
         run_small.start(0)
         pick_rows(send, cot_held, cot)
@@ -681,10 +704,21 @@
         keep_out.start()
         run_query.got(depth - 2)
         run_small.got(depth - 2)
+        for z_at in range(depth):
+            for y_at in range(2):
+                at = owner(z_at, y_at) * rows_own
+                small_rows[:, at : at + rows_own] = wide(small_all[z_at, y_at])
         y_up.got()
         runs = (*run_outs, run_kv, run_query, run_small, tok_run, kv_run)
         for run in (*runs, tok_deal, cot_deal):
             run.finish()
+        for y_at in range(2):
+            for xc_at in range(4):
+                for z_at in range(depth):
+                    at = owner(z_at, y_at) * rows_own + xc_at * kv_rows
+                    w_keyval[at : at + kv_rows, :] = kv_all[
+                        y_at * 4 + xc_at, z_at * kv_rows : (z_at + 1) * kv_rows, :
+                    ]
         for copy in (y_query, y_small, y_up):
             copy.sent()
         keep_out.wait()
@@ -703,15 +737,17 @@
             low_shape(rows, width),
             low_shape(rows, width),
             low_shape(2, *up_mine.shape),
+            wide_shape(small.shape[0], width),
+            low_shape(width, kv_cols),
             low_shape(8, rows, width),
             low_shape(depth, 2, rows_own, head_cols),
-            low_shape(8, depth * kv_rows, kv_cols),
-            low_shape(depth, 2, *small.shape),
             low_shape(group, rows_own, width),
         ],
         in_specs=[IN_VMEM] * 4 + [ANY] * 3 + [IN_VMEM] * 3,
-        out_specs=[IN_VMEM] * 3 + [ANY] * 5,
+        out_specs=[IN_VMEM] * 5 + [ANY] * 3,
         scratch_shapes=[
+            low_vmem(8, depth * kv_rows, kv_cols),
+            low_vmem(depth, 2, *small.shape),
             *[low_vmem(*tokens.shape)] * 4,
             low_vmem(group, rows_own, width),
             low_vmem(depth * kv_rows, kv_cols),
@@ -741,7 +777,31 @@
     return decorate
 
 
-def feed_blocks(run, c, parts, block, prepare=None):
+class Loads:
+    def __init__(self, net, far, near):
+        self.net, self.far, self.near = net, far, near
+        self.first = net.local_count
+        net.local_count += 8
+
+    def copy(self, member):
+        return pltpu.make_async_copy(
+            self.far.at[member], self.near.at[member], self.net.local_sems.at[self.first + member]
+        )
+
+    def start(self, spot):
+        def at(y, x, c):
+            return y * 4 + x * 2 + c
+
+        y, x, c = spot.y, spot.x, spot.c
+        for y_at, x_at in ((1 - y, 1 - x), (y, 1 - x), (1 - y, x), (y, x)):
+            for c_at in (1 - c, c):
+                self.copy(at(y_at, x_at, c_at)).start()
+
+    def wait(self, member):
+        self.copy(member).wait()
+
+
+def feed_blocks(run, parts, block, prepare=None):
     width = parts.shape[-1]
 
     def columns(body):
@@ -749,26 +809,23 @@
         def _(index):
             body(pl.ds(pl.multiple_of(index * 512, 512), 512))
 
-    def send(at, member):
+    def ready(member):
         if prepare is not None:
             prepare(member)
+
+    def send(at, member):
+        ready(member)
 
         @columns
         def _(cols):
             parts[at, :, cols] = low(block(member, cols))
 
     def merge(member, at):
-        if prepare is not None:
-            prepare(member)
-
         @columns
         def _(cols):
             run.sums[at, :, cols] = low(wide(run.sums[at, :, cols]) + block(member, cols))
 
-    run.compute = merge
-    for key, at in (("d", run.nd), ("x", run.nx), ("y", run.ny), ("o", run.own)):
-        send(at, at * 2 + 1 - c)
-        run.first[key].start()
+    run.send, run.merge, run.prepare = send, merge, ready
 
 
 SCORE_SCALE = 1.0 / math.sqrt(HEAD)
@@ -790,17 +847,17 @@
     return exps / jnp.sum(exps, axis=-1, keepdims=True)
 
 
-def attend(depth, tok_all, own_tok, own_cot, w_query, w_keyval, w_output, gain_a, shift_a, bias_q, bias_kv, allowed, bias, gain, shift, up_own, down_own, down_1):
+def attend(depth, tok_all, own_tok, own_cot, w_query, w_keyval, w_output, bias_q, bias_kv, allowed, small, up_own, down_own, down_1):
     rows, width = own_tok.shape
     total = 8 * rows
     head_cols = w_query.shape[1]
     micros = rows // PACK
 
     def kernel(
-        tok_far, tok, cot, w_q, w_kv, w_out, gain_1, shift_1, b_q, b_kv, allow, bias_row, gain_row, shift_row,
+        tok_far, tok, cot, w_q, w_kv, w_out, b_q, b_kv, allow, small,
         up, down, down_b,
         middle, normed_a, query, keyval, attended, normed_all, cot_all, up_all, down_all, down_2,
-        parts, normed, sums, diag, from_x, from_y, *sems,
+        tok_near, parts, normed, sums, diag, from_x, from_y, *sems,
     ):
         spot = Spot(depth)
         net = Net(*sems)
@@ -825,14 +882,17 @@
             ups.append(net.remote(at, at, after, up_all.at[behind(step)]))
         down_hop = net.remote(down_b, down_2, after)
 
+        tok_loads = Loads(net, tok_far, tok_near)
+
         def one_member(member):
+            tok_loads.wait(member)
             first = pl.multiple_of(member * rows, rows)
 
             @pl.loop(0, rows // ROWS_STEP)
             def _(index):
                 at = pl.multiple_of(index * ROWS_STEP, ROWS_STEP)
-                xhat, _ = normalize(wide(tok_far[member, pl.ds(at, ROWS_STEP), :]))
-                normed_a[pl.ds(first + at, ROWS_STEP), :] = low(xhat * gain_1[...] + shift_1[...])
+                xhat, _ = normalize(wide(tok_near[member, pl.ds(at, ROWS_STEP), :]))
+                normed_a[pl.ds(first + at, ROWS_STEP), :] = low(xhat * small[0:1, :] + small[1:2, :])
 
             rows_at = pl.ds(first, rows)
             query[rows_at, :] = low(product(normed_a[rows_at, :], w_q[...]) + b_q[...])
@@ -850,15 +910,16 @@
             rows_at = pl.ds(pl.multiple_of(member * rows, rows), rows)
             return product(attended[rows_at, :], w_out[:, cols])
 
+        tok_loads.start(spot)
         for copy in keeps:
             copy.start()
         spot.barrier((spot.to_c, spot.to_x, spot.to_y, *spot.ring()), False)
         ups[0].start()
         cot_run.start()
-        feed_blocks(run, spot.c, parts, block, one_member)
+        feed_blocks(run, parts, block, one_member)
+        run.middle()
         down_hop.start()
         cot_run.middle()
-        run.middle()
         ups[0].got()
         ups[1].start()
         run.last()
@@ -867,10 +928,10 @@
 
         @row_loop(rows)
         def _(at):
-            total_rows = wide(tok[at, :]) + (middle[at, :] + bias_row[...])
+            total_rows = wide(tok[at, :]) + (middle[at, :] + small[2:3, :])
             middle[at, :] = total_rows
             xhat, _ = normalize(total_rows)
-            normed[at, :] = low(xhat * gain_row[...] + shift_row[...])
+            normed[at, :] = low(xhat * small[3:4, :] + small[4:5, :])
 
         gather.start()
         down_hop.got()
@@ -902,23 +963,24 @@
             low_shape(depth, *down_own.shape),
             low_shape(*down_own.shape),
         ],
-        in_specs=[IN_VMEM] * 17,
+        in_specs=[ANY] + [IN_VMEM] * 12,
         out_specs=[IN_VMEM] * 5 + [ANY] * 4 + [IN_VMEM],
         scratch_shapes=[
+            low_vmem(8, rows, width),
             low_vmem(4, rows, width),
             low_vmem(rows, width),
             *PlaneScatter.buffers(rows, width),
-            *net_scratch(PlaneScatter.remotes + 2 * PlaneGather.remotes + depth, 6),
+            *net_scratch(PlaneScatter.remotes + 2 * PlaneGather.remotes + depth, 14),
         ],
         compiler_params=comm_params(3),
         cost_estimate=lasts(90, 1 << 20),
     )(
-        tok_all, own_tok, own_cot, w_query, w_keyval, w_output, gain_a, shift_a, bias_q, bias_kv,
-        allowed, bias, gain, shift, up_own, down_own, down_1,
+        tok_all, own_tok, own_cot, w_query, w_keyval, w_output, bias_q, bias_kv, allowed, small,
+        up_own, down_own, down_1,
     )
 
 
-def attend_back(depth, branch_all, query, keyval, allowed, w_output, w_query, w_keyval, own_tok, grad_middle, gain, block, chooser, holder, d_out, up_sum, up_parts):
+def attend_back(depth, branch_all, query, keyval, allowed, w_output, w_query, w_keyval, own_tok, grad_middle, gain, block, chooser, holder, d_out, up_sum, up_parts, down_sum):
     group = depth // 4
     rows, width = own_tok.shape
     total, head_cols = query.shape
@@ -926,16 +988,17 @@
     slots = chooser.shape[0] // 4
 
     def kernel(
-        branch, q_all, kv_all, allow, w_out, w_q, w_kv, tok, grad_mid, gain_row, block_own, choose, hold,
-        out, du, du_far,
-        grad_q, kv_rows_all, vec, block_res, grad_res, out_sum, du_sum,
+        branch_far, q_all, kv_all, allow, w_out, w_q, w_kv, tok, grad_mid, small, block_own, choose, hold,
+        out, du, dd, du_far,
+        grad_q, kv_rows_all, vec, block_res, grad_res, out_sum, du_sum, dd_x,
         parts, sums, diag, from_x, from_y, first, grad_low, block_send, grad_send, block_got, grad_got,
-        out_mix, out_lo, out_hi, du_term,
+        branch, out_mix, out_lo, out_hi, du_term, du_mid,
         grad_kv, kv_sums, kv_diag, kv_from_x, kv_from_y, kv_wide, kv_own, *sems,
     ):
         spot = Spot(depth)
         net = Net(*sems)
-        run = PlaneScatter(net, spot, parts, sums, diag, from_x, from_y)
+        run = PlaneScatter(net, spot, parts, sums, diag, from_x, from_y, share=1)
+        down_over = net.remote(dd, dd_x, spot.to_x)
         z = spot.z
         after, _ = spot.ring()
         deal = DpExchange(net, spot, out, out_mix)
@@ -949,12 +1012,28 @@
         kv_run = PlaneScatter(net, spot, grad_kv, kv_sums, kv_diag, kv_from_x, kv_from_y)
         kv_gather = PlaneGather(net, spot, kv_own, kv_rows_all)
         run_out = LineScatter(net, spot, mixed, out_lo, out_hi, add2)
-        up_hop = net.remote(du, du_sum, after)
-        up_term = net.local(du_far.at[z], du_term)
+        hops = [net.remote(du, du_mid, after), net.remote(du_mid, du_sum, after)]
+        terms = [
+            net.local(du_far.at[lax.rem(z + 1, depth)], du_term.at[0]),
+            net.local(du_far.at[z], du_term.at[1]),
+        ]
+
+        def up_step(step):
+            into = (du_mid, du_sum)[step]
+            hops[step].got()
+            terms[step].wait()
+            for at in range(2):
+                add_rows(into.at[at], du_term.at[step, at], 32)
+            if step == 0:
+                hops[1].start()
+
         back_block = DpExchange(net, spot, block_send, block_got)
         back_grad = DpExchange(net, spot, grad_send, grad_got)
 
+        branch_loads = Loads(net, branch_far, branch)
+
         def one_member(member):
+            branch_loads.wait(member)
             begin = pl.multiple_of(member * rows, rows)
             grad_att = low(product_cols(branch[member], w_out[...]))
             for index in range(micros):
@@ -980,24 +1059,27 @@
                 grad_kv[member], w_kv[cols, :]
             )
 
-        up_term.start()
+        branch_loads.start(spot)
+        for copy in terms:
+            copy.start()
         spot.barrier((spot.to_c, spot.to_x, spot.to_y, spot.to_xc, *spot.ring()), False)
         deal.start()
-        up_hop.start()
+        hops[0].start()
+        down_over.start()
         pick_rows(choose, block_own, block_send)
-        back_block.start()
-        feed_blocks(run, spot.c, parts, block_of, one_member)
+        feed_blocks(run, parts, block_of, one_member)
+        run.middle()
+        kv_run.start()
         deal.got()
         run_out.stage(0)
-        kv_run.start()
-        run.middle()
+        up_step(0)
         kv_run.middle()
-        for step in range(1, depth - 1):
-            run_out.stage(step)
         run.last()
+        run_out.stage(1)
         kv_run.last()
         run.finish(first)
         kv_run.finish(kv_wide)
+        back_block.start()
         kv_own[...] = low(kv_wide[...])
         kv_gather.start()
         vec[...] = jnp.zeros_like(vec)
@@ -1005,29 +1087,30 @@
         @row_loop(rows)
         def _(at):
             xhat, scale = normalize(wide(tok[at, :]))
-            grad = grad_mid[at, :] + norm_back(first[at, :], gain_row[...], xhat, scale)
+            grad = grad_mid[at, :] + norm_back(first[at, :], small[0:1, :], xhat, scale)
             grad_low[at, :] = low(grad)
             vec[0:1, :] += jnp.sum(first[at, :] * xhat, axis=0, keepdims=True)
             vec[1:2, :] += jnp.sum(first[at, :], axis=0, keepdims=True)
 
         pick_rows(choose, grad_low, grad_send)
         back_grad.start()
+        for step in range(2, depth - 1):
+            run_out.stage(step)
         kv_gather.middle()
         run_out.total()
         out_sum[...] = mixed(z)[...]
         kv_gather.last()
         back_block.got()
         pick_rows(hold, block_got, block_res)
-        up_hop.got()
-        up_term.wait()
-        for at in range(2):
-            add_rows(du_sum.at[at], du_term.at[at], 32)
         back_grad.got()
         pick_rows(hold, grad_got, grad_res)
+        up_step(1)
         for run_done in (back_block, back_grad, deal, run_out):
             run_done.finish()
         kv_gather.finish()
-        up_hop.sent()
+        down_over.got()
+        for copy in (*hops, down_over):
+            copy.sent()
 
     return pl.pallas_call(
         kernel,
@@ -1039,40 +1122,43 @@
             low_shape(4, slots, width),
             low_shape(*d_out.shape[2:]),
             low_shape(*up_sum.shape),
+            low_shape(*down_sum.shape),
         ],
-        in_specs=[IN_VMEM] * 15 + [ANY],
-        out_specs=[IN_VMEM, ANY] + [IN_VMEM] * 5,
+        in_specs=[ANY] + [IN_VMEM] * 15 + [ANY],
+        out_specs=[IN_VMEM, ANY] + [IN_VMEM] * 6,
         scratch_shapes=[
             low_vmem(4, rows, width),
             *PlaneScatter.buffers(rows, width),
             pltpu.VMEM((rows, width), jnp.float32),
             low_vmem(rows, width),
             *[low_vmem(4, slots, width)] * 4,
+            low_vmem(8, rows, width),
             low_vmem(*d_out.shape),
             *[low_vmem(depth - 1, *d_out.shape[2:])] * 2,
+            low_vmem(2, *up_sum.shape),
             low_vmem(*up_sum.shape),
             low_vmem(8, rows, 2 * HEAD),
             *PlaneScatter.buffers(rows, 2 * HEAD),
             pltpu.VMEM((rows, 2 * HEAD), jnp.float32),
             low_vmem(rows, 2 * HEAD),
             *net_scratch(
-                2 * PlaneScatter.remotes + PlaneGather.remotes + 3 * DpExchange.remotes + LineGather.remotes(depth) + 1, 6
+                2 * PlaneScatter.remotes + PlaneGather.remotes + 3 * DpExchange.remotes + LineGather.remotes(depth) + 3, 14
             ),
         ],
         compiler_params=comm_params(4),
         cost_estimate=lasts(70, 1 << 20),
     )(
         branch_all, query, keyval, allowed, w_output, w_query, w_keyval, own_tok, grad_middle, gain,
-        block, chooser, holder, d_out, up_sum, up_parts,
+        block, chooser, holder, d_out, up_sum, down_sum, up_parts,
     )
 
 
-def mlp_back(depth, grad_hidden, w_up, activated, w_down, middle, own_cot, gain, bias, down_first, d_down, d_up):
+def mlp_back(depth, grad_hidden, w_up, activated, w_down, middle, own_cot, small, down_first, d_down, d_up):
     rows, width = own_cot.shape
-    up_hops = min(2, depth - 1)
-
-    def kernel(gh, up, act_far, down_far, mid, cot, gain_row, bias_row, dd_first, dd, du,
-               vec, grad_middle, branch_all, block_out, dd_sum, du_sum, dd_x,
+    up_hops = 1
+
+    def kernel(gh, up, act_far, down_far, mid, cot, small, dd_first, dd, du,
+               vec, grad_middle, branch_all, block_out, dd_sum, du_sum,
                parts, branch, sums, diag, from_x, from_y,
                parts2, sums2, diag2, from_x2, from_y2, mlp_sum, act, down,
                dd_got, du_got, dd_term, du_term, grad_normed, *sems):
@@ -1106,16 +1192,12 @@
         ups = [net.remote(du.at[slot(0)], up_at(1), after)]
         ups += [net.remote(up_at(step - 1), up_at(step), after) for step in range(2, up_hops + 1)]
 
-        down_over = net.remote(dd_sum, dd_x, spot.to_x)
-
         def down_step(step):
             down_hops[step - 2].got()
             down_terms[step - 1].wait()
             add_rows(down_at(step), dd_term.at[step - 1], 32)
             if step < depth - 1:
                 down_hops[step - 1].start()
-            else:
-                down_over.start()
 
         def up_step(step):
             ups[step - 1].got()
@@ -1144,14 +1226,13 @@
             dd_got[0, at, :] = low(wide(dd_first[at, :]) + wide(dd_term[0, at, :]))
 
         down_hops[0].start()
-        feed_blocks(run, spot.c, parts, block)
+        feed_blocks(run, parts, block)
         run.middle()
         for copy in loads:
             copy.wait()
-        feed_blocks(run2, spot.c, parts2, block2)
+        feed_blocks(run2, parts2, block2)
         run.last()
         down_step(2)
-        ups[0].start()
         run.finish(grad_normed)
         vec[...] = jnp.zeros_like(vec)
 
@@ -1160,7 +1241,7 @@
             xhat, scale = normalize(mid[at, :])
             grad_n = grad_normed[at, :]
             grad_o = wide(cot[at, :])
-            grad = grad_o + norm_back(grad_n, gain_row[...], xhat, scale)
+            grad = grad_o + norm_back(grad_n, small[3:4, :], xhat, scale)
             grad_b = low(grad)
             grad_middle[at, :] = grad
             branch[at, :] = grad_b
@@ -1168,26 +1249,24 @@
                 vec[row : row + 1, :] += jnp.sum(values, axis=0, keepdims=True)
 
         gather.start()
-        for step in range(3, depth):
-            if step < depth - 1:
-                down_step(step)
+        for step in range(3, depth - 1):
+            down_step(step)
+        run2.middle()
+        down_step(depth - 1)
+        ups[0].start()
         gather.middle()
-        run2.middle()
         gather.last()
-        down_step(depth - 1)
-        up_step(1)
         run2.last()
         gather.finish()
         run2.finish(mlp_sum)
 
         @row_loop(rows)
         def _(at):
-            block_out[at, :] = low(mid[at, :] + (mlp_sum[at, :] + bias_row[...]))
-
-        for step in range(2, up_hops + 1):
+            block_out[at, :] = low(mid[at, :] + (mlp_sum[at, :] + small[5:6, :]))
+
+        for step in range(1, up_hops + 1):
             up_step(step)
-        down_over.got()
-        for copy in (*down_hops, *ups, down_over):
+        for copy in (*down_hops, *ups):
             copy.sent()
 
     return pl.pallas_call(
@@ -1199,10 +1278,9 @@
             low_shape(rows, width),
             low_shape(*d_down.shape[1:]),
             low_shape(*d_up.shape[1:]),
-            low_shape(*d_down.shape[1:]),
         ],
-        in_specs=[IN_VMEM] * 2 + [ANY] * 2 + [IN_VMEM] * 5 + [ANY] * 2,
-        out_specs=[IN_VMEM, IN_VMEM, ANY, IN_VMEM, IN_VMEM, IN_VMEM, IN_VMEM],
+        in_specs=[IN_VMEM] * 2 + [ANY] * 2 + [IN_VMEM] * 4 + [ANY] * 2,
+        out_specs=[IN_VMEM, IN_VMEM, ANY, IN_VMEM, IN_VMEM, IN_VMEM],
         scratch_shapes=[
             low_vmem(4, rows, width),
             low_vmem(rows, width),
@@ -1218,14 +1296,14 @@
             low_vmem(up_hops, *d_up.shape[1:]),
             pltpu.VMEM((rows, width), jnp.float32),
             *net_scratch(
-                2 * PlaneScatter.remotes + PlaneGather.remotes + depth + up_hops + 1,
+                2 * PlaneScatter.remotes + PlaneGather.remotes + depth + up_hops,
                 depth + up_hops + 3,
             ),
         ],
         compiler_params=comm_params(5),
         cost_estimate=lasts(95, 1 << 20),
     )(
-        grad_hidden, w_up, activated, w_down, middle, own_cot, gain, bias, down_first, d_down, d_up
+        grad_hidden, w_up, activated, w_down, middle, own_cot, small, down_first, d_down, d_up
     )
 
 
@@ -1365,7 +1443,7 @@
     seg = up_all.shape[3] // depth
     head_cols = query_all.shape[3]
     down_rows, width = down_all.shape
-    steps = rows // 16
+    steps = rows // 32
 
     def kernel(up, query, down, out, kv, up_w, query_w, down_w, out_w, kv_w):
         for y in range(2):
@@ -1384,7 +1462,7 @@
         return pl.BlockSpec((array.shape[0] // steps, array.shape[1]), lambda index: (index, 0))
 
     def blocks_of(array):
-        return pl.BlockSpec((2, 4, 16, array.shape[3]), lambda index: (0, 0, index, 0))
+        return pl.BlockSpec((2, 4, 32, array.shape[3]), lambda index: (0, 0, index, 0))
 
     shapes = [
         wide_shape(rows, 8 * depth * seg),
@@ -1519,9 +1597,15 @@
             up_bias,
             value_bias,
         ]
-        small = low(lax.optimization_barrier(jnp.concatenate(small_parts)))
-        small_count = small.shape[0]
-        small = jnp.pad(small, (0, 16 * 256 - small_count)).reshape(16, 256)
+        sizes = [item.shape[0] for item in small_parts]
+        begins = [sum(sizes[:index]) for index in range(len(sizes))]
+        small_count = sum(sizes)
+        small_size = 16 * rows_own
+        small = sum(
+            jnp.pad(item, (begin, small_size - begin - size))
+            for item, begin, size in zip(small_parts, begins, sizes)
+        )
+        small = low(small).reshape(16, rows_own)
         down_own = low(lax.dynamic_slice_in_dim(down_weight, my_xc * ff_seg, ff_seg, axis=0))
         ring = [(index, (index + 1) % depth) for index in range(depth)]
 
@@ -1542,10 +1626,10 @@
             own_low,
             own_cot,
             up_piece,
+            small_rows,
+            w_keyval,
             tokens_all,
             query_all,
-            keyval_all,
-            small_all,
             w_output,
         ) = opening(
             depth,
@@ -1563,34 +1647,13 @@
         )
         w_output = w_output.reshape(head_cols, width)
 
-        if y_slow:
-            small_all = jnp.transpose(small_all, (1, 0, 2, 3))
-        gathered_small = wide(small_all.reshape(fsdp_size, 16 * 256)[:, :small_count])
-        sizes = [item.shape[0] for item in small_parts]
-        begins = [sum(sizes[:index]) for index in range(len(sizes))]
-        (
-            gain_a,
-            shift_a,
-            bias_o,
-            gain_m,
-            shift_m,
-            bias_d,
-            bias_q,
-            bias_u,
-            bias_v,
-        ) = [
-            gathered_small[:, start : start + size].reshape(-1)
-            for start, size in zip(begins, sizes)
-        ]
-        my_bias_q = lax.dynamic_slice_in_dim(bias_q, head_base(my_y), head_cols)
-        my_bias_u = jnp.concatenate(
-            [
-                lax.dynamic_slice_in_dim(
-                    bias_u, owner(z_at, my_y) * ff_own + my_xc * ff_seg, ff_seg
-                )
-                for z_at in range(depth)
-            ]
-        )
+        my_bias_q = lax.dynamic_slice(small_rows, (6, head_base(my_y)), (1, head_cols))
+        bias_u = lax.dynamic_slice_in_dim(small_rows, 7 + my_xc, 1)
+        bias_u = bias_u.reshape((2, depth, ff_seg) if y_slow else (depth, 2, ff_seg))
+        my_bias_u = lax.dynamic_index_in_dim(
+            bias_u, my_y, 0 if y_slow else 1, keepdims=False
+        ).reshape(depth * ff_seg)
+        bias_v = small_rows[11].reshape(fsdp_size, rows_own)[:, : HEAD // fsdp_size].reshape(HEAD)
         bias_kv = jnp.concatenate([jnp.zeros((HEAD,), jnp.float32), bias_v])
 
         def rows_in_order(gathered):
@@ -1606,9 +1669,6 @@
             return values.reshape(depth, 2, rows_own, values.shape[-1])
 
         w_query = rows_in_order(query_all)
-        keyval_all = keyval_all.reshape(2, 4, depth, out_seg, 2 * HEAD)
-        order = (0, 2, 1, 3, 4) if y_slow else (2, 0, 1, 3, 4)
-        w_keyval = jnp.transpose(keyval_all, order).reshape(width, 2 * HEAD)
         (
             middle,
             normed_attn,
@@ -1628,14 +1688,10 @@
             w_query,
             w_keyval,
             w_output,
-            gain_a[None],
-            shift_a[None],
-            my_bias_q[None],
+            my_bias_q,
             bias_kv[None],
             wide(allowed),
-            bias_o[None],
-            gain_m[None],
-            shift_m[None],
+            small_rows,
             up_piece,
             down_own,
             down_hop_1,
@@ -1661,7 +1717,7 @@
         grad_act = product_cols(mixed_later, w_down)
         grad_hidden = low(slope * grad_act)
         up_parts = rows_by_z(low(product_rows(normed_mlp, grad_hidden)))
-        second_sums, grad_middle, grad_branch, block_own, d_down, d_up, down_x = mlp_back(
+        second_sums, grad_middle, grad_branch, block_own, d_down, d_up = mlp_back(
             depth,
             grad_hidden,
             w_up,
@@ -1669,14 +1725,13 @@
             w_down,
             middle,
             own_cot,
-            gain_m[None],
-            bias_d[None],
+            small_rows,
             down_first,
             down_parts,
             up_parts,
         )
         grad_flat = grad_branch.reshape(micro * PACK, width)
-        for step in range(3, depth - 1):
+        for step in range(2, depth - 2):
             d_up = lax.ppermute(d_up, "z", ring)
             at = (my_z - 1 - step + 2 * depth) % depth
             term = lax.dynamic_index_in_dim(up_parts, at, 0, keepdims=False)
@@ -1693,7 +1748,7 @@
         d_out_parts = jnp.transpose(
             d_output.reshape(depth // 4, 4, out_seg, width), (1, 0, 2, 3)
         )
-        grad_query, grad_keyval, first_sums, block_out, input_grad, out_own, d_up = attend_back(
+        grad_query, grad_keyval, first_sums, block_out, input_grad, out_own, d_up, down_x = attend_back(
             depth,
             grad_branch,
             query,
@@ -1704,13 +1759,14 @@
             w_keyval,
             own_low,
             grad_middle,
-            gain_a[None],
+            small_rows,
             block_own,
             back_chooser,
             holder,
             d_out_parts,
             d_up,
             up_parts,
+            d_down,
         )
         d_query = low(product_rows(normed_attn, grad_query))
         grad_keyval = grad_keyval.reshape(micro * PACK, 2 * HEAD)
@@ -1747,11 +1803,11 @@
             colsum(own_keyval[:, HEAD:]),
         ]
         vectors = jnp.concatenate([item.reshape(fsdp_size, -1) for item in vectors], axis=1)
-        vectors = jnp.pad(low(vectors), ((0, 0), (0, 16 * 256 - small_count)))
+        vectors = jnp.pad(low(vectors), ((0, 0), (0, small_size - small_count)))
         if y_slow:
-            d_vec = jnp.transpose(vectors.reshape(2, depth, 16, 256), (1, 0, 2, 3))
+            d_vec = jnp.transpose(vectors.reshape(2, depth, 16, rows_own), (1, 0, 2, 3))
         else:
-            d_vec = vectors.reshape(depth, 2, 16, 256)
+            d_vec = vectors.reshape(depth, 2, 16, rows_own)
 
         if y_slow:
             d_keyval = d_keyval.reshape(2, depth, 4, out_seg, 2 * HEAD)
@@ -1773,7 +1829,7 @@
             out_all.reshape(rows_own, width),
             kv_sum.reshape(rows_own, 2 * HEAD),
         )
-        vec_own = jnp.sum(wide(vec_all), axis=0).reshape(16 * 256)
+        vec_own = jnp.sum(wide(vec_all), axis=0).reshape(small_size)
         (
             gain_a_grad,
             shift_a_grad,

time: 568 us -> 505 us (0.89)
  Pallas kernels: 462 us -> 409 us
  local copies, waits for them, and re-layouts: 29.3 us -> 18 us
    pallas_call x1, Pallas kernels: 66.6 us -> 42.1 us  [closing(): pl.pallas_call(kernel, out_shape=[low_shape(2, 4, *up_own.shape[1:]), low...]
    pallas_call x1, Pallas kernels: 110 us -> 87.3 us  [mlp_back(): pl.pallas_call(kernel, out_shape=[wide_shape(8, width), wide_shape(rows,...]
    pallas_call x1, Pallas kernels: 102 us -> 91.5 us  [attend_back(): pl.pallas_call(kernel, out_shape=[low_shape(total, head_cols), low_shape(...]
    unnamed x63 -> x44, local copies, waits for them, and re-layouts: 15.2 us -> 5.22 us
    pallas_call x1, Pallas kernels: 61 us -> 67.1 us  [opening(): pl.pallas_call(kernel, out_shape=[low_shape(rows, width), low_shape(rows,...]
  transfers between devices with their start and end apart: 3 -> 3, of which waited for: 2 -> 2; matrix products, arithmetic and copies ran while one was open for 11% -> 10% of each run, Pallas kernels for 11% -> 14%
where the time goes in v4:
time: 505 us; the launch traced here: 496 us
  Pallas kernels  409 us (81%)
  matrix products  48.5 us (10%)
  local copies, waits for them, and re-layouts  18 us (4%)
  other arithmetic  9.74 us (2%)
  waiting for transfers between devices  8.03 us (2%)
    pallas_call x1, Pallas kernels, attend(): pl.pallas_call(kernel, out_shape=[wide_shape(rows, width), low_shape(tota...  109 us
    pallas_call x1, Pallas kernels, attend_back(): pl.pallas_call(kernel, out_shape=[low_shape(total, head_cols), low_shape(...  91.5 us
    pallas_call x1, Pallas kernels, mlp_back(): pl.pallas_call(kernel, out_shape=[wide_shape(8, width), wide_shape(rows,...  87.3 us
    pallas_call x1, Pallas kernels, opening(): pl.pallas_call(kernel, out_shape=[low_shape(rows, width), low_shape(rows,...  67.1 us
    pallas_call x1, Pallas kernels, closing(): pl.pallas_call(kernel, out_shape=[low_shape(2, 4, *up_own.shape[1:]), low...  42.1 us
    dot_general x5, matrix products, product_rows(): lax.dot_general(left_mat, right_mat, (((0,), (0,)), ((), ())), preferred_...  28.3 us
    pallas_call x1, Pallas kernels, widen(): pl.pallas_call(kernel, grid=(steps,), in_specs=[blocks_of(up_all), blocks...  12.2 us
    dot_general x1, matrix products, product_cols(): lax.dot_general(left_mat, right_mat, (((1,), (1,)), ((), ())), preferred_...  10.2 us
  transfers between devices with their start and end apart: 3, of which 2 were waited for; matrix products, arithmetic and copies ran while one was open for 10% of the time, Pallas kernels for 14%

profile of v4, /device:TPU:9, one launch (start us, length us, event | category | flops | bytes accessed | tf_op | source)
XLA Modules:
  0.0 496.5 jit_solution(7079913449180737949)
XLA Ops:
  0.7 1.7 dynamic-slice_convert_fusion.down
  2.4 1.3 collective-permute-start
  10.1 1.6 dynamic-slice_convert_fusion.4
  11.7 1.1 pad_maximum_fusion
  12.8 67.1 %shard_map.297 = (bf16[160,2048]{1,0:T(8,128)(2,1)}, bf16[160,2048]{1,0:T(8,128)(2,1)}, bf16[2,256,1024]{2,1,0:T(8,128)(2,1)}, f32[16,2048]{1,0:T(8,128)}, bf16[...) custom-call(bf16[4,64,2048]{2,1,0:T(8,128)(2,1)} %tok_held.1, ...), custom_call_target="tpu_custom_call" | custom-call | flops 74999996416 | bytes 1048576 | tf_op jit(solution)/shard_map/pallas_call | solution.py:734
  80.0 1.0 dynamic-slice_reduce_fusion.1
  81.0 1.3 constant_dynamic-slice_fusion.6.b_q
  84.0 1.1 and_convert_fusion.allow
  86.0 108.7 %shard_map.298 = (f32[160,2048]{1,0:T(8,128)}, bf16[1280,2048]{1,0:T(8,128)(2,1)}, bf16[1280,256]{1,0:T(8,128)(2,1)}, bf16[1280,256]{1,0:T(8,128)(2,1)}, bf16[12...) custom-call(bf16[8,160,2048]{2,1,0:T(8,128)(2,1)} %get-tuple-element, ...), custom_call_target="tpu_custom_call" | custom-call | flops 89999998976 | bytes 1048576 | tf_op jit(solution)/shard_map/pallas_call | solution.py:952
  195.0 10.1 %multiply_convert_fusion = (bf16[1280,1024]{1,0:T(8,128)(2,1)S(1)}, f32[1280,1024]{1,0:T(8,128)S(1)}) fusion(f32[1024]{0:T(1024)S(1)} %bitcast.71, bf16[1280,2048]{1,0:T(8,128)(2,1)} %bitcast.86, bf16[2048,1024]{1,0:T(8,128)(2,1)} %bitcast.91), kind=kOutput, calls=%fused_computation.10 | convolution fusion | flops 5381816320 | bytes 17305600 | tf_op jit(solution)/shard_map/dot_general | solution.py:33
  205.1 6.0 %convolution_convert_fusion.1 = bf16[1024,2048]{1,0:T(8,128)(2,1)S(1)} fusion(bf16[1280,1024]{1,0:T(8,128)(2,1)S(1)} %get-tuple-element.149.act_far, bf16[1280,2048]{1,0:T(8,128)(2,1)S(1)} %bitcast.88), kind=kOutput, calls=%fused_computation.12 | convolution fusion | flops 5370806272 | bytes 12058624 | tf_op jit(solution)/shard_map/dot_general | solution.py:37
  211.3 7.3 %collective-permute-done.1 = bf16[256,2048]{1,0:T(8,128)(2,1)S(1)} collective-permute-done((bf16[256,2048]{1,0:T(8,128)(2,1)}, bf16[256,2048]{1,0:T(8,128)(2,1)S(1)}, u32[]{:S(2)}, u32[]{:S(2)}) %collective-permute-start.1) | collective-permute-done | bytes 1048608 | tf_op jit(solution)/shard_map/ppermute | solution.py:1702
  218.8 10.2 %convert_reduce_fusion = (f32[1024]{0:T(1024)S(1)}, bf16[1280,1024]{1,0:T(8,128)(2,1)}) fusion(bf16[1280,2048]{1,0:T(8,128)(2,1)S(1)} %bitcast.89, bf16[1024,2048]{1,0:T(8,128)(2,1)S(1)} %bitcast.84, f32[1280,1024]{1,0:T(8,128)S(1)} %get-tuple-element.150, f32[1024]{0:T(1024)S(1)} %bitcast.72), kind=kOutput, calls=%fused_computation.9 | convolution fusion | flops 5397543936 | bytes 17309696 | tf_op jit(solution)/shard_map/dot_general | solution.py:43
  230.2 10.2 %convolution_convert_fusion = bf16[2048,1024]{1,0:T(8,128)(2,1)} fusion(bf16[1280,2048]{1,0:T(8,128)(2,1)} %bitcast.87, bf16[1280,1024]{1,0:T(8,128)(2,1)} %get-tuple-element.152.gh), kind=kOutput, calls=%fused_computation.11 | convolution fusion | flops 5370806272 | bytes 12058624 | tf_op jit(solution)/shard_map/dot_general | solution.py:37
  242.1 87.3 %shard_map.299 = (f32[8,2048]{1,0:T(8,128)}, f32[160,2048]{1,0:T(8,128)}, bf16[8,160,2048]{2,1,0:T(8,128)(2,1)}, bf16[160,2048]{1,0:T(8,128)(2,1)}, bf16[256,204...) custom-call(bf16[1280,1024]{1,0:T(8,128)(2,1)} %get-tuple-element.152.gh, bf16[2048,1024]{1,0:T(8,128)(2,1)} %bitcast.92, ...), custom_call_target="tpu_custom_call" | custom-call | flops 95000002560 | bytes 1048576 | tf_op jit(solution)/shard_map/pallas_call | solution.py:1272
  329.5 5.0 %convolution_convert_fusion.4 = bf16[256,2048]{1,0:T(8,128)(2,1)} fusion(bf16[1280,256]{1,0:T(8,128)(2,1)S(1)} %copy-done.12, bf16[1280,2048]{1,0:T(8,128)(2,1)} %bitcast.90), kind=kOutput, calls=%fused_computation.15 | convolution fusion | flops 1342701568 | bytes 6946816 | tf_op jit(solution)/shard_map/dot_general | solution.py:37
  334.5 91.5 %shard_map.300 = (bf16[1280,256]{1,0:T(8,128)(2,1)}, bf16[8,160,256]{2,1,0:T(8,128)(2,1)}, f32[8,2048]{1,0:T(8,128)}, bf16[4,64,2048]{2,1,0:T(8,128)(2,1)}, bf16...) custom-call(bf16[8,160,2048]{2,1,0:T(8,128)(2,1)} %get-tuple-element, ...), custom_call_target="tpu_custom_call" | custom-call | flops 70000001024 | bytes 1048576 | tf_op jit(solution)/shard_map/pallas_call | solution.py:1115
  427.1 1.3 convert_reduce_fusion.1
  428.6 5.4 %convolution_convert_fusion.3 = bf16[2048,256]{1,0:T(8,128)(2,1)} fusion(bf16[1280,2048]{1,0:T(8,128)(2,1)} %get-tuple-element.89, bf16[1280,256]{1,0:T(8,128)(2,1)} %get-tuple-element.90), kind=kOutput, calls=%fused_computation.14 | convolution fusion | flops 1342701568 | bytes 6946816 | tf_op jit(solution)/shard_map/dot_general | solution.py:37
  434.0 1.7 convolution_convert_fusion.2
  437.2 42.1 %shard_map.301 = (bf16[2,4,256,1024]{3,2,1,0:T(8,128)(2,1)}, bf16[4,256,2048]{2,1,0:T(8,128)(2,1)}, bf16[2,4,256,256]{3,2,1,0:T(8,128)(2,1)}, bf16[4,64,256]{2,1...) custom-call(bf16[2,256,1024]{2,1,0:T(8,128)(2,1)} %get-tuple-element.87.up, ...), custom_call_target="tpu_custom_call" | custom-call | flops 70000001024 | bytes 1048576 | tf_op jit(solution)/shard_map/pallas_call | solution.py:1415
  481.8 12.2 %shard_map.302 = (f32[256,8192]{1,0:T(8,128)}, f32[256,2048]{1,0:T(8,128)}, f32[1024,2048]{1,0:T(8,128)}, f32[256,2048]{1,0:T(8,128)}, f32[256,256]{1,0:T(8,128)}) custom-call(bf16[2,4,256,1024]{3,2,1,0:T(8,128)(2,1)} %get-tuple-element.96.up, bf16[2,4,256,256]{3,2,1,0:T(8,128)(2,1)} %get-tuple-element.97.query, bf16[1024,2048]{1,0:T(8,128)(2,1)} %bitcast.60, ...), custom_call_target="tpu_custom_call" | custom-call | tf_op jit(solution)/shard_map/pallas_call | solution.py:1474
  494.1 1.0 copy.72
  495.0 1.0 copy.73
  (124 shorter events, 17.6 us)
Async XLA Ops:
  2.4 77.6 %copy-start = (bf16[256,2048]{1,0:T(8,128)(2,1)}, bf16[256,2048]{1,0:T(8,128)(2,1)S(1)}, u32[]{:S(2)}) copy-start(bf16[256,2048]{1,0:T(8,128)(2,1)S(1)} %dynamic-slice_convert_fusion.down) | copy-start | bytes 3145732
  2.4 82.7 %collective-permute-start = (bf16[256,2048]{1,0:T(8,128)(2,1)S(1)}, bf16[256,2048]{1,0:T(8,128)(2,1)S(1)}, u32[]{:S(2)}, u32[]{:S(2)}) collective-permute-start(bf16[256,2048]{1,0:T(8,128)(2,1)S(1)} %dynamic-slice_convert_fusion.down), channel_id=1, source_target_pairs={{0,8},{8,16},{16,24},{24,0},{1,9},{9,17},{17,25},{25,1},{2,10},{10... | collective-permute-start | bytes 3145736 | tf_op jit(solution)/shard_map/ppermute | solution.py:1618
  85.1 1.0 copy-start.9
  194.8 23.9 %collective-permute-start.1 = (bf16[256,2048]{1,0:T(8,128)(2,1)}, bf16[256,2048]{1,0:T(8,128)(2,1)S(1)}, u32[]{:S(2)}, u32[]{:S(2)}) collective-permute-start(bf16[256,2048]{1,0:T(8,128)(2,1)} %get-tuple-element.74), channel_id=1, source_target_pairs={{0,8},{8,16},{16,24},{24,0},{1,9},{9,17},{17,25},{25,1},{2,10},{10... | collective-permute-start | bytes 3145736 | tf_op jit(solution)/shard_map/ppermute | solution.py:1702
  195.0 10.1 %copy-start.11 = (bf16[8,160,2048]{2,1,0:T(8,128)(2,1)S(1)}, bf16[8,160,2048]{2,1,0:T(8,128)(2,1)}, u32[]{:S(2)}) copy-start(bf16[8,160,2048]{2,1,0:T(8,128)(2,1)} %get-tuple-element.71) | copy-start | bytes 15728644
  205.1 6.1 %copy-start.14 = (bf16[1280,1024]{1,0:T(8,128)(2,1)}, bf16[1280,1024]{1,0:T(8,128)(2,1)S(1)}, u32[]{:S(2)}) copy-start(bf16[1280,1024]{1,0:T(8,128)(2,1)S(1)} %get-tuple-element.149.act_far) | copy-start | bytes 7864324
  205.1 13.5 %copy-start.7 = (bf16[4,256,2048]{2,1,0:T(8,128)(2,1)S(1)}, bf16[4,256,2048]{2,1,0:T(8,128)(2,1)}, u32[]{:S(2)}) copy-start(bf16[4,256,2048]{2,1,0:T(8,128)(2,1)} %get-tuple-element.73) | copy-start | bytes 12582916
  211.2 7.6 %copy-start.3 = (bf16[1024,2048]{1,0:T(8,128)(2,1)}, bf16[1024,2048]{1,0:T(8,128)(2,1)S(1)}, u32[]{:S(2)}) copy-start(bf16[1024,2048]{1,0:T(8,128)(2,1)S(1)} %convolution_convert_fusion.1) | copy-start | bytes 12582916
  211.3 29.9 %collective-permute-start.2 = (bf16[256,2048]{1,0:T(8,128)(2,1)S(1)}, bf16[256,2048]{1,0:T(8,128)(2,1)S(1)}, u32[]{:S(2)}, u32[]{:S(2)}) collective-permute-start(bf16[256,2048]{1,0:T(8,128)(2,1)S(1)} %dynamic-slice_bitcast_fusion), channel_id=1, source_target_pairs={{0,8},{8,16},{16,24},{24,0},{1,9},{9,17},{17,25},{25,1},{2,10},{10... | collective-permute-start | bytes 3145736 | tf_op jit(solution)/shard_map/ppermute | solution.py:1710
  218.8 10.2 %copy-start.8 = (bf16[4,256,2048]{2,1,0:T(8,128)(2,1)}, bf16[4,256,2048]{2,1,0:T(8,128)(2,1)S(1)}, u32[]{:S(2)}) copy-start(bf16[4,256,2048]{2,1,0:T(8,128)(2,1)S(1)} %bitcast_dynamic-update-slice_fusion) | copy-start | bytes 12582916
  241.1 1.0 copy-start.10
  242.1 87.4 %copy-start.12 = (bf16[1280,256]{1,0:T(8,128)(2,1)S(1)}, bf16[1280,256]{1,0:T(8,128)(2,1)}, u32[]{:S(2)}) copy-start(bf16[1280,256]{1,0:T(8,128)(2,1)} %get-tuple-element.82) | copy-start | bytes 1966084
  334.4 92.4 %copy-start.4 = (f32[8,2048]{1,0:T(8,128)S(1)}, f32[8,2048]{1,0:T(8,128)}, u32[]{:S(2)}) copy-start(f32[8,2048]{1,0:T(8,128)} %get-tuple-element.93) | copy-start | bytes 196612
  428.6 5.4 %copy-start.6 = (bf16[8,160,256]{2,1,0:T(8,128)(2,1)S(1)}, bf16[8,160,256]{2,1,0:T(8,128)(2,1)}, u32[]{:S(2)}) copy-start(bf16[8,160,256]{2,1,0:T(8,128)(2,1)} %get-tuple-element.91) | copy-start | bytes 1966084
  428.6 5.4 %copy-start.13 = (bf16[1280,2048]{1,0:T(8,128)(2,1)S(1)}, bf16[1280,2048]{1,0:T(8,128)(2,1)}, u32[]{:S(2)}) copy-start(bf16[1280,2048]{1,0:T(8,128)(2,1)} %get-tuple-element.89) | copy-start | bytes 15728644
  434.0 1.9 copy-start.5
  481.8 12.3 %copy-start.2 = (bf16[4,64,2048]{2,1,0:T(8,128)(2,1)S(1)}, bf16[4,64,2048]{2,1,0:T(8,128)(2,1)}, u32[]{:S(2)}) copy-start(bf16[4,64,2048]{2,1,0:T(8,128)(2,1)} %get-tuple-element.172) | copy-start | bytes 3145732
  481.8 13.2 %copy-start.1 = (bf16[4,64,2048]{2,1,0:T(8,128)(2,1)S(1)}, bf16[4,64,2048]{2,1,0:T(8,128)(2,1)}, u32[]{:S(2)}) copy-start(bf16[4,64,2048]{2,1,0:T(8,128)(2,1)} %get-tuple-element.173) | copy-start | bytes 3145732

commit v5 on v4

--- a/solution.py
+++ b/solution.py
@@ -847,17 +847,17 @@
     return exps / jnp.sum(exps, axis=-1, keepdims=True)
 
 
-def attend(depth, tok_all, own_tok, own_cot, w_query, w_keyval, w_output, bias_q, bias_kv, allowed, small, up_own, down_own, down_1):
+def attend(depth, owner, tok_all, own_tok, own_cot, w_query, w_keyval, w_output, allowed, small, up_own, down_own, down_1):
     rows, width = own_tok.shape
     total = 8 * rows
     head_cols = w_query.shape[1]
     micros = rows // PACK
 
     def kernel(
-        tok_far, tok, cot, w_q, w_kv, w_out, b_q, b_kv, allow, small,
+        tok_far, tok, cot, w_q, w_kv, w_out, allow, small,
         up, down, down_b,
-        middle, normed_a, query, keyval, attended, normed_all, cot_all, up_all, down_all, down_2,
-        tok_near, parts, normed, sums, diag, from_x, from_y, *sems,
+        middle, normed_a, query, keyval, attended, normed_all, cot_all, up_all, down_all,
+        tok_near, b_kv, parts, normed, sums, diag, from_x, from_y, *sems,
     ):
         spot = Spot(depth)
         net = Net(*sems)
@@ -875,12 +875,15 @@
             net.local(down, down_all.at[z]),
             net.local(down_b, down_all.at[behind(1)]),
         ]
-        keep_2 = net.local(down_2, down_all.at[behind(2)])
         ups = [net.remote(up, up_all.at[z], after, up_all.at[behind(1)])]
         for step in range(2, depth):
             at = up_all.at[behind(step - 1)]
             ups.append(net.remote(at, at, after, up_all.at[behind(step)]))
-        down_hop = net.remote(down_b, down_2, after)
+
+        xc = spot.x * 2 + spot.c
+        group = depth // 4
+        rows_own = width // (2 * depth)
+        head_base = pl.multiple_of(owner(xc * group, spot.y) * rows_own, 128)
 
         tok_loads = Loads(net, tok_far, tok_near)
 
@@ -895,7 +898,10 @@
                 normed_a[pl.ds(first + at, ROWS_STEP), :] = low(xhat * small[0:1, :] + small[1:2, :])
 
             rows_at = pl.ds(first, rows)
-            query[rows_at, :] = low(product(normed_a[rows_at, :], w_q[...]) + b_q[...])
+            query[rows_at, :] = low(
+                product(normed_a[rows_at, :], w_q[...])
+                + small[6:7, pl.ds(head_base, head_cols)]
+            )
             keyval[rows_at, :] = low(product(normed_a[rows_at, :], w_kv[...]) + b_kv[...])
 
             for index in range(micros):
@@ -911,6 +917,17 @@
             return product(attended[rows_at, :], w_out[:, cols])
 
         tok_loads.start(spot)
+        each = HEAD // (2 * depth)
+        lane = lax.broadcasted_iota(jnp.int32, (1, HEAD), 1)
+        values = jnp.zeros((1, HEAD), jnp.float32)
+        for at in range(2 * depth):
+            begin = at * rows_own // HEAD * HEAD
+            found = pltpu.roll(
+                small[11:12, begin : begin + HEAD], (at * each - at * rows_own + begin) % HEAD, 1
+            )
+            values = jnp.where((lane >= at * each) & (lane < (at + 1) * each), found, values)
+        b_kv[:, :HEAD] = jnp.zeros((1, HEAD), jnp.float32)
+        b_kv[:, HEAD:] = values
         for copy in keeps:
             copy.start()
         spot.barrier((spot.to_c, spot.to_x, spot.to_y, *spot.ring()), False)
@@ -918,7 +935,6 @@
         cot_run.start()
         feed_blocks(run, parts, block, one_member)
         run.middle()
-        down_hop.start()
         cot_run.middle()
         ups[0].got()
         ups[1].start()
@@ -934,8 +950,6 @@
             normed[at, :] = low(xhat * small[3:4, :] + small[4:5, :])
 
         gather.start()
-        down_hop.got()
-        keep_2.start()
         for step in range(2, depth - 1):
             ups[step - 1].got()
             ups[step].start()
@@ -944,9 +958,9 @@
         gather.finish()
         cot_run.finish()
         ups[-1].got()
-        for copy in (*ups, down_hop):
+        for copy in ups:
             copy.sent()
-        for copy in (*keeps, keep_2):
+        for copy in keeps:
             copy.wait()
 
     return pl.pallas_call(
@@ -961,12 +975,12 @@
             low_shape(8, rows, width),
             low_shape(depth, *up_own.shape),
             low_shape(depth, *down_own.shape),
-            low_shape(*down_own.shape),
         ],
-        in_specs=[ANY] + [IN_VMEM] * 12,
-        out_specs=[IN_VMEM] * 5 + [ANY] * 4 + [IN_VMEM],
+        in_specs=[ANY] + [IN_VMEM] * 10,
+        out_specs=[IN_VMEM] * 5 + [ANY] * 4,
         scratch_shapes=[
             low_vmem(8, rows, width),
+            pltpu.VMEM((1, 2 * HEAD), jnp.float32),
             low_vmem(4, rows, width),
             low_vmem(rows, width),
             *PlaneScatter.buffers(rows, width),
@@ -975,7 +989,7 @@
         compiler_params=comm_params(3),
         cost_estimate=lasts(90, 1 << 20),
     )(
-        tok_all, own_tok, own_cot, w_query, w_keyval, w_output, bias_q, bias_kv, allowed, small,
+        tok_all, own_tok, own_cot, w_query, w_keyval, w_output, allowed, small,
         up_own, down_own, down_1,
     )
 
@@ -1647,15 +1661,11 @@
         )
         w_output = w_output.reshape(head_cols, width)
 
-        my_bias_q = lax.dynamic_slice(small_rows, (6, head_base(my_y)), (1, head_cols))
         bias_u = lax.dynamic_slice_in_dim(small_rows, 7 + my_xc, 1)
         bias_u = bias_u.reshape((2, depth, ff_seg) if y_slow else (depth, 2, ff_seg))
         my_bias_u = lax.dynamic_index_in_dim(
             bias_u, my_y, 0 if y_slow else 1, keepdims=False
         ).reshape(depth * ff_seg)
-        bias_v = small_rows[11].reshape(fsdp_size, rows_own)[:, : HEAD // fsdp_size].reshape(HEAD)
-        bias_kv = jnp.concatenate([jnp.zeros((HEAD,), jnp.float32), bias_v])
-
         def rows_in_order(gathered):
             if y_slow:
                 gathered = jnp.transpose(gathered, (1, 0, 2, 3))
@@ -1669,6 +1679,9 @@
             return values.reshape(depth, 2, rows_own, values.shape[-1])
 
         w_query = rows_in_order(query_all)
+        down_hop_1, up_piece = lax.optimization_barrier((down_hop_1, up_piece))
+        down_piece = lax.ppermute(down_hop_1, "z", ring)
+
         (
             middle,
             normed_attn,
@@ -1679,17 +1692,15 @@
             cotangent_all,
             up_all,
             down_all,
-            down_piece,
         ) = attend(
             depth,
+            owner,
             tokens_all,
             own_low,
             own_cot,
             w_query,
             w_keyval,
             w_output,
-            my_bias_q,
-            bias_kv[None],
             wide(allowed),
             small_rows,
             up_piece,
@@ -1698,6 +1709,8 @@
         )
         normed_mlp = normed_mlp.reshape(micro * PACK, width)
         grad_mixed = cotangent_all.reshape(micro * PACK, width)
+        down_piece, normed_mlp = lax.optimization_barrier((down_piece, normed_mlp))
+        down_all = ring_slot(down_all, down_piece, 2)
         for step in range(3, depth):
             down_piece = lax.ppermute(down_piece, "z", ring)
             down_all = ring_slot(down_all, down_piece, step)

time: 505 us -> 496 us (0.982)
  Pallas kernels: 409 us -> 403 us
    pallas_call x1, Pallas kernels: 109 us -> 99.3 us  [attend(): pl.pallas_call(kernel, out_shape=[wide_shape(rows, width), low_shape(tota...]
  transfers between devices with their start and end apart: 3 -> 4, of which waited for: 2 -> 2; matrix products, arithmetic and copies ran while one was open for 10% -> 10% of each run, Pallas kernels for 14% -> 34%
where the time goes in v5:
time: 496 us; the launch traced here: 488 us
  Pallas kernels  403 us (81%)
  matrix products  48.5 us (10%)
  local copies, waits for them, and re-layouts  15 us (3%)
  other arithmetic  9.74 us (2%)
  starting transfers between devices  5.48 us (1%)
    pallas_call x1, Pallas kernels, attend(): pl.pallas_call(kernel, out_shape=[wide_shape(rows, width), low_shape(tota...  99.3 us
    pallas_call x1, Pallas kernels, attend_back(): pl.pallas_call(kernel, out_shape=[low_shape(total, head_cols), low_shape(...  91.3 us
    pallas_call x1, Pallas kernels, mlp_back(): pl.pallas_call(kernel, out_shape=[wide_shape(8, width), wide_shape(rows,...  91 us
    pallas_call x1, Pallas kernels, opening(): pl.pallas_call(kernel, out_shape=[low_shape(rows, width), low_shape(rows,...  67.2 us
    pallas_call x1, Pallas kernels, closing(): pl.pallas_call(kernel, out_shape=[low_shape(2, 4, *up_own.shape[1:]), low...  42.1 us
    dot_general x5, matrix products, product_rows(): lax.dot_general(left_mat, right_mat, (((0,), (0,)), ((), ())), preferred_...  28.3 us
    pallas_call x1, Pallas kernels, widen(): pl.pallas_call(kernel, grid=(steps,), in_specs=[blocks_of(up_all), blocks...  12.2 us
    dot_general x1, matrix products, product_cols(): lax.dot_general(left_mat, right_mat, (((1,), (1,)), ((), ())), preferred_...  10.2 us
  transfers between devices with their start and end apart: 4, of which 2 were waited for; matrix products, arithmetic and copies ran while one was open for 10% of the time, Pallas kernels for 34%

profile of v5, /device:TPU:9, one launch (start us, length us, event | category | flops | bytes accessed | tf_op | source)
XLA Modules:
  0.0 488.2 jit_solution(5734108674143272280)
XLA Ops:
  0.7 1.7 dynamic-slice_convert_fusion.down
  2.4 1.3 collective-permute-start
  10.1 1.6 dynamic-slice_convert_fusion.4
  11.7 1.1 pad_maximum_fusion
  12.8 67.2 %shard_map.297 = (bf16[160,2048]{1,0:T(8,128)(2,1)}, bf16[160,2048]{1,0:T(8,128)(2,1)}, bf16[2,256,1024]{2,1,0:T(8,128)(2,1)}, f32[16,2048]{1,0:T(8,128)}, bf16[...) custom-call(bf16[4,64,2048]{2,1,0:T(8,128)(2,1)} %tok_held.1, ...), custom_call_target="tpu_custom_call" | custom-call | flops 74999996416 | bytes 1048576 | tf_op jit(solution)/shard_map/pallas_call | solution.py:734
  82.0 1.1 and_convert_fusion.allow
  83.0 2.4 collective-permute-start.1
  85.4 99.3 %shard_map.298 = (f32[160,2048]{1,0:T(8,128)}, bf16[1280,2048]{1,0:T(8,128)(2,1)}, bf16[1280,256]{1,0:T(8,128)(2,1)}, bf16[1280,256]{1,0:T(8,128)(2,1)}, bf16[12...) custom-call(bf16[8,160,2048]{2,1,0:T(8,128)(2,1)} %get-tuple-element, ...), custom_call_target="tpu_custom_call" | custom-call | flops 89999998976 | bytes 1048576 | tf_op jit(solution)/shard_map/pallas_call | solution.py:966
  184.8 1.7 collective-permute-start.2
  186.4 10.0 %multiply_convert_fusion = (bf16[1280,1024]{1,0:T(8,128)(2,1)S(1)}, f32[1280,1024]{1,0:T(8,128)S(1)}) fusion(f32[1024]{0:T(1024)S(1)} %bitcast.72, bf16[1280,2048]{1,0:T(8,128)(2,1)} %bitcast.86, bf16[2048,1024]{1,0:T(8,128)(2,1)} %bitcast.91), kind=kOutput, calls=%fused_computation.10 | convolution fusion | flops 5381816320 | bytes 17305600 | tf_op jit(solution)/shard_map/dot_general | solution.py:33
  196.5 6.0 %convolution_convert_fusion.1 = bf16[1024,2048]{1,0:T(8,128)(2,1)S(1)} fusion(bf16[1280,1024]{1,0:T(8,128)(2,1)S(1)} %get-tuple-element.153.act_far, bf16[1280,2048]{1,0:T(8,128)(2,1)S(1)} %bitcast.88), kind=kOutput, calls=%fused_computation.12 | convolution fusion | flops 5370806272 | bytes 12058624 | tf_op jit(solution)/shard_map/dot_general | solution.py:37
  202.9 4.0 collective-permute-done.2
  207.0 10.2 %convert_reduce_fusion = (f32[1024]{0:T(1024)S(1)}, bf16[1280,1024]{1,0:T(8,128)(2,1)}) fusion(bf16[1280,2048]{1,0:T(8,128)(2,1)S(1)} %bitcast.89, bf16[1024,2048]{1,0:T(8,128)(2,1)S(1)} %bitcast.84, f32[1280,1024]{1,0:T(8,128)S(1)} %get-tuple-element.154, f32[1024]{0:T(1024)S(1)} %bitcast.73), kind=kOutput, calls=%fused_computation.9 | convolution fusion | flops 5397543936 | bytes 17309696 | tf_op jit(solution)/shard_map/dot_general | solution.py:43
  218.4 10.2 %convolution_convert_fusion = bf16[2048,1024]{1,0:T(8,128)(2,1)} fusion(bf16[1280,2048]{1,0:T(8,128)(2,1)} %bitcast.87, bf16[1280,1024]{1,0:T(8,128)(2,1)} %get-tuple-element.156.gh), kind=kOutput, calls=%fused_computation.11 | convolution fusion | flops 5370806272 | bytes 12058624 | tf_op jit(solution)/shard_map/dot_general | solution.py:37
  230.3 91.0 %shard_map.299 = (f32[8,2048]{1,0:T(8,128)}, f32[160,2048]{1,0:T(8,128)}, bf16[8,160,2048]{2,1,0:T(8,128)(2,1)}, bf16[160,2048]{1,0:T(8,128)(2,1)}, bf16[256,204...) custom-call(bf16[1280,1024]{1,0:T(8,128)(2,1)} %get-tuple-element.156.gh, bf16[2048,1024]{1,0:T(8,128)(2,1)} %bitcast.92, ...), custom_call_target="tpu_custom_call" | custom-call | flops 95000002560 | bytes 1048576 | tf_op jit(solution)/shard_map/pallas_call | solution.py:1286
  321.3 5.0 %convolution_convert_fusion.4 = bf16[256,2048]{1,0:T(8,128)(2,1)} fusion(bf16[1280,256]{1,0:T(8,128)(2,1)S(1)} %copy-done.12, bf16[1280,2048]{1,0:T(8,128)(2,1)} %bitcast.90), kind=kOutput, calls=%fused_computation.15 | convolution fusion | flops 1342701568 | bytes 6946816 | tf_op jit(solution)/shard_map/dot_general | solution.py:37
  326.3 91.3 %shard_map.300 = (bf16[1280,256]{1,0:T(8,128)(2,1)}, bf16[8,160,256]{2,1,0:T(8,128)(2,1)}, f32[8,2048]{1,0:T(8,128)}, bf16[4,64,2048]{2,1,0:T(8,128)(2,1)}, bf16...) custom-call(bf16[8,160,2048]{2,1,0:T(8,128)(2,1)} %get-tuple-element, ...), custom_call_target="tpu_custom_call" | custom-call | flops 70000001024 | bytes 1048576 | tf_op jit(solution)/shard_map/pallas_call | solution.py:1129
  418.8 1.3 convert_reduce_fusion.1
  420.3 5.4 %convolution_convert_fusion.3 = bf16[2048,256]{1,0:T(8,128)(2,1)} fusion(bf16[1280,2048]{1,0:T(8,128)(2,1)} %get-tuple-element.95, bf16[1280,256]{1,0:T(8,128)(2,1)} %get-tuple-element.96), kind=kOutput, calls=%fused_computation.14 | convolution fusion | flops 1342701568 | bytes 6946816 | tf_op jit(solution)/shard_map/dot_general | solution.py:37
  425.7 1.7 convolution_convert_fusion.2
  429.0 42.1 %shard_map.301 = (bf16[2,4,256,1024]{3,2,1,0:T(8,128)(2,1)}, bf16[4,256,2048]{2,1,0:T(8,128)(2,1)}, bf16[2,4,256,256]{3,2,1,0:T(8,128)(2,1)}, bf16[4,64,256]{2,1...) custom-call(bf16[2,256,1024]{2,1,0:T(8,128)(2,1)} %get-tuple-element.93.up, ...), custom_call_target="tpu_custom_call" | custom-call | flops 70000001024 | bytes 1048576 | tf_op jit(solution)/shard_map/pallas_call | solution.py:1429
  473.5 12.2 %shard_map.302 = (f32[256,8192]{1,0:T(8,128)}, f32[256,2048]{1,0:T(8,128)}, f32[1024,2048]{1,0:T(8,128)}, f32[256,2048]{1,0:T(8,128)}, f32[256,256]{1,0:T(8,128)}) custom-call(bf16[2,4,256,1024]{3,2,1,0:T(8,128)(2,1)} %get-tuple-element.102.up, bf16[2,4,256,256]{3,2,1,0:T(8,128)(2,1)} %get-tuple-element.103.query, bf16[1024,2048]{1,0:T(8,128)(2,1)} %bitcast.61, ...), custom_call_target="tpu_custom_call" | custom-call | tf_op jit(solution)/shard_map/pallas_call | solution.py:1488
  485.8 1.0 copy.73
  486.8 1.0 copy.74
  (122 shorter events, 16.8 us)
Async XLA Ops:
  2.4 77.6 %copy-start = (bf16[256,2048]{1,0:T(8,128)(2,1)}, bf16[256,2048]{1,0:T(8,128)(2,1)S(1)}, u32[]{:S(2)}) copy-start(bf16[256,2048]{1,0:T(8,128)(2,1)S(1)} %dynamic-slice_convert_fusion.down) | copy-start | bytes 3145732
  2.4 80.6 %collective-permute-start = (bf16[256,2048]{1,0:T(8,128)(2,1)S(1)}, bf16[256,2048]{1,0:T(8,128)(2,1)S(1)}, u32[]{:S(2)}, u32[]{:S(2)}) collective-permute-start(bf16[256,2048]{1,0:T(8,128)(2,1)S(1)} %dynamic-slice_convert_fusion.down), channel_id=1, source_target_pairs={{0,8},{8,16},{16,24},{24,0},{1,9},{9,17},{17,25},{25,1},{2,10},{10... | collective-permute-start | bytes 3145736 | tf_op jit(solution)/shard_map/ppermute | solution.py:1632
  83.0 2.4 copy-start.9
  83.0 101.7 %collective-permute-start.1 = (bf16[256,2048]{1,0:T(8,128)(2,1)S(1)}, bf16[256,2048]{1,0:T(8,128)(2,1)S(1)}, u32[]{:S(2)}, u32[]{:S(2)}) collective-permute-start(bf16[256,2048]{1,0:T(8,128)(2,1)S(1)} %collective-permute-done.down_b), channel_id=1, source_target_pairs={{0,8},{8,16},{16,24},{24,0},{1,9},{9,17},{17,25},{25,1},{2,10},{10... | collective-permute-start | bytes 3145736 | tf_op jit(solution)/shard_map/ppermute | solution.py:1683
  184.8 22.1 %collective-permute-start.2 = (bf16[256,2048]{1,0:T(8,128)(2,1)S(1)}, bf16[256,2048]{1,0:T(8,128)(2,1)S(1)}, u32[]{:S(2)}, u32[]{:S(2)}) collective-permute-start(bf16[256,2048]{1,0:T(8,128)(2,1)S(1)} %collective-permute-done.1), channel_id=1, source_target_pairs={{0,8},{8,16},{16,24},{24,0},{1,9},{9,17},{17,25},{25,1},{2,10},{10... | collective-permute-start | bytes 3145736 | tf_op jit(solution)/shard_map/ppermute | solution.py:1715
  186.4 10.1 %copy-start.11 = (bf16[8,160,2048]{2,1,0:T(8,128)(2,1)S(1)}, bf16[8,160,2048]{2,1,0:T(8,128)(2,1)}, u32[]{:S(2)}) copy-start(bf16[8,160,2048]{2,1,0:T(8,128)(2,1)} %get-tuple-element.77) | copy-start | bytes 15728644
  196.5 6.1 %copy-start.14 = (bf16[1280,1024]{1,0:T(8,128)(2,1)}, bf16[1280,1024]{1,0:T(8,128)(2,1)S(1)}, u32[]{:S(2)}) copy-start(bf16[1280,1024]{1,0:T(8,128)(2,1)S(1)} %get-tuple-element.153.act_far) | copy-start | bytes 7864324
  196.5 6.2 %copy-start.7 = (bf16[4,256,2048]{2,1,0:T(8,128)(2,1)S(1)}, bf16[4,256,2048]{2,1,0:T(8,128)(2,1)}, u32[]{:S(2)}) copy-start(bf16[4,256,2048]{2,1,0:T(8,128)(2,1)} %get-tuple-element.79) | copy-start | bytes 12582916
  202.6 4.4 copy-start.3
  202.7 26.7 %collective-permute-start.3 = (bf16[256,2048]{1,0:T(8,128)(2,1)S(1)}, bf16[256,2048]{1,0:T(8,128)(2,1)S(1)}, u32[]{:S(2)}, u32[]{:S(2)}) collective-permute-start(bf16[256,2048]{1,0:T(8,128)(2,1)S(1)} %dynamic-slice_bitcast_fusion), channel_id=1, source_target_pairs={{0,8},{8,16},{16,24},{24,0},{1,9},{9,17},{17,25},{25,1},{2,10},{10... | collective-permute-start | bytes 3145736 | tf_op jit(solution)/shard_map/ppermute | solution.py:1723
  207.0 10.2 %copy-start.8 = (bf16[4,256,2048]{2,1,0:T(8,128)(2,1)}, bf16[4,256,2048]{2,1,0:T(8,128)(2,1)S(1)}, u32[]{:S(2)}) copy-start(bf16[4,256,2048]{2,1,0:T(8,128)(2,1)S(1)} %bitcast_dynamic-update-slice_fusion) | copy-start | bytes 12582916
  229.3 1.0 copy-start.10
  230.3 91.0 %copy-start.12 = (bf16[1280,256]{1,0:T(8,128)(2,1)S(1)}, bf16[1280,256]{1,0:T(8,128)(2,1)}, u32[]{:S(2)}) copy-start(bf16[1280,256]{1,0:T(8,128)(2,1)} %get-tuple-element.88) | copy-start | bytes 1966084
  326.3 92.3 %copy-start.4 = (f32[8,2048]{1,0:T(8,128)S(1)}, f32[8,2048]{1,0:T(8,128)}, u32[]{:S(2)}) copy-start(f32[8,2048]{1,0:T(8,128)} %get-tuple-element.99) | copy-start | bytes 196612
  420.3 5.4 %copy-start.6 = (bf16[8,160,256]{2,1,0:T(8,128)(2,1)S(1)}, bf16[8,160,256]{2,1,0:T(8,128)(2,1)}, u32[]{:S(2)}) copy-start(bf16[8,160,256]{2,1,0:T(8,128)(2,1)} %get-tuple-element.97) | copy-start | bytes 1966084
  420.3 5.4 %copy-start.13 = (bf16[1280,2048]{1,0:T(8,128)(2,1)S(1)}, bf16[1280,2048]{1,0:T(8,128)(2,1)}, u32[]{:S(2)}) copy-start(bf16[1280,2048]{1,0:T(8,128)(2,1)} %get-tuple-element.95) | copy-start | bytes 15728644
  425.7 1.9 copy-start.5
  473.5 12.3 %copy-start.2 = (bf16[4,64,2048]{2,1,0:T(8,128)(2,1)S(1)}, bf16[4,64,2048]{2,1,0:T(8,128)(2,1)}, u32[]{:S(2)}) copy-start(bf16[4,64,2048]{2,1,0:T(8,128)(2,1)} %get-tuple-element.176) | copy-start | bytes 3145732
  473.5 13.2 %copy-start.1 = (bf16[4,64,2048]{2,1,0:T(8,128)(2,1)S(1)}, bf16[4,64,2048]{2,1,0:T(8,128)(2,1)}, u32[]{:S(2)}) copy-start(bf16[4,64,2048]{2,1,0:T(8,128)(2,1)} %get-tuple-element.177) | copy-start | bytes 3145732

commit v6 on v5

--- a/solution.py
+++ b/solution.py
@@ -1635,7 +1635,17 @@
         from_slot = jnp.repeat(slot_for, slot_len) * slot_len + places % slot_len
         sender = low(from_slot[:, None] == places[None, :])
         holder = low(places[:, None] == from_slot[None, :])
+        hits = my_holders[None, :] == jnp.arange(4)[:, None]
+        seq_starts = (my_starts + jnp.arange(MB)[:, None] * PACK).reshape(held)
+        send_lens = jnp.sum(jnp.where(hits, my_lens[None, :], 0), axis=1)
+        send_starts = jnp.sum(jnp.where(hits, seq_starts[None, :], 0), axis=1)
+        pos = jnp.arange(slot_len)
+        live = pos[None, :] < send_lens[:, None]
+        send_rows = jnp.where(live, send_starts[:, None] + pos[None, :], -1)
+        back_chooser = low(send_rows.reshape(flat)[:, None] == jnp.arange(own_count)[None, :])
         chooser = low((source_row[:, None] == jnp.arange(flat)[None, :]) & own_valid)
+        allow = wide(allowed)
+        tokens, allow, back_chooser = lax.optimization_barrier((tokens, allow, back_chooser))
         (
             own_low,
             own_cot,
@@ -1661,11 +1671,6 @@
         )
         w_output = w_output.reshape(head_cols, width)
 
-        bias_u = lax.dynamic_slice_in_dim(small_rows, 7 + my_xc, 1)
-        bias_u = bias_u.reshape((2, depth, ff_seg) if y_slow else (depth, 2, ff_seg))
-        my_bias_u = lax.dynamic_index_in_dim(
-            bias_u, my_y, 0 if y_slow else 1, keepdims=False
-        ).reshape(depth * ff_seg)
         def rows_in_order(gathered):
             if y_slow:
                 gathered = jnp.transpose(gathered, (1, 0, 2, 3))
@@ -1701,7 +1706,7 @@
             w_query,
             w_keyval,
             w_output,
-            wide(allowed),
+            allow,
             small_rows,
             up_piece,
             down_own,
@@ -1709,7 +1714,14 @@
         )
         normed_mlp = normed_mlp.reshape(micro * PACK, width)
         grad_mixed = cotangent_all.reshape(micro * PACK, width)
-        down_piece, normed_mlp = lax.optimization_barrier((down_piece, normed_mlp))
+        down_piece, normed_mlp, late_rows = lax.optimization_barrier(
+            (down_piece, normed_mlp, small_rows)
+        )
+        bias_u = lax.dynamic_slice_in_dim(late_rows, 7 + my_xc, 1)
+        bias_u = bias_u.reshape((2, depth, ff_seg) if y_slow else (depth, 2, ff_seg))
+        my_bias_u = lax.dynamic_index_in_dim(
+            bias_u, my_y, 0 if y_slow else 1, keepdims=False
+        ).reshape(depth * ff_seg)
         down_all = ring_slot(down_all, down_piece, 2)
         for step in range(3, depth):
             down_piece = lax.ppermute(down_piece, "z", ring)
@@ -1750,14 +1762,6 @@
             term = lax.dynamic_index_in_dim(up_parts, at, 0, keepdims=False)
             d_up = low(wide(d_up) + wide(term))
         d_output = low(product_rows(attended, grad_flat))
-        hits = my_holders[None, :] == jnp.arange(4)[:, None]
-        seq_starts = (my_starts + jnp.arange(MB)[:, None] * PACK).reshape(held)
-        send_lens = jnp.sum(jnp.where(hits, my_lens[None, :], 0), axis=1)
-        send_starts = jnp.sum(jnp.where(hits, seq_starts[None, :], 0), axis=1)
-        pos = jnp.arange(slot_len)
-        live = pos[None, :] < send_lens[:, None]
-        send_rows = jnp.where(live, send_starts[:, None] + pos[None, :], -1)
-        back_chooser = low(send_rows.reshape(flat)[:, None] == jnp.arange(own_count)[None, :])
         d_out_parts = jnp.transpose(
             d_output.reshape(depth // 4, 4, out_seg, width), (1, 0, 2, 3)
         )
@@ -1766,7 +1770,7 @@
             grad_branch,
             query,
             keyval,
-            wide(allowed),
+            allow,
             w_output,
             w_query,
             w_keyval,

time: 496 us -> 493 us (level)
  no operation moved by 1% of the time
where the time goes in v6:
time: 493 us; the launch traced here: 484 us
  Pallas kernels  401 us (81%)
  matrix products  48.5 us (10%)
  local copies, waits for them, and re-layouts  13.7 us (3%)
  other arithmetic  10.5 us (2%)
    pallas_call x1, Pallas kernels, attend(): pl.pallas_call(kernel, out_shape=[wide_shape(rows, width), low_shape(tota...  101 us
    pallas_call x1, Pallas kernels, attend_back(): pl.pallas_call(kernel, out_shape=[low_shape(total, head_cols), low_shape(...  91.2 us
    pallas_call x1, Pallas kernels, mlp_back(): pl.pallas_call(kernel, out_shape=[wide_shape(8, width), wide_shape(rows,...  90.9 us
    pallas_call x1, Pallas kernels, opening(): pl.pallas_call(kernel, out_shape=[low_shape(rows, width), low_shape(rows,...  64.2 us
    pallas_call x1, Pallas kernels, closing(): pl.pallas_call(kernel, out_shape=[low_shape(2, 4, *up_own.shape[1:]), low...  42.1 us
    dot_general x5, matrix products, product_rows(): lax.dot_general(left_mat, right_mat, (((0,), (0,)), ((), ())), preferred_...  28.3 us
    pallas_call x1, Pallas kernels, widen(): pl.pallas_call(kernel, grid=(steps,), in_specs=[blocks_of(up_all), blocks...  12.2 us
    dot_general x1, matrix products, product_cols(): lax.dot_general(left_mat, right_mat, (((1,), (1,)), ((), ())), preferred_...  10.2 us
  transfers between devices with their start and end apart: 4, of which 2 were waited for; matrix products, arithmetic and copies ran while one was open for 10% of the time, Pallas kernels for 34%

profile of v6, /device:TPU:9, one launch (start us, length us, event | category | flops | bytes accessed | tf_op | source)
XLA Modules:
  0.0 484.4 jit_solution(3800424810862840405)
XLA Ops:
  0.7 1.7 dynamic-slice_convert_fusion.down
  2.4 1.3 collective-permute-start
  8.0 1.1 and_convert_fusion.allow
  12.6 1.6 dynamic-slice_convert_fusion.4
  14.2 1.1 pad_maximum_fusion
  15.3 64.2 %shard_map.297 = (bf16[160,2048]{1,0:T(8,128)(2,1)}, bf16[160,2048]{1,0:T(8,128)(2,1)}, bf16[2,256,1024]{2,1,0:T(8,128)(2,1)}, f32[16,2048]{1,0:T(8,128)}, bf16[...) custom-call(bf16[4,64,2048]{2,1,0:T(8,128)(2,1)} %tok_held, ...), custom_call_target="tpu_custom_call" | custom-call | flops 74999996416 | bytes 1048576 | tf_op jit(solution)/shard_map/pallas_call | solution.py:734
  79.6 1.8 collective-permute-start.1
  81.4 100.5 %shard_map.298 = (f32[160,2048]{1,0:T(8,128)}, bf16[1280,2048]{1,0:T(8,128)(2,1)}, bf16[1280,256]{1,0:T(8,128)(2,1)}, bf16[1280,256]{1,0:T(8,128)(2,1)}, bf16[12...) custom-call(bf16[8,160,2048]{2,1,0:T(8,128)(2,1)} %get-tuple-element, ...), custom_call_target="tpu_custom_call" | custom-call | flops 89999998976 | bytes 1048576 | tf_op jit(solution)/shard_map/pallas_call | solution.py:966
  182.0 1.5 collective-permute-start.2
  184.4 10.0 %multiply_convert_fusion = (bf16[1280,1024]{1,0:T(8,128)(2,1)S(1)}, f32[1280,1024]{1,0:T(8,128)S(1)}) fusion(f32[1024]{0:T(1024)S(1)} %bitcast.73, bf16[1280,2048]{1,0:T(8,128)(2,1)} %bitcast.86, bf16[2048,1024]{1,0:T(8,128)(2,1)} %bitcast.91), kind=kOutput, calls=%fused_computation.10 | convolution fusion | flops 5381816320 | bytes 17305600 | tf_op jit(solution)/shard_map/dot_general | solution.py:33
  194.5 6.0 %convolution_convert_fusion.1 = bf16[1024,2048]{1,0:T(8,128)(2,1)S(1)} fusion(bf16[1280,1024]{1,0:T(8,128)(2,1)S(1)} %get-tuple-element.161.act_far, bf16[1280,2048]{1,0:T(8,128)(2,1)S(1)} %bitcast.88), kind=kOutput, calls=%fused_computation.12 | convolution fusion | flops 5370806272 | bytes 12058624 | tf_op jit(solution)/shard_map/dot_general | solution.py:37
  200.8 3.3 collective-permute-done.2
  204.2 10.2 %convert_reduce_fusion = (f32[1024]{0:T(1024)S(1)}, bf16[1280,1024]{1,0:T(8,128)(2,1)}) fusion(bf16[1280,2048]{1,0:T(8,128)(2,1)S(1)} %bitcast.89, bf16[1024,2048]{1,0:T(8,128)(2,1)S(1)} %bitcast.84, f32[1280,1024]{1,0:T(8,128)S(1)} %get-tuple-element.162, f32[1024]{0:T(1024)S(1)} %bitcast.74), kind=kOutput, calls=%fused_computation.9 | convolution fusion | flops 5397543936 | bytes 17309696 | tf_op jit(solution)/shard_map/dot_general | solution.py:43
  215.6 10.2 %convolution_convert_fusion = bf16[2048,1024]{1,0:T(8,128)(2,1)} fusion(bf16[1280,2048]{1,0:T(8,128)(2,1)} %bitcast.87, bf16[1280,1024]{1,0:T(8,128)(2,1)} %get-tuple-element.164.gh), kind=kOutput, calls=%fused_computation.11 | convolution fusion | flops 5370806272 | bytes 12058624 | tf_op jit(solution)/shard_map/dot_general | solution.py:37
  226.7 90.9 %shard_map.299 = (f32[8,2048]{1,0:T(8,128)}, f32[160,2048]{1,0:T(8,128)}, bf16[8,160,2048]{2,1,0:T(8,128)(2,1)}, bf16[160,2048]{1,0:T(8,128)(2,1)}, bf16[256,204...) custom-call(bf16[1280,1024]{1,0:T(8,128)(2,1)} %get-tuple-element.164.gh, bf16[2048,1024]{1,0:T(8,128)(2,1)} %bitcast.92, ...), custom_call_target="tpu_custom_call" | custom-call | flops 95000002560 | bytes 1048576 | tf_op jit(solution)/shard_map/pallas_call | solution.py:1286
  317.6 5.0 %convolution_convert_fusion.4 = bf16[256,2048]{1,0:T(8,128)(2,1)} fusion(bf16[1280,256]{1,0:T(8,128)(2,1)S(1)} %copy-done.11, bf16[1280,2048]{1,0:T(8,128)(2,1)} %bitcast.90), kind=kOutput, calls=%fused_computation.15 | convolution fusion | flops 1342701568 | bytes 6946816 | tf_op jit(solution)/shard_map/dot_general | solution.py:37
  322.6 91.2 %shard_map.300 = (bf16[1280,256]{1,0:T(8,128)(2,1)}, bf16[8,160,256]{2,1,0:T(8,128)(2,1)}, f32[8,2048]{1,0:T(8,128)}, bf16[4,64,2048]{2,1,0:T(8,128)(2,1)}, bf16...) custom-call(bf16[8,160,2048]{2,1,0:T(8,128)(2,1)} %get-tuple-element, ...), custom_call_target="tpu_custom_call" | custom-call | flops 70000001024 | bytes 1048576 | tf_op jit(solution)/shard_map/pallas_call | solution.py:1129
  414.9 1.3 convert_reduce_fusion.1
  416.5 5.4 %convolution_convert_fusion.3 = bf16[2048,256]{1,0:T(8,128)(2,1)} fusion(bf16[1280,2048]{1,0:T(8,128)(2,1)} %get-tuple-element.103, bf16[1280,256]{1,0:T(8,128)(2,1)} %get-tuple-element.104), kind=kOutput, calls=%fused_computation.14 | convolution fusion | flops 1342701568 | bytes 6946816 | tf_op jit(solution)/shard_map/dot_general | solution.py:37
  421.9 1.7 convolution_convert_fusion.2
  425.1 42.1 %shard_map.301 = (bf16[2,4,256,1024]{3,2,1,0:T(8,128)(2,1)}, bf16[4,256,2048]{2,1,0:T(8,128)(2,1)}, bf16[2,4,256,256]{3,2,1,0:T(8,128)(2,1)}, bf16[4,64,256]{2,1...) custom-call(bf16[2,256,1024]{2,1,0:T(8,128)(2,1)} %get-tuple-element.101.up, ...), custom_call_target="tpu_custom_call" | custom-call | flops 70000001024 | bytes 1048576 | tf_op jit(solution)/shard_map/pallas_call | solution.py:1429
  469.7 12.2 %shard_map.302 = (f32[256,8192]{1,0:T(8,128)}, f32[256,2048]{1,0:T(8,128)}, f32[1024,2048]{1,0:T(8,128)}, f32[256,2048]{1,0:T(8,128)}, f32[256,256]{1,0:T(8,128)}) custom-call(bf16[2,4,256,1024]{3,2,1,0:T(8,128)(2,1)} %get-tuple-element.110.up, bf16[2,4,256,256]{3,2,1,0:T(8,128)(2,1)} %get-tuple-element.111.query, bf16[1024,2048]{1,0:T(8,128)(2,1)} %bitcast.61, ...), custom_call_target="tpu_custom_call" | custom-call | tf_op jit(solution)/shard_map/pallas_call | solution.py:1488
  482.0 1.0 copy.67
  482.9 1.0 copy.68
  (116 shorter events, 16.4 us)
Async XLA Ops:
  2.4 77.1 %copy-start = (bf16[256,2048]{1,0:T(8,128)(2,1)}, bf16[256,2048]{1,0:T(8,128)(2,1)S(1)}, u32[]{:S(2)}) copy-start(bf16[256,2048]{1,0:T(8,128)(2,1)S(1)} %dynamic-slice_convert_fusion.down) | copy-start | bytes 3145732
  2.4 77.2 %collective-permute-start = (bf16[256,2048]{1,0:T(8,128)(2,1)S(1)}, bf16[256,2048]{1,0:T(8,128)(2,1)S(1)}, u32[]{:S(2)}, u32[]{:S(2)}) collective-permute-start(bf16[256,2048]{1,0:T(8,128)(2,1)S(1)} %dynamic-slice_convert_fusion.down), channel_id=1, source_target_pairs={{0,8},{8,16},{16,24},{24,0},{1,9},{9,17},{17,25},{25,1},{2,10},{10... | collective-permute-start | bytes 3145736 | tf_op jit(solution)/shard_map/ppermute | solution.py:1632
  79.6 1.8 copy-start.9
  79.6 102.4 %collective-permute-start.1 = (bf16[256,2048]{1,0:T(8,128)(2,1)S(1)}, bf16[256,2048]{1,0:T(8,128)(2,1)S(1)}, u32[]{:S(2)}, u32[]{:S(2)}) collective-permute-start(bf16[256,2048]{1,0:T(8,128)(2,1)S(1)} %collective-permute-done.down_b), channel_id=1, source_target_pairs={{0,8},{8,16},{16,24},{24,0},{1,9},{9,17},{17,25},{25,1},{2,10},{10... | collective-permute-start | bytes 3145736 | tf_op jit(solution)/shard_map/ppermute | solution.py:1688
  182.0 22.1 %collective-permute-start.2 = (bf16[256,2048]{1,0:T(8,128)(2,1)S(1)}, bf16[256,2048]{1,0:T(8,128)(2,1)S(1)}, u32[]{:S(2)}, u32[]{:S(2)}) collective-permute-start(bf16[256,2048]{1,0:T(8,128)(2,1)S(1)} %collective-permute-done.1), channel_id=1, source_target_pairs={{0,8},{8,16},{16,24},{24,0},{1,9},{9,17},{17,25},{25,1},{2,10},{10... | collective-permute-start | bytes 3145736 | tf_op jit(solution)/shard_map/ppermute | solution.py:1727
  184.4 10.1 %copy-start.10 = (bf16[8,160,2048]{2,1,0:T(8,128)(2,1)S(1)}, bf16[8,160,2048]{2,1,0:T(8,128)(2,1)}, u32[]{:S(2)}) copy-start(bf16[8,160,2048]{2,1,0:T(8,128)(2,1)} %get-tuple-element.84) | copy-start | bytes 15728644
  194.4 6.1 %copy-start.13 = (bf16[1280,1024]{1,0:T(8,128)(2,1)}, bf16[1280,1024]{1,0:T(8,128)(2,1)S(1)}, u32[]{:S(2)}) copy-start(bf16[1280,1024]{1,0:T(8,128)(2,1)S(1)} %get-tuple-element.161.act_far) | copy-start | bytes 7864324
  194.5 6.3 %copy-start.7 = (bf16[4,256,2048]{2,1,0:T(8,128)(2,1)S(1)}, bf16[4,256,2048]{2,1,0:T(8,128)(2,1)}, u32[]{:S(2)}) copy-start(bf16[4,256,2048]{2,1,0:T(8,128)(2,1)} %get-tuple-element.86) | copy-start | bytes 12582916
  200.5 3.7 copy-start.3
  200.6 26.0 %collective-permute-start.3 = (bf16[256,2048]{1,0:T(8,128)(2,1)S(1)}, bf16[256,2048]{1,0:T(8,128)(2,1)}, u32[]{:S(2)}, u32[]{:S(2)}) collective-permute-start(bf16[256,2048]{1,0:T(8,128)(2,1)S(1)} %dynamic-slice_bitcast_fusion), channel_id=1, source_target_pairs={{0,8},{8,16},{16,24},{24,0},{1,9},{9,17},{17,25},{25,1},{2,10},{10... | collective-permute-start | bytes 3145736 | tf_op jit(solution)/shard_map/ppermute | solution.py:1735
  204.2 10.2 %copy-start.8 = (bf16[4,256,2048]{2,1,0:T(8,128)(2,1)}, bf16[4,256,2048]{2,1,0:T(8,128)(2,1)S(1)}, u32[]{:S(2)}) copy-start(bf16[4,256,2048]{2,1,0:T(8,128)(2,1)S(1)} %bitcast_dynamic-update-slice_fusion) | copy-start | bytes 12582916
  226.7 90.9 %copy-start.11 = (bf16[1280,256]{1,0:T(8,128)(2,1)S(1)}, bf16[1280,256]{1,0:T(8,128)(2,1)}, u32[]{:S(2)}) copy-start(bf16[1280,256]{1,0:T(8,128)(2,1)} %get-tuple-element.96) | copy-start | bytes 1966084
  322.6 92.2 %copy-start.4 = (f32[8,2048]{1,0:T(8,128)S(1)}, f32[8,2048]{1,0:T(8,128)}, u32[]{:S(2)}) copy-start(f32[8,2048]{1,0:T(8,128)} %get-tuple-element.107) | copy-start | bytes 196612
  416.5 5.4 %copy-start.6 = (bf16[8,160,256]{2,1,0:T(8,128)(2,1)S(1)}, bf16[8,160,256]{2,1,0:T(8,128)(2,1)}, u32[]{:S(2)}) copy-start(bf16[8,160,256]{2,1,0:T(8,128)(2,1)} %get-tuple-element.105) | copy-start | bytes 1966084
  416.5 5.4 %copy-start.12 = (bf16[1280,2048]{1,0:T(8,128)(2,1)S(1)}, bf16[1280,2048]{1,0:T(8,128)(2,1)}, u32[]{:S(2)}) copy-start(bf16[1280,2048]{1,0:T(8,128)(2,1)} %get-tuple-element.103) | copy-start | bytes 15728644
  421.9 1.9 copy-start.5
  469.7 12.3 %copy-start.2 = (bf16[4,64,2048]{2,1,0:T(8,128)(2,1)S(1)}, bf16[4,64,2048]{2,1,0:T(8,128)(2,1)}, u32[]{:S(2)}) copy-start(bf16[4,64,2048]{2,1,0:T(8,128)(2,1)} %get-tuple-element.184) | copy-start | bytes 3145732
  469.7 13.2 %copy-start.1 = (bf16[4,64,2048]{2,1,0:T(8,128)(2,1)S(1)}, bf16[4,64,2048]{2,1,0:T(8,128)(2,1)}, u32[]{:S(2)}) copy-start(bf16[4,64,2048]{2,1,0:T(8,128)(2,1)} %get-tuple-element.185) | copy-start | bytes 3145732
